TPU v7x, 32 devices: a whole 2x2x4 slice. The times are simulated.
32 devices in a mesh: seq: 2 (over x), rows: 16 (over z, y, core).
Axes of the slice: x: 2, y: 2, z: 4, core: 2. Of those that a mesh axis runs over, the one named last changes fastest.
Arguments:
- inputs: bfloat16 [32, 1024, 768], P('rows', 'seq'), may hold values from -6 to 6
- timesteps: int32 [32], P('rows'), may hold values from 0 to 999
- boundary: int32 [16], P('rows'), may hold values from 0 to 1
- step_table: bfloat16 [1000, 768], P(None, ('seq', 'rows')), may hold values from -3 to 3
- w_qkv: bfloat16 [768, 2304], P(('seq', 'rows')), may hold values from -0.21875 to 0.21875
- w_out: bfloat16 [768, 768], P(('seq', 'rows')), may hold values from -0.875 to 0.875
- w_up: bfloat16 [768, 3072], P(('seq', 'rows')), may hold values from -0.21875 to 0.21875
- w_down: bfloat16 [3072, 768], P(('seq', 'rows')), may hold values from -0.109375 to 0.109375
- norm1_gain: bfloat16 [768], P(('seq', 'rows')), may hold values from 0.5 to 1.5
- norm1_shift: bfloat16 [768], P(('seq', 'rows')), may hold values from -1.5 to 1.5
- norm2_gain: bfloat16 [768], P(('seq', 'rows')), may hold values from 0.5 to 1.5
- norm2_shift: bfloat16 [768], P(('seq', 'rows')), may hold values from -1.5 to 1.5
- up_bias: bfloat16 [3072], P(('seq', 'rows')), may hold values from -2.5 to 2.5
- down_bias: bfloat16 [768], P(('seq', 'rows')), may hold values from -1.5 to 1.5
- cotangent: bfloat16 [32, 1024, 768], P('rows', 'seq'), may hold values from -6 to 6
Outputs:
- block_out: bfloat16 [32, 1024, 768], P('rows', 'seq')
- grad_inputs: bfloat16 [32, 1024, 768], P('rows', 'seq')
- grad_step_table: float32 [1000, 768], P(None, ('seq', 'rows'))
- grad_w_qkv: float32 [768, 2304], P(('seq', 'rows'))
- grad_w_out: float32 [768, 768], P(('seq', 'rows'))
- grad_w_up: float32 [768, 3072], P(('seq', 'rows'))
- grad_w_down: float32 [3072, 768], P(('seq', 'rows'))
- grad_norm1_gain: float32 [768], P(('seq', 'rows'))
- grad_norm1_shift: float32 [768], P(('seq', 'rows'))
- grad_norm2_gain: float32 [768], P(('seq', 'rows'))
- grad_norm2_shift: float32 [768], P(('seq', 'rows'))
- grad_up_bias: float32 [3072], P(('seq', 'rows'))
- grad_down_bias: float32 [768], P(('seq', 'rows'))
All inputs are finite; a program needn't handle non-finite values.
Results may differ from a plain program's by a relative error of at most 0.008.
Values may be sent and summed in bfloat16 or wider, within the bound.
No kernel may reach another device: no remote copies, remote signals or barrier semaphores. Data moves between devices by JAX's collectives and lax.ppermute only.
A program may use at most 192 MiB of HBM per device.

v0:
```python
import math

import jax
import jax.numpy as jnp
from jax import lax
from jax.sharding import PartitionSpec as P

HD = 64


epsilon = 1e-05
masked = -1e30


def layer_norm(values, norm_gain, norm_shift):
    average = jnp.mean(values, axis=-1, keepdims=True)
    centred = values - average
    spread = jnp.mean(centred * centred, axis=-1, keepdims=True)
    return centred * lax.rsqrt(spread + epsilon) * norm_gain + norm_shift


def exact_gelu(values):
    return jax.nn.gelu(values, approximate=False)


def masked_scores(query, keys, short_rows):
    length = query.shape[1]
    scale = query.shape[-1] ** (-0.5)
    scores = jnp.einsum("gqhe,gkhe->ghqk", query, keys, preferred_element_type=jnp.float32) * scale
    places = jnp.arange(length)
    same_half = places[:, None] // (length // 2) == places[None, :] // (length // 2)
    allowed = jnp.logical_or(jnp.logical_not(short_rows)[:, None, None], same_half[None])
    return jnp.where(allowed[:, None], scores, masked)


def attend_group(packed):
    group_heads, short_rows = packed
    query = group_heads[:, :, 0]
    keys = group_heads[:, :, 1]
    values = group_heads[:, :, 2]
    scores = masked_scores(query, keys, short_rows)
    top = jnp.max(scores, axis=-1, keepdims=True)
    expo = jnp.exp(scores - top)
    total = jnp.sum(expo, axis=-1, keepdims=True)
    probs = (expo / total).astype(jnp.bfloat16)
    attended = jnp.einsum("ghqk,gkhe->gqhe", probs, values, preferred_element_type=jnp.float32)
    return (attended.astype(jnp.bfloat16), (top + jnp.log(total))[..., 0])


def attend_back(packed):
    group_heads, short_rows, log_total, d_out = packed
    query = group_heads[:, :, 0]
    keys = group_heads[:, :, 1]
    values = group_heads[:, :, 2]
    scale = query.shape[-1] ** (-0.5)
    scores = masked_scores(query, keys, short_rows)
    probs = jnp.exp(scores - log_total[..., None])
    d_values = jnp.einsum(
        "ghqk,gqhe->gkhe", probs.astype(jnp.bfloat16), d_out, preferred_element_type=jnp.float32
    )
    d_probs = jnp.einsum("gqhe,gkhe->ghqk", d_out, values, preferred_element_type=jnp.float32)
    row_dots = jnp.sum(d_probs * probs, axis=-1, keepdims=True)
    d_scores = (probs * (d_probs - row_dots)).astype(jnp.bfloat16)
    d_query = (
        jnp.einsum("ghqk,gkhe->gqhe", d_scores, keys, preferred_element_type=jnp.float32) * scale
    )
    d_keys = (
        jnp.einsum("ghqk,gqhe->gkhe", d_scores, query, preferred_element_type=jnp.float32) * scale
    )
    return jnp.stack([d_query, d_keys, d_values], axis=2).astype(jnp.bfloat16)


def local(
    inputs,
    timesteps,
    boundary,
    step_table,
    w_qkv,
    w_out,
    w_up,
    w_down,
    norm1_gain,
    norm1_shift,
    norm2_gain,
    norm2_shift,
    up_bias,
    down_bias,
    cotangent,
):
    gathered = (
        lax.all_gather(step_table, ("seq", "rows"), axis=1, tiled=True),
        lax.all_gather(w_qkv, ("seq", "rows"), axis=0, tiled=True),
        lax.all_gather(w_out, ("seq", "rows"), axis=0, tiled=True),
        lax.all_gather(w_up, ("seq", "rows"), axis=0, tiled=True),
        lax.all_gather(w_down, ("seq", "rows"), axis=0, tiled=True),
        lax.all_gather(norm1_gain, ("seq", "rows"), axis=0, tiled=True),
        lax.all_gather(norm1_shift, ("seq", "rows"), axis=0, tiled=True),
        lax.all_gather(norm2_gain, ("seq", "rows"), axis=0, tiled=True),
        lax.all_gather(norm2_shift, ("seq", "rows"), axis=0, tiled=True),
        lax.all_gather(up_bias, ("seq", "rows"), axis=0, tiled=True),
        lax.all_gather(down_bias, ("seq", "rows"), axis=0, tiled=True),
    )
    table_all, qkv_full, out_full, up_full, down_full = (
        gathered[0],
        gathered[1],
        gathered[2],
        gathered[3],
        gathered[4],
    )
    gain_one, shift_one, gain_two, shift_two, up_shift, down_shift = [
        piece.astype(jnp.float32) for piece in gathered[5:]
    ]
    rows_here, half_len, width = inputs.shape
    seq_count = lax.axis_size("seq")
    length = half_len * seq_count
    whole_in, whole_cot = (inputs, cotangent)
    local_short = jnp.arange(rows_here, dtype=jnp.int32) < boundary[0]
    heads_here = width // seq_count // HD
    count_rows, count_pos = (whole_in.shape[0], whole_in.shape[1])
    per_step = math.gcd(count_rows, max(1, 512 // length))
    steps_count = count_rows // per_step
    short_rows = local_short.reshape(steps_count, per_step)
    base = (
        whole_in.astype(jnp.float32)
        + jnp.take(table_all, timesteps, axis=0).astype(jnp.float32)[:, None, :]
    )
    flat = base.reshape(-1, width)
    normed_one, back_one = jax.vjp(layer_norm, flat, gain_one, shift_one)
    normed_low = normed_one.astype(jnp.bfloat16)
    projected = jnp.dot(normed_low, qkv_full, preferred_element_type=jnp.float32).astype(
        jnp.bfloat16
    )
    heads = projected.reshape(count_rows, count_pos, 3, width)
    heads = lax.all_to_all(heads, "seq", split_axis=3, concat_axis=1, tiled=True)
    grouped = heads.reshape(steps_count, per_step, length, 3, heads_here, HD)
    attended, log_total = lax.map(attend_group, (grouped, short_rows))
    attended = attended.reshape(count_rows, length, heads_here * HD)
    attended = lax.all_to_all(attended, "seq", split_axis=1, concat_axis=2, tiled=True)
    mixed = attended.reshape(-1, width)
    middle = flat + jnp.dot(mixed, out_full, preferred_element_type=jnp.float32)
    normed_two, back_two = jax.vjp(layer_norm, middle, gain_two, shift_two)
    normed_low_two = normed_two.astype(jnp.bfloat16)
    upper = jnp.dot(normed_low_two, up_full, preferred_element_type=jnp.float32) + up_shift
    active, back_gelu = jax.vjp(exact_gelu, upper)
    active_low = active.astype(jnp.bfloat16)
    result = (
        middle + jnp.dot(active_low, down_full, preferred_element_type=jnp.float32) + down_shift
    )
    block_local = result.astype(jnp.bfloat16).reshape(whole_in.shape)
    qkv_back, out_back, up_back, down_back = (qkv_full, out_full, up_full, down_full)
    d_below = whole_cot.reshape(-1, width)
    d_result = d_below.astype(jnp.float32)
    grad_down = jnp.einsum("tf,td->fd", active_low, d_below, preferred_element_type=jnp.float32)
    grad_down_shift = jnp.sum(d_result, axis=0)
    d_active = jnp.einsum("td,fd->tf", d_below, down_back, preferred_element_type=jnp.float32)
    (d_upper,) = back_gelu(d_active)
    d_upper_low = d_upper.astype(jnp.bfloat16)
    grad_up = jnp.einsum(
        "td,tf->df", normed_low_two, d_upper_low, preferred_element_type=jnp.float32
    )
    grad_up_shift = jnp.sum(d_upper_low.astype(jnp.float32), axis=0)
    d_normed_two = jnp.einsum("tf,df->td", d_upper_low, up_back, preferred_element_type=jnp.float32)
    d_middle_in, gain_two_grad, shift_two_grad = back_two(d_normed_two)
    d_middle = d_result + d_middle_in
    d_branch = d_middle.astype(jnp.bfloat16)
    grad_out = jnp.einsum("td,te->de", mixed, d_branch, preferred_element_type=jnp.float32)
    d_mixed = jnp.einsum(
        "te,de->td", d_branch, out_back, preferred_element_type=jnp.float32
    ).astype(jnp.bfloat16)
    d_heads = d_mixed.reshape(count_rows, count_pos, width)
    d_heads = lax.all_to_all(d_heads, "seq", split_axis=2, concat_axis=1, tiled=True)
    d_grouped = d_heads.reshape(steps_count, per_step, length, heads_here, HD)
    d_qkv = lax.map(attend_back, (grouped, short_rows, log_total, d_grouped))
    d_qkv = d_qkv.reshape(count_rows, length, 3, heads_here * HD)
    d_qkv = lax.all_to_all(d_qkv, "seq", split_axis=1, concat_axis=3, tiled=True)
    d_projected = d_qkv.reshape(-1, 3 * width)
    grad_qkv = jnp.einsum("td,te->de", normed_low, d_projected, preferred_element_type=jnp.float32)
    d_normed_one = jnp.einsum(
        "te,de->td", d_projected, qkv_back, preferred_element_type=jnp.float32
    )
    d_base_in, gain_one_grad, shift_one_grad = back_one(d_normed_one)
    d_base = d_middle + d_base_in
    grad_local = d_base.astype(jnp.bfloat16).reshape(whole_in.shape)
    row_sums = jnp.sum(d_base.reshape(count_rows, count_pos, width), axis=1)
    one_hot = (
        timesteps[:, None] == jnp.arange(table_all.shape[0], dtype=jnp.int32)[None, :]
    ).astype(jnp.float32)
    grad_table = jnp.dot(
        one_hot.T, row_sums, precision=lax.Precision.HIGHEST, preferred_element_type=jnp.float32
    )
    block_out, grad_inputs = (block_local, grad_local)
    summed = (
        lax.psum_scatter(grad_table, ("seq", "rows"), scatter_dimension=1, tiled=True),
        lax.psum_scatter(grad_qkv, ("seq", "rows"), scatter_dimension=0, tiled=True),
        lax.psum_scatter(grad_out, ("seq", "rows"), scatter_dimension=0, tiled=True),
        lax.psum_scatter(grad_up, ("seq", "rows"), scatter_dimension=0, tiled=True),
        lax.psum_scatter(grad_down, ("seq", "rows"), scatter_dimension=0, tiled=True),
        lax.psum_scatter(gain_one_grad, ("seq", "rows"), scatter_dimension=0, tiled=True),
        lax.psum_scatter(shift_one_grad, ("seq", "rows"), scatter_dimension=0, tiled=True),
        lax.psum_scatter(gain_two_grad, ("seq", "rows"), scatter_dimension=0, tiled=True),
        lax.psum_scatter(shift_two_grad, ("seq", "rows"), scatter_dimension=0, tiled=True),
        lax.psum_scatter(grad_up_shift, ("seq", "rows"), scatter_dimension=0, tiled=True),
        lax.psum_scatter(grad_down_shift, ("seq", "rows"), scatter_dimension=0, tiled=True),
    )
    return (
        block_out,
        grad_inputs,
        summed[0],
        summed[1],
        summed[2],
        summed[3],
        summed[4],
        summed[5],
        summed[6],
        summed[7],
        summed[8],
        summed[9],
        summed[10],
    )


def solution(mesh):
    in_specs = (
        P("rows", "seq", None),
        P("rows"),
        P("rows"),
        P(None, ("seq", "rows")),
        P(("seq", "rows"), None),
        P(("seq", "rows"), None),
        P(("seq", "rows"), None),
        P(("seq", "rows"), None),
        P(("seq", "rows")),
        P(("seq", "rows")),
        P(("seq", "rows")),
        P(("seq", "rows")),
        P(("seq", "rows")),
        P(("seq", "rows")),
        P("rows", "seq", None),
    )
    out_specs = (
        P("rows", "seq", None),
        P("rows", "seq", None),
        P(None, ("seq", "rows")),
        P(("seq", "rows"), None),
        P(("seq", "rows"), None),
        P(("seq", "rows"), None),
        P(("seq", "rows"), None),
        P(("seq", "rows")),
        P(("seq", "rows")),
        P(("seq", "rows")),
        P(("seq", "rows")),
        P(("seq", "rows")),
        P(("seq", "rows")),
    )
    return jax.shard_map(local, mesh=mesh, in_specs=in_specs, out_specs=out_specs, check_vma=False)
```

profile of v0, /device:TPU:0, one launch (start us, length us, event | category | flops | bytes accessed | tf_op | source)
XLA Modules:
  0.0 1264.8 jit_solution(3846162108230439298)
XLA Ops:
  15.8 42.3 %all-reduce.13 = (bf16[768]{0:T(1024)(128)(2,1)S(1)}, bf16[768]{0:T(1024)(128)(2,1)S(1)}, bf16[768]{0:T(1024)(128)(2,1)}, bf16[768]{0:T(1024)(128)(2,1)}, bf16[3...) all-reduce(bf16[768]{0:T(1024)(128)(2,1)S(1)} %dynamic-update-slice.1, ...), channel_id=1, replica_groups=mesh['seq'=2,'rows'=16] {'seq','rows'}, use_global_device_ids=true, to_apply=%add.1 | all-reduce | flops 6912 | bytes 27648
  77.8 53.0 %all-gather.8.cloned.1.call-done = bf16[768,2304]{1,0:T(8,128)(2,1)} async-done(((bf16[24,2304]{1,0:T(8,128)(2,1)}), bf16[768,2304]{1,0:T(8,128)(2,1)}) %all-gather.8.cloned.1.call-update) | async-done | bytes 3538960 | tf_op jit(solution)/shard_map/all_gather | solution.py:92
  138.3 11.3 reshape.729
  149.6 16.5 %copy.98 = bf16[2,512,3,768]{1,0,2,3:T(2,128)(2,1)} copy(bf16[2,512,3,768]{3,2,1,0:T(4,128)(2,1)} %reshape.729) | data formatting | bytes 9437184 | tf_op jit(solution)/shard_map/reshape | solution.py:133
  173.7 59.3 %all-to-all-done = bf16[2,512,3,768]{1,0,2,3:T(2,128)(2,1)} async-done(((bf16[2,512,3,768]{1,0,2,3:T(2,128)(2,1)}), bf16[2,512,3,768]{1,0,2,3:T(2,128)(2,1)}, u32[]{:S(2)}, u32[]{:S(2)}) %all-to-all-start) | async-done | bytes 4718624 | tf_op jit(solution)/shard_map/all_to_all | solution.py:134
  256.9 75.8 %while.28 = (s32[]{:T(128)}, bf16[2,1,1024,6,64]{2,4,3,1,0:T(8,128)(2,1)S(1)}, f32[2,1,6,1024]{3,2,1,0:T(8,128)S(1)}, bf16[2,1,1024,3,6,64]{2,5,4,3,1,0:T(8,128)(2,1)}, pred[2,1]{1,0:T(4,128)(4,1)}, /*index=5*/s32[]{:T(128)}) while((s32[]{:T(128)}, bf16[2,1,1024,6,64]{2,4,3,1,0:T(8,128)(2,1)S(1)}, f32[2,1,6,1024]{3,2,1,0:T(8,128)S(1)}, ...), condition=%wide.region_5.6_spmd, body=%wide.region_2.0_spmd.sunk | while | flops 1688602624 | bytes 87801944 | solution.py:136
  261.3 10.6 fusion.105
  271.9 11.2 fusion.106
  283.1 11.6 fusion.107
  299.3 10.6 fusion.105
  309.8 11.2 fusion.106
  321.1 11.6 fusion.107
  340.0 20.0 %all-to-all-done.1 = bf16[2,1024,384]{2,0,1:T(2,128)(2,1)S(1)} async-done(((bf16[2,1024,384]{2,0,1:T(2,128)(2,1)}), bf16[2,1024,384]{2,0,1:T(2,128)(2,1)S(1)}, u32[]{:S(2)}, u32[]{:S(2)}) %all-to-all-start.1) | async-done | bytes 1572896 | tf_op jit(solution)/shard_map/all_to_all | solution.py:138
  368.1 36.5 %multiply_convert_fusion.3 = (bf16[1024,3072]{1,0:T(8,128)(2,1)}, f32[1024,3072]{1,0:T(8,128)}, f32[1024,3072]{1,0:T(8,128)}) fusion(f32[3072]{0:T(1024)S(1)} %convert_element_type.130, bf16[768,3072]{1,0:T(8,128)(2,1)} %all-gather.12.cloned.1.call-done, f32[1024,768]{1,0:T(8,128)S(1)} %get-tuple-element.302, f32[768]{0:T(1024)S(1)} %convert_element_type.128, ...), kind=kOutput, calls=%fused_computation.68 | convolution fusion | flops 5043388416 | bytes 39348224 | tf_op jit(solution)/shard_map/dot_general | solution.py:143
  406.6 18.7 %convert_reduce_fusion = (f32[3072]{0:T(1024)}, bf16[1024,3072]{1,0:T(8,128)(2,1)}) fusion(f32[1024,3072]{1,0:T(8,128)} %get-tuple-element.290, bf16[1024,768]{1,0:T(8,128)(2,1)} %bitcast.197, bf16[3072,768]{1,0:T(8,128)(2,1)} %all-gather.14.cloned.1.call-done, f32[1024,3072]{1,0:T(8,128)} %get-tuple-element.303, f32[3072]{0:T(1024)S(1)} %convert_element_type.130), kind=kOutput, calls=%fused_computation.66 | convolution fusion | flops 4885312512 | bytes 37773312 | tf_op jit(solution)/shard_map/td,fd->tf/dot_general | solution.py:155
  447.1 19.9 %all-to-all-done.2 = bf16[2,512,768]{1,0,2:T(2,128)(2,1)S(1)} async-done(((bf16[2,512,768]{1,0,2:T(2,128)(2,1)}), bf16[2,512,768]{1,0,2:T(2,128)(2,1)S(1)}, u32[]{:S(2)}, u32[]{:S(2)}) %all-to-all-start.2) | async-done | bytes 1572896 | tf_op jit(solution)/shard_map/all_to_all | solution.py:171
  471.0 146.0 %while.29 = (s32[]{:T(128)}, bf16[2,1,1024,3,6,64]{2,5,4,3,1,0:T(8,128)(2,1)}, bf16[2,1,1024,3,6,64]{2,5,4,3,1,0:T(8,128)(2,1)}, pred[2,1]{1,0:T(4,128)(4,1)}, f...) while((s32[]{:T(128)}, bf16[2,1,1024,3,6,64]{2,5,4,3,1,0:T(8,128)(2,1)}, ...), condition=%wide.region_12.13_spmd, body=%wide.region_10.12_spmd.sunk | while | flops 4132046848 | bytes 226164912 | solution.py:173
  486.1 12.4 fusion.114
  498.5 17.1 %multiply_reduce_fusion.8 = (f32[6,1024]{1,0:T(8,128)S(1)}, f32[6,1024,1024]{1,2,0:T(8,128)}) fusion(f32[6,1024,1024]{1,2,0:T(8,128)} %fusion.112, f32[6,1024]{1,0:T(8,128)S(1)} %dynamic-slice_bitcast_fusion.8, pred[1024,1024]{0,1:T(8,128)(4,1)S(1)} %compare_or_fusion.5, bf16[1,1024,3,6,64]{1,4,3,2,0:T(8,128)(2,1)S(1)} %dynamic-slice_bitcast_fusion.7, ...), kind=kOutput, calls=%fused_computation.28.clone.1 | convolution fusion | flops 836757504 | bytes 53010436 | tf_op jit(solution)/shard_map/while/body/eval_jaxpr/gqhe,gkhe->ghqk/dot_general | solution.py:61
  515.6 17.2 %multiply_convert_fusion.5 = bf16[6,1024,1024]{1,2,0:T(8,128)(2,1)S(1)} fusion(f32[6,1024,1024]{1,2,0:T(8,128)} %get-tuple-element.382, f32[6,1024,1024]{1,2,0:T(8,128)} %fusion.112, f32[6,1024]{1,0:T(8,128)S(1)} %get-tuple-element.383, f32[6,1024]{1,0:T(8,128)S(1)} %dynamic-slice_bitcast_fusion.8, pred[1024,1024]{0,1:T(8,128)(4,1)S(1)} %compare_or_fusion.5), kind=kLoop, calls=%fused_computation.27.clone.1 | loop fusion | flops 37748736 | bytes 64012288 | tf_op jit(solution)/shard_map/while/body/eval_jaxpr/convert_element_type | solution.py:63
  558.8 12.4 fusion.114
  571.2 17.1 %multiply_reduce_fusion.8 = (f32[6,1024]{1,0:T(8,128)S(1)}, f32[6,1024,1024]{1,2,0:T(8,128)}) fusion(f32[6,1024,1024]{1,2,0:T(8,128)} %fusion.112, f32[6,1024]{1,0:T(8,128)S(1)} %dynamic-slice_bitcast_fusion.8, pred[1024,1024]{0,1:T(8,128)(4,1)S(1)} %compare_or_fusion.5, bf16[1,1024,3,6,64]{1,4,3,2,0:T(8,128)(2,1)S(1)} %dynamic-slice_bitcast_fusion.7, ...), kind=kOutput, calls=%fused_computation.28.clone.1 | convolution fusion | flops 836757504 | bytes 53010436 | tf_op jit(solution)/shard_map/while/body/eval_jaxpr/gqhe,gkhe->ghqk/dot_general | solution.py:61
  588.3 17.2 %multiply_convert_fusion.5 = bf16[6,1024,1024]{1,2,0:T(8,128)(2,1)S(1)} fusion(f32[6,1024,1024]{1,2,0:T(8,128)} %get-tuple-element.382, f32[6,1024,1024]{1,2,0:T(8,128)} %fusion.112, f32[6,1024]{1,0:T(8,128)S(1)} %get-tuple-element.383, f32[6,1024]{1,0:T(8,128)S(1)} %dynamic-slice_bitcast_fusion.8, pred[1024,1024]{0,1:T(8,128)(4,1)S(1)} %compare_or_fusion.5), kind=kLoop, calls=%fused_computation.27.clone.1 | loop fusion | flops 37748736 | bytes 64012288 | tf_op jit(solution)/shard_map/while/body/eval_jaxpr/convert_element_type | solution.py:63
  617.1 12.6 copy.108
  638.8 49.9 %all-to-all-done.3 = bf16[2,1024,3,384]{3,0,2,1:T(2,128)(2,1)} async-done(((bf16[2,1024,3,384]{3,0,2,1:T(2,128)(2,1)}), bf16[2,1024,3,384]{3,0,2,1:T(2,128)(2,1)}, u32[]{:S(2)}, u32[]{:S(2)}) %all-to-all-start.3) | async-done | bytes 4718624 | tf_op jit(solution)/shard_map/all_to_all | solution.py:175
  703.5 11.5 reshape.705
  730.3 11.0 fusion.55
  772.0 40.3 %all-reduce.12 = (f32[768]{0:T(1024)S(1)}, f32[768]{0:T(1024)S(1)}, f32[768]{0:T(1024)S(1)}, f32[768]{0:T(1024)S(1)}, f32[3072]{0:T(1024)S(1)}, /*index=5*/f32[768]{0:T(1024)S(1)}) all-reduce(f32[768]{0:T(1024)S(1)} %get-tuple-element.245, f32[768]{0:T(1024)S(1)} %get-tuple-element.248, ...), channel_id=7, replica_groups=mesh['seq'=2,'rows'=16] {'seq','rows'}, use_global_device_ids=true, to_apply=%region_22.23.clone | all-reduce | flops 6912 | bytes 55296
  820.0 29.0 %reduce-scatter.6.cloned.1.call-done = f32[1000,24]{0,1:T(8,128)} async-done(((f32[1000,768]{0,1:T(8,128)}), f32[1000,24]{0,1:T(8,128)}) %reduce-scatter.6.cloned.1.call-update) | async-done | bytes 96016 | tf_op jit(solution)/shard_map/reduce_scatter | solution.py:193
  849.0 142.0 %reduce-scatter.12.cloned.1.call-done = f32[24,3072]{1,0:T(8,128)} async-done(((f32[768,3072]{1,0:T(8,128)}), f32[24,3072]{1,0:T(8,128)}) %reduce-scatter.12.cloned.1.call-update) | async-done | bytes 294928 | tf_op jit(solution)/shard_map/reduce_scatter | solution.py:196
  991.0 124.6 %reduce-scatter.8.cloned.1.call-done = f32[24,2304]{1,0:T(8,128)} async-done(((f32[768,2304]{1,0:T(8,128)}), f32[24,2304]{1,0:T(8,128)}) %reduce-scatter.8.cloned.1.call-update) | async-done | bytes 221200 | tf_op jit(solution)/shard_map/reduce_scatter | solution.py:194
  1115.6 142.1 %reduce-scatter.14.cloned.1.call-done = f32[96,768]{1,0:T(8,128)} async-done(((f32[3072,768]{1,0:T(8,128)}), f32[96,768]{1,0:T(8,128)}) %reduce-scatter.14.cloned.1.call-update) | async-done | bytes 294928 | tf_op jit(solution)/shard_map/reduce_scatter | solution.py:197
  (226 shorter events, 247.5 us)
Async XLA Ops:
  7.2 65.8 %copy-start.9 = (bf16[2,512,768]{2,1,0:T(8,128)(2,1)S(1)}, bf16[2,512,768]{2,1,0:T(8,128)(2,1)}, u32[]{:S(2)}) copy-start(bf16[2,512,768]{2,1,0:T(8,128)(2,1)} %param.19) | copy-start | bytes 4718596
  7.2 61.4 %all-gather.6.cloned.1.call-start = ((), (), s32[]{:S(2)}) async-start(), calls=%async_computation.9 | async-start | bytes 1622016 | tf_op jit(solution)/shard_map/all_gather | solution.py:91
  7.9 122.9 %all-gather.8.cloned.1.call-start = ((), (), s32[]{:S(2)}) async-start(), calls=%async_computation.10 | async-start | bytes 3649536 | tf_op jit(solution)/shard_map/all_gather | solution.py:92
  8.7 354.7 %all-gather.10.cloned.1.call-start = ((), (), s32[]{:S(2)}) async-start(), calls=%async_computation.11 | async-start | bytes 1216512 | tf_op jit(solution)/shard_map/all_gather | solution.py:93
  58.1 17.5 %copy-start.23 = (f32[768]{0:T(1024)}, f32[768]{0:T(1024)S(1)}, u32[]{:S(2)}) copy-start(f32[768]{0:T(1024)S(1)} %convert_element_type.123) | copy-start | bytes 9220
  166.1 66.9 %all-to-all-start = ((bf16[2,512,3,768]{1,0,2,3:T(2,128)(2,1)}), bf16[2,512,3,768]{1,0,2,3:T(2,128)(2,1)}, u32[]{:S(2)}, u32[]{:S(2)}) async-start(bf16[2,512,3,768]{1,0,2,3:T(2,128)(2,1)} %copy.98), calls=%async_computation | async-start | bytes 9437184 | tf_op jit(solution)/shard_map/all_to_all | solution.py:134
  171.9 196.2 %all-gather.12.cloned.1.call-start = ((), (), s32[]{:S(2)}) async-start(), calls=%async_computation.12 | async-start | bytes 4866048 | tf_op jit(solution)/shard_map/all_gather | solution.py:94
  332.7 27.5 %copy-start.15 = (f32[2,1,6,1024]{3,2,1,0:T(8,128)}, f32[2,1,6,1024]{3,2,1,0:T(8,128)S(1)}, u32[]{:S(2)}) copy-start(f32[2,1,6,1024]{3,2,1,0:T(8,128)S(1)} %get-tuple-element.406) | copy-start | bytes 147460
  335.7 24.4 %all-to-all-start.1 = ((bf16[2,1024,384]{2,0,1:T(2,128)(2,1)}), bf16[2,1024,384]{2,0,1:T(2,128)(2,1)S(1)}, u32[]{:S(2)}, u32[]{:S(2)}) async-start(bf16[2,1024,384]{2,0,1:T(2,128)(2,1)} %copy.102), calls=%async_computation.1 | async-start | bytes 3145728 | tf_op jit(solution)/shard_map/all_to_all | solution.py:138
  339.4 67.2 %all-gather.14.cloned.1.call-start = ((), (), s32[]{:S(2)}) async-start(), calls=%async_computation.13 | async-start | bytes 4866048 | tf_op jit(solution)/shard_map/all_gather | solution.py:95
  340.0 95.1 %copy-start.21 = (f32[768]{0:T(1024)}, f32[768]{0:T(1024)S(1)}, u32[]{:S(2)}) copy-start(f32[768]{0:T(1024)S(1)} %convert_element_type.127) | copy-start | bytes 9220
  340.0 28.1 %copy-start.25 = (f32[768]{0:T(1024)}, f32[768]{0:T(1024)S(1)}, u32[]{:S(2)}) copy-start(f32[768]{0:T(1024)S(1)} %convert_element_type.128) | copy-start | bytes 9220
  367.5 67.6 %copy-start.3 = (f32[1024,768]{1,0:T(8,128)}, f32[1024,768]{1,0:T(8,128)S(1)}, u32[]{:S(2)}) copy-start(f32[1024,768]{1,0:T(8,128)S(1)} %get-tuple-element.302) | copy-start | bytes 9437188
  367.6 67.5 %copy-start.17 = (f32[1024]{0:T(1024)}, f32[1024]{0:T(1024)S(1)}, u32[]{:S(2)}) copy-start(f32[1024]{0:T(1024)S(1)} %broadcast_multiply_fusion) | copy-start | bytes 12292
  368.1 67.0 %copy-start.19 = (f32[1024]{0:T(1024)}, f32[1024]{0:T(1024)S(1)}, u32[]{:S(2)}) copy-start(f32[1024]{0:T(1024)S(1)} %fusion.49) | copy-start | bytes 12292
  443.3 27.7 %copy-start.16 = (f32[2,1,6,1024]{3,2,1,0:T(8,128)S(1)}, f32[2,1,6,1024]{3,2,1,0:T(8,128)}, u32[]{:S(2)}) copy-start(f32[2,1,6,1024]{3,2,1,0:T(8,128)} %copy-done.15) | copy-start | bytes 147460
  443.3 23.7 %all-to-all-start.2 = ((bf16[2,512,768]{1,0,2:T(2,128)(2,1)}), bf16[2,512,768]{1,0,2:T(2,128)(2,1)S(1)}, u32[]{:S(2)}, u32[]{:S(2)}) async-start(bf16[2,512,768]{1,0,2:T(2,128)(2,1)} %copy.105), calls=%async_computation.2 | async-start | bytes 3145728 | tf_op jit(solution)/shard_map/all_to_all | solution.py:171
  475.9 22.6 %copy-start = (bf16[1,1024,3,6,64]{1,4,3,2,0:T(8,128)(2,1)}, bf16[1,1024,3,6,64]{1,4,3,2,0:T(8,128)(2,1)S(1)}, u32[]{:S(2)}) copy-start(bf16[1,1024,3,6,64]{1,4,3,2,0:T(8,128)(2,1)S(1)} %dynamic-slice_bitcast_fusion.7) | copy-start | bytes 7077892 | tf_op jit(solution)/shard_map/while
  476.0 10.1 copy-start.8
  548.7 22.6 %copy-start = (bf16[1,1024,3,6,64]{1,4,3,2,0:T(8,128)(2,1)}, bf16[1,1024,3,6,64]{1,4,3,2,0:T(8,128)(2,1)S(1)}, u32[]{:S(2)}) copy-start(bf16[1,1024,3,6,64]{1,4,3,2,0:T(8,128)(2,1)S(1)} %dynamic-slice_bitcast_fusion.7) | copy-start | bytes 7077892 | tf_op jit(solution)/shard_map/while
  548.7 10.1 copy-start.8
  629.7 59.0 %all-to-all-start.3 = ((bf16[2,1024,3,384]{3,0,2,1:T(2,128)(2,1)}), bf16[2,1024,3,384]{3,0,2,1:T(2,128)(2,1)}, u32[]{:S(2)}, u32[]{:S(2)}) async-start(bf16[2,1024,3,384]{3,0,2,1:T(2,128)(2,1)} %copy.108), calls=%async_computation.3 | async-start | bytes 9437184 | tf_op jit(solution)/shard_map/all_to_all | solution.py:175
  635.8 184.3 %reduce-scatter.10.cloned.1.call-start = ((), (), s32[]{:S(2)}) async-start(), calls=%async_computation.16 | async-start | bytes 2433024 | tf_op jit(solution)/shard_map/reduce_scatter | solution.py:195
  638.8 210.2 %reduce-scatter.6.cloned.1.call-start = ((), (), s32[]{:S(2)}) async-start(), calls=%async_computation.14 | async-start | bytes 3244032 | tf_op jit(solution)/shard_map/reduce_scatter | solution.py:193
  703.4 11.5 copy-start.5
  703.4 11.5 copy-start.24
  703.4 11.5 copy-start.30
  703.4 11.5 copy-start.32
  730.2 260.8 %reduce-scatter.12.cloned.1.call-start = ((), (), s32[]{:S(2)}) async-start(), calls=%async_computation.17 | async-start | bytes 9732096 | tf_op jit(solution)/shard_map/reduce_scatter | solution.py:196
  741.3 374.3 %reduce-scatter.8.cloned.1.call-start = ((), (), s32[]{:S(2)}) async-start(), calls=%async_computation.15 | async-start | bytes 7299072 | tf_op jit(solution)/shard_map/reduce_scatter | solution.py:194
  751.2 506.4 %reduce-scatter.14.cloned.1.call-start = ((), (), s32[]{:S(2)}) async-start(), calls=%async_computation.18 | async-start | bytes 9732096 | tf_op jit(solution)/shard_map/reduce_scatter | solution.py:197
  761.9 10.1 copy-start.38
  (28 other events, 124.3 us)
Sparse Core Ops, SparseCore 0:
  10.9 57.6 all-gather.5
  71.5 59.3 all-gather.7
  133.8 53.9 all-gather.9
  190.6 65.5 all-gather.11
  342.8 63.7 all-gather.13
  642.2 99.2 reduce-scatter.9
  748.4 100.5 reduce-scatter.5
  856.5 134.4 reduce-scatter.11
  997.2 118.2 reduce-scatter.7
  1122.9 134.7 reduce-scatter.13
where the time goes:
time: 1270 us; the launch traced here: 1260 us
  waiting for transfers between devices  655 us (52%)
  matrix products  273 us (21%)
  local copies, waits for them, and re-layouts  128 us (10%)
  other arithmetic  89 us (7%)
  blocking collectives  82.6 us (7%)
  starting transfers between devices  20.3 us (2%)
  between operations  15.9 us (1%)
    reduce_scatter x1, waiting for transfers between devices, local(): lax.psum_scatter(grad_down, ('seq', 'rows'), scatter_dimension=0, tiled=T...  142 us
    reduce_scatter x1, waiting for transfers between devices, local(): lax.psum_scatter(grad_up, ('seq', 'rows'), scatter_dimension=0, tiled=True)  142 us
    reduce_scatter x1, waiting for transfers between devices, local(): lax.psum_scatter(grad_qkv, ('seq', 'rows'), scatter_dimension=0, tiled=True)  125 us
    unnamed x2, blocking collectives  82.6 us
    all_to_all x1, waiting for transfers between devices, local(): lax.all_to_all(heads, 'seq', split_axis=3, concat_axis=1, tiled=True)  59.3 us
    all_gather x1, waiting for transfers between devices, local(): lax.all_gather(w_qkv, ('seq', 'rows'), axis=0, tiled=True)  53 us
    all_to_all x1, waiting for transfers between devices, local(): lax.all_to_all(d_qkv, 'seq', split_axis=1, concat_axis=3, tiled=True)  49.9 us
    dot_general x4, matrix products, masked_scores(): jnp.einsum('gqhe,gkhe->ghqk', query, keys, preferred_element_type=jnp.flo...  41.4 us
  transfers between devices with their start and end apart: 14, of which 11 were waited for; matrix products, arithmetic and copies ran while one was open for 23% of the time, Pallas kernels for 0%

commit v1 on v0

v1 whole, which is shorter than its diff:
```python
import functools

import jax
import jax.numpy as jnp
from jax import lax
from jax.experimental import pallas as pl
from jax.experimental.pallas import tpu as pltpu
from jax.sharding import PartitionSpec as P

f32 = jnp.float32
bf16 = jnp.bfloat16
HD = 64
EPS = 1e-5
LOG2E = 1.4426950408889634
VMEM = 56 * 1024 * 1024
BOTH = ("seq", "rows")
WEIGHT = 0.02


def nn(a, b):
    return lax.dot_general(a, b, (((1,), (0,)), ((), ())), preferred_element_type=f32)


def nt(a, b):
    return lax.dot_general(a, b, (((1,), (1,)), ((), ())), preferred_element_type=f32)


def tn(a, b):
    return lax.dot_general(a, b, (((0,), (0,)), ((), ())), preferred_element_type=f32)


def sds(shape, dtype):
    return jax.ShapeDtypeStruct(shape, dtype)


def whole(*shape):
    return pl.BlockSpec(shape, lambda *_: (0,) * len(shape))


def params():
    return pltpu.CompilerParams(vmem_limit_bytes=VMEM, dimension_semantics=("arbitrary",))


def cost(flops, nbytes, trans=0):
    return pl.CostEstimate(
        flops=int(flops * WEIGHT), bytes_accessed=int(nbytes * WEIGHT), transcendentals=int(trans * WEIGHT)
    )


def norm_parts(v):
    c = v - jnp.mean(v, axis=1, keepdims=True)
    s = lax.rsqrt(jnp.mean(c * c, axis=1, keepdims=True) + EPS)
    return c * s, s


def norm_back(e, gain, xhat, s):
    f = e * gain
    return s * (
        f
        - jnp.mean(f, axis=1, keepdims=True)
        - xhat * jnp.mean(f * xhat, axis=1, keepdims=True)
    )


def norm_one_kernel(x_ref, row_ref, n_ref):
    xhat, _ = norm_parts(x_ref[...].astype(f32) + row_ref[0:1, :])
    n_ref[...] = (xhat * row_ref[1:2, :] + row_ref[2:3, :]).astype(bf16)


def norm_one(x, rows, tb=256):
    t, d = x.shape
    tok = pl.BlockSpec((tb, d), lambda i: (i, 0))
    return pl.pallas_call(
        norm_one_kernel,
        grid=(t // tb,),
        in_specs=[tok, whole(*rows.shape)],
        out_specs=tok,
        out_shape=sds((t, d), bf16),
        compiler_params=params(),
        cost_estimate=cost(10 * t * d, 4 * t * d),
        name="norm_one",
    )(x, rows)


def attend_kernel(
    short_ref, n_ref, wq_ref, wk_ref, wv_ref, q_ref, k_ref, v_ref, o_ref, lse_ref, *, heads, qb
):
    t = n_ref.shape[0]
    n = n_ref[...]
    q_ref[...] = nn(n, wq_ref[...]).astype(bf16)
    k_ref[...] = nn(n, wk_ref[...]).astype(bf16)
    v_ref[...] = nn(n, wv_ref[...]).astype(bf16)

    def run(parts):
        span = t // parts
        for h in range(heads):
            hs = slice(h * HD, (h + 1) * HD)
            for q0 in range(0, t, qb):
                k0 = (q0 // span) * span
                q = q_ref[q0 : q0 + qb, hs] * bf16(0.125)
                s = nt(k_ref[k0 : k0 + span, hs], q)
                top = jnp.max(s, axis=0, keepdims=True)
                p = jnp.exp2((s - top) * f32(LOG2E))
                total = jnp.sum(p, axis=0, keepdims=True)
                probs = (p * (1.0 / total)).astype(bf16)
                o_ref[q0 : q0 + qb, hs] = tn(probs, v_ref[k0 : k0 + span, hs]).astype(bf16)
                lse_ref[0, h : h + 1, q0 : q0 + qb] = top + jnp.log(total)

    short = short_ref[0]

    @pl.when(short == 0)
    def _():
        run(1)

    @pl.when(short != 0)
    def _():
        run(2)


def attend(short, n, w_qk, w_v, heads=4, qb=256):
    t, d = n.shape
    c = heads * HD
    groups = d // c

    def col(part):
        return pl.BlockSpec((d, c), lambda g, s: (0, part * groups + g))

    tok = pl.BlockSpec((t, c), lambda g, s: (0, g))
    return pl.pallas_call(
        functools.partial(attend_kernel, heads=heads, qb=qb),
        grid_spec=pltpu.PrefetchScalarGridSpec(
            num_scalar_prefetch=1,
            grid=(groups,),
            in_specs=[whole(t, d), col(0), col(1), col(0)],
            out_specs=[tok] * 4 + [pl.BlockSpec((1, heads, t), lambda g, s: (g, 0, 0))],
        ),
        out_shape=[sds((t, d), bf16)] * 4 + [sds((groups, heads, t), f32)],
        compiler_params=params(),
        cost_estimate=cost(6 * t * d * d + 16 * t * t * d, 20 * t * d, t * t * d // HD),
        name="attend",
    )(short, n, w_qk, w_qk, w_v)


def attend_back_kernel(
    short_ref, q_ref, k_ref, v_ref, o_ref, do_ref, lse_ref, dq_ref, dk_ref, dv_ref, *, heads, qb
):
    t = q_ref.shape[0]

    def run(parts):
        span = t // parts
        for h in range(heads):
            hs = slice(h * HD, (h + 1) * HD)
            for b in range(parts):
                ks = slice(b * span, (b + 1) * span)
                k = k_ref[ks, hs]
                v = v_ref[ks, hs]
                dk = dv = None
                for q0 in range(b * span, (b + 1) * span, qb):
                    qs = slice(q0, q0 + qb)
                    q = q_ref[qs, hs] * bf16(0.125)
                    do = do_ref[qs, hs]
                    prod = do.astype(f32) * o_ref[qs, hs].astype(f32)
                    delta = jnp.sum(jnp.transpose(prod), axis=0, keepdims=True)
                    p = jnp.exp2((nt(k, q) - lse_ref[0, h : h + 1, qs]) * f32(LOG2E))
                    ds = (p * (nt(v, do) - delta)).astype(bf16)
                    dv_part = nn(p.astype(bf16), do)
                    dk_part = nn(ds, q)
                    dv = dv_part if dv is None else dv + dv_part
                    dk = dk_part if dk is None else dk + dk_part
                    dq_ref[qs, hs] = (tn(ds, k) * f32(0.125)).astype(bf16)
                dk_ref[ks, hs] = dk.astype(bf16)
                dv_ref[ks, hs] = dv.astype(bf16)

    short = short_ref[0]

    @pl.when(short == 0)
    def _():
        run(1)

    @pl.when(short != 0)
    def _():
        run(2)


def attend_back(short, q, k, v, o, do, lse, part, parts, heads=2, qb=256):
    t, d = q.shape
    c = heads * HD
    count = d // c // parts
    first = part * count
    tok = pl.BlockSpec((t, c), lambda g, s: (0, first + g))
    out = pl.BlockSpec((t, c), lambda g, s: (0, g))
    d = d // parts
    return pl.pallas_call(
        functools.partial(attend_back_kernel, heads=heads, qb=qb),
        grid_spec=pltpu.PrefetchScalarGridSpec(
            num_scalar_prefetch=1,
            grid=(count,),
            in_specs=[tok] * 5 + [pl.BlockSpec((1, heads, t), lambda g, s: (first + g, 0, 0))],
            out_specs=[out] * 3,
        ),
        out_shape=[sds((t, d), bf16)] * 3,
        compiler_params=params(),
        cost_estimate=cost(40 * t * t * d, 16 * t * d, t * t * d // HD),
        name=f"attend_back_{part}",
    )(short, q, k, v, o, do, lse.reshape(-1, heads, t))


def mix_kernel(x_ref, o_ref, w_ref, row_ref, mid_ref, n_ref):
    mid = x_ref[...].astype(f32) + row_ref[0:1, :] + nn(o_ref[...], w_ref[...])
    mid_ref[...] = mid
    xhat, _ = norm_parts(mid)
    n_ref[...] = (xhat * row_ref[3:4, :] + row_ref[4:5, :]).astype(bf16)


def mix(x, o, up_out, rows, tb=256):
    t, d = x.shape
    tok = pl.BlockSpec((tb, d), lambda i: (i, 0))
    last = up_out.shape[1] // d - 1
    return pl.pallas_call(
        mix_kernel,
        grid=(t // tb,),
        in_specs=[tok, tok, pl.BlockSpec((d, d), lambda i: (0, last)), whole(*rows.shape)],
        out_specs=[tok, tok],
        out_shape=[sds((t, d), f32), sds((t, d), bf16)],
        compiler_params=params(),
        cost_estimate=cost(2 * t * d * d, 12 * t * d),
        name="mix",
    )(x, o, up_out, rows)


def gelu_parts(u):
    e = jnp.exp(u * u * f32(-0.5))
    r = pl.reciprocal(1.0 + f32(0.3275911 * 0.7071067811865476) * jnp.abs(u))
    poly = f32(-1.453152027) + r * f32(1.061405429)
    poly = f32(1.421413741) + r * poly
    poly = f32(-0.284496736) + r * poly
    poly = r * (f32(0.254829592) + r * poly)
    tail = f32(0.5) * poly * e
    return jnp.where(u >= 0, 1.0 - tail, tail), e * f32(0.3989422804014327)


def ffn_kernel(
    n_ref, dy_ref, mid_ref, wu_ref, wd_ref, ub_ref, row_ref,
    out_ref, du_ref, gwd_ref, gub_ref, small_ref, acc,
):
    j = pl.program_id(0)

    @pl.when(j == 0)
    def _():
        acc[...] = mid_ref[...] + row_ref[5:6, :]

    dy = dy_ref[...]
    wd = wd_ref[...]
    u = nn(n_ref[...], wu_ref[...]) + ub_ref[...].astype(f32)
    cdf, pdf = gelu_parts(u)
    active = (u * cdf).astype(bf16)
    acc[...] += nn(active, wd)
    gwd_ref[...] = tn(active, dy).astype(bf16)
    du = (nt(dy, wd) * (cdf + u * pdf)).astype(bf16)
    du_ref[...] = du
    gub_ref[...] = jnp.sum(du.astype(f32), axis=0, keepdims=True)

    @pl.when(j == pl.num_programs(0) - 1)
    def _():
        out_ref[...] = acc[...].astype(bf16)
        small_ref[...] = jnp.sum(dy_ref[...].astype(f32), axis=0, keepdims=True)


def ffn(n, dy, mid, up_out, down, up_bias, rows, fb=512):
    t, d = n.shape
    ff = down.shape[0]
    return pl.pallas_call(
        ffn_kernel,
        grid=(ff // fb,),
        in_specs=[
            whole(t, d),
            whole(t, d),
            whole(t, d),
            pl.BlockSpec((d, fb), lambda j: (0, j)),
            pl.BlockSpec((fb, d), lambda j: (j, 0)),
            pl.BlockSpec((1, fb), lambda j: (0, j)),
            whole(*rows.shape),
        ],
        out_specs=[
            whole(t, d),
            pl.BlockSpec((t, fb), lambda j: (0, j)),
            pl.BlockSpec((fb, d), lambda j: (j, 0)),
            pl.BlockSpec((1, fb), lambda j: (0, j)),
            whole(1, d),
        ],
        out_shape=[
            sds((t, d), bf16),
            sds((t, ff), bf16),
            sds((ff, d), bf16),
            sds((1, ff), f32),
            sds((1, d), f32),
        ],
        scratch_shapes=[pltpu.VMEM((t, d), f32)],
        compiler_params=params(),
        cost_estimate=cost(8 * t * d * ff, 20 * t * d + 8 * d * ff, 2 * t * ff),
        name="ffn",
    )(n, dy, mid, up_out, down, up_bias, rows)


def unffn_kernel(
    n_ref, dy_ref, mid_ref, du_ref, wu_ref, wo_ref, o_ref, row_ref,
    dmid_ref, do_ref, gwu_ref, gwo_ref, small_ref, acc, turned,
):
    j = pl.program_id(0)

    @pl.when(j == 0)
    def _():
        acc[...] = jnp.zeros_like(acc)
        turned[...] = n_ref[...].T

    du = du_ref[...]
    gwu_ref[...] = nn(turned[...], du).astype(bf16)
    acc[...] += nt(du, wu_ref[...])

    @pl.when(j == pl.num_programs(0) - 1)
    def _():
        xhat, s = norm_parts(mid_ref[...])
        e = acc[...]
        small_ref[...] = jnp.concatenate(
            [jnp.sum(e * xhat, axis=0, keepdims=True), jnp.sum(e, axis=0, keepdims=True)], axis=0
        )
        dmid = dy_ref[...].astype(f32) + norm_back(e, row_ref[3:4, :], xhat, s)
        dmid_ref[...] = dmid
        db = dmid.astype(bf16)
        do_ref[...] = nt(db, wo_ref[...]).astype(bf16)
        gwo_ref[...] = tn(o_ref[...], db).astype(bf16)


def unffn(n, dy, mid, du, up_out, o, rows, fb=512):
    t, d = n.shape
    ff = du.shape[1]
    last = up_out.shape[1] // d - 1
    return pl.pallas_call(
        unffn_kernel,
        grid=(ff // fb,),
        in_specs=[
            whole(t, d),
            whole(t, d),
            whole(t, d),
            pl.BlockSpec((t, fb), lambda j: (0, j)),
            pl.BlockSpec((d, fb), lambda j: (0, j)),
            pl.BlockSpec((d, d), lambda j: (0, last)),
            whole(t, d),
            whole(*rows.shape),
        ],
        out_specs=[
            whole(t, d),
            whole(t, d),
            pl.BlockSpec((d, fb), lambda j: (0, j)),
            whole(d, d),
            whole(2, d),
        ],
        out_shape=[
            sds((t, d), f32),
            sds((t, d), bf16),
            sds((d, ff), bf16),
            sds((d, d), bf16),
            sds((2, d), f32),
        ],
        scratch_shapes=[pltpu.VMEM((t, d), f32), pltpu.VMEM((d, t), bf16)],
        compiler_params=params(),
        cost_estimate=cost(4 * t * d * (ff + d), 20 * t * d + 8 * d * ff),
        name="unffn",
    )(n, dy, mid, du, up_out, up_out, o, rows)


def unqkv_kernel(
    x_ref, row_ref, n_ref, dmid_ref, wq_ref, wk_ref, wv_ref, dq_ref, dk_ref, dv_ref,
    dx_ref, gq_ref, gk_ref, gv_ref, small_ref, acc, turned,
):
    i = pl.program_id(0)

    @pl.when(i == 0)
    def _():
        turned[...] = n_ref[...].T

    n = turned[...]
    e = None
    for d_ref, w_ref, g_ref in (
        (dq_ref, wq_ref, gq_ref),
        (dk_ref, wk_ref, gk_ref),
        (dv_ref, wv_ref, gv_ref),
    ):
        piece = d_ref[...]
        g_ref[...] = nn(n, piece).astype(bf16)
        part = nt(piece, w_ref[...])
        e = part if e is None else e + part

    @pl.when(i == 0)
    def _():
        acc[...] = e

    @pl.when(i > 0)
    def _():
        acc[...] += e

    @pl.when(i == pl.num_programs(0) - 1)
    def _():
        e = acc[...]
        xhat, s = norm_parts(x_ref[...].astype(f32) + row_ref[0:1, :])
        d_base = dmid_ref[...] + norm_back(e, row_ref[1:2, :], xhat, s)
        dx_ref[...] = d_base.astype(bf16)
        small_ref[...] = jnp.concatenate(
            [
                jnp.sum(d_base, axis=0, keepdims=True),
                jnp.sum(e * xhat, axis=0, keepdims=True),
                jnp.sum(e, axis=0, keepdims=True),
                jnp.zeros((5, e.shape[1]), f32),
            ],
            axis=0,
        )


def unqkv(x, rows, n, dmid, w_qk, w_v, dq, dk, dv, cb=256):
    t, d = x.shape
    count = d // cb

    def col(part):
        return pl.BlockSpec((d, cb), lambda i: (0, part * count + i))

    tok = pl.BlockSpec((t, cb), lambda i: (0, i))
    return pl.pallas_call(
        unqkv_kernel,
        grid=(count,),
        in_specs=[whole(t, d), whole(*rows.shape), whole(t, d), whole(t, d)]
        + [col(0), col(1), col(0)]
        + [tok] * 3,
        out_specs=[whole(t, d)] + [col(0)] * 3 + [whole(8, d)],
        out_shape=[sds((t, d), bf16)] + [sds((d, d), bf16)] * 3 + [sds((8, d), f32)],
        scratch_shapes=[pltpu.VMEM((t, d), f32), pltpu.VMEM((d, t), bf16)],
        compiler_params=params(),
        cost_estimate=cost(12 * t * d * d, 30 * t * d),
        name="unqkv",
    )(x, rows, n, dmid, w_qk, w_qk, w_v, dq, dk, dv)


class Grid:
    def __init__(self, seq, rows):
        self.seq, self.rows = seq, rows
        self.known = seq == 2 and rows == 16
        at = lax.axis_index("rows")
        self.x = lax.axis_index("seq")
        self.z, self.y, self.c = at // 4, (at // 2) % 2, at % 2

    def table(self, move):
        pairs = []
        for x in range(self.seq):
            for z in range(4):
                for y in range(2):
                    for c in range(2):
                        x2, z2, y2, c2 = move(x, z, y, c)
                        pairs.append((x * 16 + z * 4 + y * 2 + c, x2 * 16 + z2 * 4 + y2 * 2 + c2))
        return pairs

    def swap(self, v, axis):
        move = {
            "x": lambda x, z, y, c: (1 - x, z, y, c),
            "y": lambda x, z, y, c: (x, z, 1 - y, c),
            "c": lambda x, z, y, c: (x, z, y, 1 - c),
        }[axis]
        return lax.ppermute(v, BOTH, self.table(move))

    def shift(self, v, by):
        return lax.ppermute(v, BOTH, self.table(lambda x, z, y, c: (x, (z + by) % 4, y, c)))


def after(v, *first):
    return lax.optimization_barrier((v, first))[0]


def spread(v, axis, count):
    return jnp.broadcast_to(jnp.expand_dims(v, axis), v.shape[:axis] + (count,) + v.shape[axis:])


def pair(own, other, at, axis):
    shape = own.shape[:axis] + (2,) + own.shape[axis:]
    here = lax.broadcasted_iota(jnp.int32, shape, axis) == at
    return jnp.where(here, spread(own, axis, 2), spread(other, axis, 2))


def gather_z(g, v, ring):
    out = spread(v, 0, 4)
    place = lax.broadcasted_iota(jnp.int32, out.shape, 0)
    last = v
    for k in range(1, 4):
        last = g.shift(last, 1) if ring else g.shift(v, k)
        out = jnp.where(place == (g.z - k) % 4, spread(last, 0, 4), out)
    return out


def gather_plane(g, a, b):
    a = pair(a, g.swap(a, "x"), g.x, 0)
    b = pair(b, g.swap(b, "y"), g.y, 1)
    yield a, b
    a = pair(a, g.swap(a, "y"), g.y, 2)
    b = pair(b, g.swap(b, "x"), g.x, 0)
    yield a, b


def gather_core(g, v):
    v = pair(v, g.swap(v, "c"), g.c, 3)
    return v.reshape(-1, v.shape[-1])


def keep(v, at, axis):
    return lax.dynamic_index_in_dim(v, at, axis, keepdims=False)


def add(a, b):
    return (a.astype(f32) + b.astype(f32)).astype(bf16)


def split_core(g, v):
    v = v.reshape(2, 4, 2, 2, -1, v.shape[-1])
    return add(keep(v, g.c, 3), g.swap(keep(v, 1 - g.c, 3), "c"))


def split_plane(g, a, b):
    a = add(keep(a, g.x, 0), g.swap(keep(a, 1 - g.x, 0), "x"))
    b = add(keep(b, g.y, 2), g.swap(keep(b, 1 - g.y, 2), "y"))
    yield a, b
    a = add(keep(a, g.y, 1), g.swap(keep(a, 1 - g.y, 1), "y"))
    b = add(keep(b, g.x, 0), g.swap(keep(b, 1 - g.x, 0), "x"))
    yield a, b


def split_z(g, v):
    total = keep(v, g.z, 0).astype(f32)
    for k in range(1, 4):
        total = total + g.shift(keep(v, (g.z + k) % 4, 0), k).astype(f32)
    return total


def scatter_plain(v):
    return lax.psum_scatter(v.astype(f32), BOTH, scatter_dimension=0, tiled=True)


def trade(v, at, rows):
    if rows:
        own = keep(v, at, 0)
        other = swap_seq(keep(v, 1 - at, 0))
        first, second = jnp.where(at == 0, own, other), jnp.where(at == 0, other, own)
        return jnp.concatenate([first, second], axis=0)
    v = v.reshape(2, v.shape[0] // 2, v.shape[1])
    own = keep(v, at, 0)
    other = swap_seq(keep(v, 1 - at, 0))
    return pair(own, other, at, 0)


def swap_seq(v):
    return lax.ppermute(v, "seq", [(0, 1), (1, 0)])


def local(
    inputs, timesteps, boundary, step_table, w_qkv, w_out, w_up, w_down,
    norm1_gain, norm1_shift, norm2_gain, norm2_shift, up_bias, down_bias, cotangent,
):
    seq, row_blocks = lax.axis_size("seq"), lax.axis_size("rows")
    g = Grid(seq, row_blocks)
    at = g.x
    devices = seq * row_blocks
    d = inputs.shape[2]
    shard = w_qkv.shape[0]
    ff = w_up.shape[1]
    steps = step_table.shape[0]
    wide = (ff // devices) // shard

    digits = jnp.stack([timesteps // 128, timesteps % 128], axis=1).astype(bf16)
    digits = jnp.pad(digits, ((0, shard - digits.shape[0]), (0, -(steps + 7 + wide) % 128)))
    short_ones = jnp.stack([norm1_gain, norm1_shift, norm2_gain, norm2_shift, down_bias], axis=1)
    table = jnp.concatenate(
        [step_table.T, short_ones, up_bias.reshape(shard, wide), digits], axis=1
    )
    up_out = jnp.concatenate([w_up, w_out], axis=1)
    x = trade(inputs, at, True)
    if g.known:
        qkv = gather_z(g, w_qkv, False)
        table = gather_z(g, table, False)
        up_out = gather_z(g, after(up_out, qkv), True)
        down = gather_z(g, after(w_down, qkv), True)
        qkv = after(qkv, x)
        w_qk, w_v = qkv[..., : 2 * d], jnp.concatenate([qkv[..., 2 * d :], table], axis=-1)
        plane = gather_plane(g, w_qk, w_v)
        next(plane)
        w_qk, w_v = next(plane)
        up_out, down = after((up_out, down), w_qk, w_v)
        table = gather_core(g, w_v[..., d:])
        w_qk, w_v = gather_core(g, w_qk), gather_core(g, w_v[..., :d])
        plane = gather_plane(g, up_out, down)
        next(plane)
    else:
        w_qk, w_v = w_qkv[:, : 2 * d], w_qkv[:, 2 * d :]
        table, w_qk, w_v, up_out, down = [
            lax.all_gather(v, BOTH, axis=0, tiled=True) for v in (table, w_qk, w_v, up_out, w_down)
        ]

    short = (at < boundary[0]).astype(jnp.int32).reshape(1)
    step = lax.dynamic_index_in_dim(timesteps, at, 0, keepdims=False)
    wanted = jnp.concatenate([step[None], jnp.arange(5 + wide, dtype=jnp.int32) + steps])
    wanted = jnp.pad(wanted, (0, -wanted.shape[0] % 8), constant_values=-1)
    pick = (wanted[:, None] == jnp.arange(table.shape[1], dtype=jnp.int32)[None]).astype(bf16)
    rows = nt(pick, table)
    up_row = rows[6 : 6 + wide].T.reshape(1, ff)
    digits = table[: shard * row_blocks, steps + 5 + wide : steps + 7 + wide]
    digits = digits.reshape(row_blocks, shard, 2)[:, : timesteps.shape[0]].reshape(-1, 2)
    digits = digits.astype(jnp.int32)
    all_steps = digits[:, 0] * 128 + digits[:, 1]

    normed_one = norm_one(x, rows)
    q, k, v, attended, lse = attend(short, normed_one, w_qk, w_v)
    dy = trade(after(cotangent, rows), at, True)
    if g.known:
        up_out, down = [gather_core(g, after(v, attended, dy)) for v in next(plane)]
    middle, normed_two = mix(x, attended, up_out, rows)
    result, d_upper, g_down, g_up_row, g_down_row = ffn(
        normed_two, dy, middle, up_out, down, up_row, rows
    )
    if g.known:
        down_cores = split_core(g, g_down)
    d_middle, d_attended, g_up, g_out, small_two = unffn(
        normed_two, dy, middle, d_upper, up_out, attended, rows
    )
    block_out = trade(result, at, False)
    g_up = jnp.concatenate([g_up, g_out], axis=1)
    half, cut = d // 2, (ff + d) // 2
    if g.known:
        down_plane = split_plane(g, down_cores[..., :half], down_cores[..., half:])
        d_attended = after(d_attended, block_out, down_cores)
    back = attend_back(short, q, k, v, attended, d_attended, lse, 0, 2)
    if g.known:
        up_cores = split_core(g, g_up)
        up_plane = split_plane(g, up_cores[..., :cut], up_cores[..., cut:])
        d_attended = after(d_attended, back, up_cores, next(down_plane))
    more = attend_back(short, q, k, v, attended, d_attended, lse, 1, 2)
    if g.known:
        down = jnp.concatenate(next(down_plane), axis=-1)
        d_middle = after(d_middle, more, down, next(up_plane))
    dq, dk, dv = [jnp.concatenate(both, axis=1) for both in zip(back, more)]
    d_x, g_q, g_k, g_v, small_one = unqkv(x, rows, normed_one, d_middle, w_qk, w_v, dq, dk, dv)
    grad_inputs = trade(d_x, at, False)

    row_count = devices
    mine = at + seq * lax.axis_index("rows")
    own_row = (jnp.arange(row_count, dtype=jnp.int32) == mine).astype(f32)
    small = jnp.concatenate(
        [
            small_one[1:3].T,
            small_two.T,
            g_down_row.T,
            g_up_row.reshape(d, wide),
            small_one[0][:, None] * own_row[None],
        ],
        axis=1,
    ).astype(bf16)
    small = jnp.pad(small, ((0, 0), (0, -small.shape[1] % 128)))
    g_qk = jnp.concatenate([g_q, g_k], axis=1)
    g_v = jnp.concatenate([g_v, small], axis=1)
    if g.known:
        up = jnp.concatenate(next(up_plane), axis=-1)
        sum_down, sum_up = split_z(g, down), split_z(g, up)
        plane = split_plane(g, split_core(g, g_qk), split_core(g, g_v))
        next(plane)
        last = split_z(g, jnp.concatenate(next(plane), axis=-1))
    else:
        sum_up, sum_down = scatter_plain(g_up), scatter_plain(g_down)
        last = scatter_plain(jnp.concatenate([g_qk, g_v], axis=1))
    sum_small = last[:, 3 * d :]
    row_sums = sum_small[:, 5 + wide : 5 + wide + row_count]
    hot = (jnp.arange(steps, dtype=jnp.int32)[:, None] == all_steps[None]).astype(f32)
    g_table = lax.dot_general(
        hot, row_sums, (((1,), (1,)), ((), ())), precision=lax.Precision.HIGHEST,
        preferred_element_type=f32,
    )
    return (
        block_out,
        grad_inputs,
        g_table,
        last[:, : 3 * d],
        sum_up[:, ff:],
        sum_up[:, :ff],
        sum_down,
        sum_small[:, 0],
        sum_small[:, 1],
        sum_small[:, 2],
        sum_small[:, 3],
        sum_small[:, 5 : 5 + wide].reshape(-1),
        sum_small[:, 4],
    )


def solution(mesh):
    tokens, weight, vector = P("rows", "seq", None), P(BOTH, None), P(BOTH)
    table = P(None, BOTH)
    in_specs = (
        (tokens, P("rows"), P("rows"), table) + (weight,) * 4 + (vector,) * 6 + (tokens,)
    )
    out_specs = (tokens, tokens, table) + (weight,) * 4 + (vector,) * 6
    return jax.shard_map(local, mesh=mesh, in_specs=in_specs, out_specs=out_specs, check_vma=False)
```

time: 1270 us -> 441 us (0.35)
  waiting for transfers between devices: 655 us -> 102 us
  matrix products: 273 us -> 2.21 us
  Pallas kernels: 0 us -> 159 us
  blocking collectives: 82.6 us -> 0 us
  local copies, waits for them, and re-layouts: 128 us -> 50 us
  starting transfers between devices: 20.3 us -> 60.8 us
  other arithmetic: 89 us -> 57.9 us
  between operations: 15.9 us -> 2.51 us
    reduce_scatter x5 -> x0, waiting for transfers between devices: 438 us -> none  [the longest x1 142 us: local(): lax.psum_scatter(grad_down, ('seq', 'rows'), scatter_dimension=0, tiled=T...]
    dot_general x27 -> x2, matrix products: 273 us -> 2.21 us  [the longest x1 1.15 us: nt(): lax.dot_general(a, b, (((1,), (1,)), ((), ())), preferred_element_type=f32)]
    pallas_call x0 -> x8, Pallas kernels: none -> 159 us  [the longest x2 40.9 us: attend_back(): pl.pallas_call(functools.partial(attend_back_kernel, heads=heads, qb=qb),...]
    all_to_all x4 -> x0, waiting for transfers between devices: 149 us -> none  [the longest x1 59.3 us: local(): lax.all_to_all(heads, 'seq', split_axis=3, concat_axis=1, tiled=True)]
    ppermute x0 -> x54, waiting for transfers between devices: none -> 102 us  [the longest x29 61.4 us: swap(): return lax.ppermute(v, BOTH, self.table(move))]
    unnamed x2 -> x0, blocking collectives: 82.6 us -> none
    all_gather x5 -> x0, waiting for transfers between devices: 65.5 us -> none  [the longest x1 53 us: local(): lax.all_gather(w_qkv, ('seq', 'rows'), axis=0, tiled=True)]
    reshape x8 -> x5, local copies, waits for them, and re-layouts: 69.5 us -> 4 us  [the longest x1 1.12 us: local(): g_up_row.reshape(d, wide)]
  transfers between devices with their start and end apart: 14 -> 54, of which waited for: 11 -> 23; matrix products, arithmetic and copies ran while one was open for 23% -> 19% of each run, Pallas kernels for 0% -> 23%
where the time goes in v1:
time: 441 us; the launch traced here: 435 us
  Pallas kernels  159 us (36%)
  waiting for transfers between devices  102 us (23%)
  starting transfers between devices  60.8 us (14%)
  other arithmetic  57.9 us (13%)
  local copies, waits for them, and re-layouts  50 us (11%)
    ppermute x29, waiting for transfers between devices, swap(): return lax.ppermute(v, BOTH, self.table(move))  61.4 us
    pallas_call x2, Pallas kernels, attend_back(): pl.pallas_call(functools.partial(attend_back_kernel, heads=heads, qb=qb),...  40.9 us
    pallas_call x1, Pallas kernels, ffn(): pl.pallas_call(ffn_kernel, grid=(ff // fb,), in_specs=[whole(t, d), whole...  35.5 us
    ppermute x21, starting transfers between devices, shift(): lax.ppermute(v, BOTH, self.table(lambda x, z, y, c: (x, (z + by) % 4, y,...  31.6 us
    pallas_call x1, Pallas kernels, attend(): pl.pallas_call(functools.partial(attend_kernel, heads=heads, qb=qb), grid...  31.5 us
    ppermute x21, waiting for transfers between devices, shift(): lax.ppermute(v, BOTH, self.table(lambda x, z, y, c: (x, (z + by) % 4, y,...  30.6 us
    select_n x15, other arithmetic, pair(): return jnp.where(here, spread(own, axis, 2), spread(other, axis, 2))  28.2 us
    ppermute x29, starting transfers between devices, swap(): return lax.ppermute(v, BOTH, self.table(move))  24.6 us
  transfers between devices with their start and end apart: 54, of which 23 were waited for; matrix products, arithmetic and copies ran while one was open for 19% of the time, Pallas kernels for 23%

profile of v1, /device:TPU:0, one launch (start us, length us, event | category | flops | bytes accessed | tf_op | source)
XLA Modules:
  0.0 434.5 jit_solution(15802499037961252177)
XLA Ops:
  17.3 4.4 %collective-permute-done.2 = bf16[24,2304]{1,0:T(8,128)(2,1)S(1)} collective-permute-done((bf16[24,2304]{1,0:T(8,128)(2,1)}, bf16[24,2304]{1,0:T(8,128)(2,1)S(1)}, u32[]{:S(2)}, u32[]{:S(2)}) %collective-permute-start.2) | collective-permute-done | bytes 110624 | tf_op jit(solution)/shard_map/ppermute | solution.py:469
  31.7 3.3 collective-permute-done.17
  35.0 3.8 collective-permute-done.14
  39.8 3.7 collective-permute-done.18
  43.5 4.3 collective-permute-done.15
  53.5 3.6 collective-permute-done.10
  58.8 4.1 collective-permute-done.7
  63.4 8.4 %collective-permute-done.11 = bf16[2,4,24,1536]{3,2,1,0:T(8,128)(2,1)S(1)} collective-permute-done((bf16[2,4,24,1536]{3,2,1,0:T(8,128)(2,1)S(1)}, bf16[2,4,24,1536]{3,2,1,0:T(8,128)(2,1)S(1)}, u32[]{:S(2)}, u32[]{:S(2)}) %collective-permute-start.11) | collective-permute-done | bytes 589856 | tf_op jit(solution)/shard_map/ppermute | solution.py:466
  79.4 10.6 %collective-permute-done.20 = bf16[4,24,3840]{2,1,0:T(8,128)(2,1)} collective-permute-done((bf16[4,24,3840]{2,1,0:T(8,128)(2,1)S(1)}, bf16[4,24,3840]{2,1,0:T(8,128)(2,1)}, u32[]{:S(2)}, u32[]{:S(2)}) %collective-permute-start.20) | collective-permute-done | bytes 737312 | tf_op jit(solution)/shard_map/ppermute | solution.py:466
  103.2 4.1 norm_one.1.n_ref
  107.3 3.2 bitcast_select_fusion.2.wq_ref.wk_ref
  110.6 31.5 %attend.1 = (bf16[1024,768]{1,0:T(8,128)(2,1)}, bf16[1024,768]{1,0:T(8,128)(2,1)}, bf16[1024,768]{1,0:T(8,128)(2,1)}, bf16[1024,768]{1,0:T(8,128)(2,1)}, f32[3,4,1024]{2,1,0:T(4,128)}) custom-call(s32[1]{0:T(128)} %bitcast.3.short_ref, bf16[1024,768]{1,0:T(8,128)(2,1)} %norm_one.1.n_ref, bf16[768,1536]{1,0:T(8,128)(2,1)} %bitcast_select_fusion.2.wq_ref.wk_ref, ...), custom_call_target="tpu_custom_call" | custom-call | flops 330175616 | bytes 314572 | tf_op jit(solution)/shard_map/attend/pallas_call | solution.py:129
  152.5 3.6 collective-permute-done.26
  156.1 5.0 %bitcast_select_fusion.1.wd_ref = bf16[3072,768]{1,0:T(8,128)(2,1)} fusion(pred[3072]{0:T(1024)(128)(4,1)S(1)} %iota.159, bf16[2,4,2,96,768]{4,3,2,1,0:T(8,128)(2,1)} %collective-permute-done.26, bf16[2,4,2,96,768]{4,3,2,1,0:T(8,128)(2,1)} %broadcast_select_fusion.1), kind=kLoop, calls=%fused_computation.6 | loop fusion | flops 2359296 | bytes 9440256 | tf_op jit(solution)/shard_map/jit(_where)/select_n | solution.py:483
  161.1 4.9 %bitcast_select_fusion.w_ref.wu_ref.wo_ref = bf16[768,3840]{1,0:T(8,128)(2,1)} fusion(pred[768]{0:T(1024)(128)(4,1)S(1)} %iota.131, bf16[2,4,2,24,3840]{4,3,2,1,0:T(8,128)(2,1)} %collective-permute-done.23, bf16[2,4,2,24,3840]{4,3,2,1,0:T(8,128)(2,1)S(1)} %broadcast_select_fusion), kind=kLoop, calls=%fused_computation.3 | loop fusion | flops 2949120 | bytes 11797248 | tf_op jit(solution)/shard_map/jit(_where)/select_n | solution.py:483
  166.0 5.8 %mix.1 = (f32[1024,768]{1,0:T(8,128)}, bf16[1024,768]{1,0:T(8,128)(2,1)}) custom-call(bf16[1024,768]{1,0:T(8,128)(2,1)} %pad_maximum_fusion.2.x_ref, bf16[1024,768]{1,0:T(8,128)(2,1)} %get-tuple-element.53.o_ref, bf16[768,3840]{1,0:T(8,128)(2,1)} %bitcast_select_fusion.w_ref.wu_ref.wo_ref, f32[16,768]{1,0:T(8,128)} %fusion.50.row_ref), custom_call_target="tpu_custom_call" | custom-call | flops 24159192 | bytes 188743 | tf_op jit(solution)/shard_map/mix/pallas_call | solution.py:219
  171.8 35.5 %ffn.1 = (bf16[1024,768]{1,0:T(8,128)(2,1)}, bf16[1024,3072]{1,0:T(8,128)(2,1)}, bf16[3072,768]{1,0:T(8,128)(2,1)}, f32[1,3072]{1,0:T(1,128)}, f32[1,768]{1,0:T(1,128)}) custom-call(bf16[1024,768]{1,0:T(8,128)(2,1)} %get-tuple-element.59.n_ref, bf16[1024,768]{1,0:T(8,128)(2,1)} %pad_maximum_fusion.3.dy_ref, f32[1024,768]{1,0:T(8,128)} %get-tuple-element.60.mid_ref, ...), custom_call_target="tpu_custom_call" | custom-call | flops 386547072 | bytes 692060 | tf_op jit(solution)/shard_map/ffn/pallas_call | solution.py:272
  207.3 4.2 constant_dynamic-slice_fusion.7
  213.2 23.5 %unffn.1 = (f32[1024,768]{1,0:T(8,128)}, bf16[1024,768]{1,0:T(8,128)(2,1)}, bf16[768,3072]{1,0:T(8,128)(2,1)}, bf16[768,768]{1,0:T(8,128)(2,1)}, f32[2,768]{1,0:T(2,128)}) custom-call(bf16[1024,768]{1,0:T(8,128)(2,1)} %get-tuple-element.59.n_ref, bf16[1024,768]{1,0:T(8,128)(2,1)} %pad_maximum_fusion.3.dy_ref, f32[1024,768]{1,0:T(8,128)} %get-tuple-element.60.mid_ref, ...), custom_call_target="tpu_custom_call" | custom-call | flops 241591904 | bytes 692060 | tf_op jit(solution)/shard_map/unffn/pallas_call | solution.py:338
  236.7 3.1 pad_maximum_fusion
  259.7 10.0 %collective-permute-done.27 = bf16[512,768]{1,0:T(8,128)(2,1)} collective-permute-done((bf16[512,768]{1,0:T(8,128)(2,1)}, bf16[512,768]{1,0:T(8,128)(2,1)}, u32[]{:S(2)}, u32[]{:S(2)}) %collective-permute-start.27) | collective-permute-done | bytes 786464 | tf_op jit(solution)/shard_map/ppermute | solution.py:556
  272.2 20.5 %attend_back_0.1 = (bf16[1024,384]{1,0:T(8,128)(2,1)}, bf16[1024,384]{1,0:T(8,128)(2,1)}, bf16[1024,384]{1,0:T(8,128)(2,1)}) custom-call(s32[1]{0:T(128)} %bitcast.3.short_ref, bf16[1024,768]{1,0:T(8,128)(2,1)} %get-tuple-element.66.q_ref, bf16[1024,768]{1,0:T(8,128)(2,1)} %get-tuple-element.67.k_ref, bf16[1024,768]{1,0:T(8,128)(2,1)} %get-tuple-element.68.v_ref, ...), custom_call_target="tpu_custom_call" | custom-call | flops 322122560 | bytes 125829 | tf_op jit(solution)/shard_map/attend_back_0/pallas_call | solution.py:193
  299.4 20.4 %attend_back_1.1 = (bf16[1024,384]{1,0:T(8,128)(2,1)}, bf16[1024,384]{1,0:T(8,128)(2,1)}, bf16[1024,384]{1,0:T(8,128)(2,1)}) custom-call(s32[1]{0:T(128)} %bitcast.3.short_ref, bf16[1024,768]{1,0:T(8,128)(2,1)} %get-tuple-element.66.q_ref, bf16[1024,768]{1,0:T(8,128)(2,1)} %get-tuple-element.67.k_ref, bf16[1024,768]{1,0:T(8,128)(2,1)} %get-tuple-element.68.v_ref, ...), custom_call_target="tpu_custom_call" | custom-call | flops 322122560 | bytes 125829 | tf_op jit(solution)/shard_map/attend_back_1/pallas_call | solution.py:193
  327.8 3.1 collective-permute-start.52
  335.7 3.2 collective-permute-done.52
  342.7 17.7 %unqkv.1 = (bf16[1024,768]{1,0:T(8,128)(2,1)}, bf16[768,768]{1,0:T(8,128)(2,1)}, bf16[768,768]{1,0:T(8,128)(2,1)}, bf16[768,768]{1,0:T(8,128)(2,1)}, f32[8,768]{1,0:T(8,128)}) custom-call(bf16[1024,768]{1,0:T(8,128)(2,1)} %pad_maximum_fusion.2.x_ref, f32[16,768]{1,0:T(8,128)} %fusion.50.row_ref, bf16[1024,768]{1,0:T(8,128)(2,1)} %norm_one.1.n_ref, ...), custom_call_target="tpu_custom_call" | custom-call | flops 144955152 | bytes 471859 | tf_op jit(solution)/shard_map/unqkv/pallas_call | solution.py:427
  375.8 7.5 %collective-permute-done.47 = bf16[4,24,1920]{2,1,0:T(8,128)(2,1)S(1)} collective-permute-done((bf16[4,24,1920]{2,1,0:T(8,128)(2,1)S(1)}, bf16[4,24,1920]{2,1,0:T(8,128)(2,1)S(1)}, u32[]{:S(2)}, u32[]{:S(2)}) %collective-permute-start.47) | collective-permute-done | bytes 368672 | tf_op jit(solution)/shard_map/ppermute | solution.py:466
  391.0 3.4 collective-permute-start.50
  394.5 14.9 %collective-permute-done.38 = bf16[4,2,24,1536]{3,2,0,1:T(8,128)(2,1)S(1)} collective-permute-done((bf16[4,2,24,1536]{3,2,0,1:T(8,128)(2,1)S(1)}, bf16[4,2,24,1536]{3,2,0,1:T(8,128)(2,1)S(1)}, u32[]{:S(2)}, u32[]{:S(2)}) %collective-permute-start.38) | collective-permute-done | bytes 589856 | tf_op jit(solution)/shard_map/ppermute | solution.py:466
  414.8 3.3 collective-permute-done.39
  418.2 4.5 %collective-permute-start.43 = (bf16[24,2432]{1,0:T(8,128)(2,1)S(1)}, bf16[24,2432]{1,0:T(8,128)(2,1)S(1)}, u32[]{:S(2)}, u32[]{:S(2)}) collective-permute-start(bf16[24,2432]{1,0:T(8,128)(2,1)S(1)} %get-tuple-element.122), channel_id=1, source_target_pairs={{0,4},{1,5},{2,6},{3,7},{4,8},{5,9},{6,10},{7,11},{8,12},{9,13},{1... | collective-permute-start | bytes 350216 | tf_op jit(solution)/shard_map/ppermute | solution.py:469
  426.6 4.3 collective-permute-done.44
  (289 shorter events, 148.6 us)
Async XLA Ops:
  6.9 22.2 %collective-permute-start.6 = (bf16[24,1024]{1,0:T(8,128)(2,1)S(1)}, bf16[24,1024]{1,0:T(8,128)(2,1)}, u32[]{:S(2)}, u32[]{:S(2)}) collective-permute-start(bf16[24,1024]{1,0:T(8,128)(2,1)S(1)} %concatenate.51), channel_id=1, source_target_pairs={{0,4},{1,5},{2,6},{3,7},{4,8},{5,9},{6,10},{7,11},{8,12},{9,13},{1... | collective-permute-start | bytes 147464 | tf_op jit(solution)/shard_map/ppermute | solution.py:469
  10.0 28.8 %collective-permute-start.5 = (bf16[24,1024]{1,0:T(8,128)(2,1)S(1)}, bf16[24,1024]{1,0:T(8,128)(2,1)}, u32[]{:S(2)}, u32[]{:S(2)}) collective-permute-start(bf16[24,1024]{1,0:T(8,128)(2,1)S(1)} %concatenate.51), channel_id=1, source_target_pairs={{0,8},{1,9},{2,10},{3,11},{4,12},{5,13},{6,14},{7,15},{8,0},{9,1},... | collective-permute-start | bytes 147464 | tf_op jit(solution)/shard_map/ppermute | solution.py:469
  12.9 11.7 %collective-permute-start.1 = (bf16[24,2304]{1,0:T(8,128)(2,1)}, bf16[24,2304]{1,0:T(8,128)(2,1)S(1)}, u32[]{:S(2)}, u32[]{:S(2)}) collective-permute-start(bf16[24,2304]{1,0:T(8,128)(2,1)} %param.19), channel_id=1, source_target_pairs={{0,12},{1,13},{2,14},{3,15},{4,0},{5,1},{6,2},{7,3},{8,4},{9,5},{1... | collective-permute-start | bytes 331784 | tf_op jit(solution)/shard_map/ppermute | solution.py:469
  21.7 26.1 %collective-permute-start = (bf16[512,768]{1,0:T(8,128)(2,1)S(1)}, bf16[512,768]{1,0:T(8,128)(2,1)}, u32[]{:S(2)}, u32[]{:S(2)}) collective-permute-start(bf16[512,768]{1,0:T(8,128)(2,1)S(1)} %dynamic-slice_bitcast_fusion.5), channel_id=1, source_target_pairs={{0,16},{16,0},{1,17},{17,1},{2,18},{18,2},{3,19},{19,3},{4,20},{20... | collective-permute-start | bytes 2359304 | tf_op jit(solution)/shard_map/ppermute | solution.py:556
  47.7 15.4 %collective-permute-start.16 = (bf16[24,3840]{1,0:T(8,128)(2,1)S(1)}, bf16[24,3840]{1,0:T(8,128)(2,1)S(1)}, u32[]{:S(2)}, u32[]{:S(2)}) collective-permute-start(bf16[24,3840]{1,0:T(8,128)(2,1)S(1)} %collective-permute-done.15), channel_id=1, source_target_pairs={{0,4},{1,5},{2,6},{3,7},{4,8},{5,9},{6,10},{7,11},{8,12},{9,13},{1... | collective-permute-start | bytes 552968 | tf_op jit(solution)/shard_map/ppermute | solution.py:469
  57.2 14.6 %collective-permute-start.11 = (bf16[2,4,24,1536]{3,2,1,0:T(8,128)(2,1)S(1)}, bf16[2,4,24,1536]{3,2,1,0:T(8,128)(2,1)S(1)}, u32[]{:S(2)}, u32[]{:S(2)}) collective-permute-start(bf16[2,4,24,1536]{3,2,1,0:T(8,128)(2,1)S(1)} %broadcast_select_fusion.9), channel_id=1, source_target_pairs={{0,2},{1,3},{2,0},{3,1},{4,6},{5,7},{6,4},{7,5},{8,10},{9,11},{10,... | collective-permute-start | bytes 1769480 | tf_op jit(solution)/shard_map/ppermute | solution.py:466
  63.0 12.5 %collective-permute-start.8 = (bf16[4,2,24,1792]{3,2,1,0:T(8,128)(2,1)S(1)}, bf16[4,2,24,1792]{3,2,1,0:T(8,128)(2,1)S(1)}, u32[]{:S(2)}, u32[]{:S(2)}) collective-permute-start(bf16[4,2,24,1792]{3,2,1,0:T(8,128)(2,1)S(1)} %broadcast_select_fusion.8), channel_id=1, source_target_pairs={{0,16},{1,17},{2,18},{3,19},{4,20},{5,21},{6,22},{7,23},{8,24},{9,... | collective-permute-start | bytes 2064392 | tf_op jit(solution)/shard_map/ppermute | solution.py:466
  75.8 14.1 %collective-permute-start.20 = (bf16[4,24,3840]{2,1,0:T(8,128)(2,1)S(1)}, bf16[4,24,3840]{2,1,0:T(8,128)(2,1)}, u32[]{:S(2)}, u32[]{:S(2)}) collective-permute-start(bf16[4,24,3840]{2,1,0:T(8,128)(2,1)S(1)} %select_select_fusion), channel_id=1, source_target_pairs={{0,16},{1,17},{2,18},{3,19},{4,20},{5,21},{6,22},{7,23},{8,24},{9,... | collective-permute-start | bytes 2211848 | tf_op jit(solution)/shard_map/ppermute | solution.py:466
  77.4 29.9 %collective-permute-start.12 = (bf16[2,4,2,24,1536]{4,3,2,1,0:T(8,128)(2,1)}, bf16[2,4,2,24,1536]{4,3,2,1,0:T(8,128)(2,1)}, u32[]{:S(2)}, u32[]{:S(2)}) collective-permute-start(bf16[2,4,2,24,1536]{4,3,2,1,0:T(8,128)(2,1)} %broadcast_select_fusion.7), channel_id=1, source_target_pairs={{0,1},{1,0},{2,3},{3,2},{4,5},{5,4},{6,7},{7,6},{8,9},{9,8},{10,11... | collective-permute-start | bytes 3538952 | tf_op jit(solution)/shard_map/ppermute | solution.py:466
  77.6 20.1 %collective-permute-start.24 = (bf16[4,96,768]{2,1,0:T(8,128)(2,1)S(1)}, bf16[4,96,768]{2,1,0:T(8,128)(2,1)}, u32[]{:S(2)}, u32[]{:S(2)}) collective-permute-start(bf16[4,96,768]{2,1,0:T(8,128)(2,1)S(1)} %select_select_fusion.1), channel_id=1, source_target_pairs={{0,2},{1,3},{2,0},{3,1},{4,6},{5,7},{6,4},{7,5},{8,10},{9,11},{10,... | collective-permute-start | bytes 1769480 | tf_op jit(solution)/shard_map/ppermute | solution.py:466
  79.2 13.7 %collective-permute-start.9 = (bf16[2,4,2,24,1024]{4,3,2,1,0:T(8,128)(2,1)S(1)}, bf16[2,4,2,24,1024]{4,3,2,1,0:T(8,128)(2,1)S(1)}, u32[]{:S(2)}, u32[]{:S(2)}) collective-permute-start(bf16[2,4,2,24,1024]{4,3,2,1,0:T(8,128)(2,1)S(1)} %slice.109), channel_id=1, source_target_pairs={{0,1},{1,0},{2,3},{3,2},{4,5},{5,4},{6,7},{7,6},{8,9},{9,8},{10,11... | collective-permute-start | bytes 2359304 | tf_op jit(solution)/shard_map/ppermute | solution.py:466
  91.3 53.3 %collective-permute-start.21 = (bf16[2,4,24,3840]{3,2,1,0:T(8,128)(2,1)S(1)}, bf16[2,4,24,3840]{3,2,1,0:T(8,128)(2,1)}, u32[]{:S(2)}, u32[]{:S(2)}) collective-permute-start(bf16[2,4,24,3840]{3,2,1,0:T(8,128)(2,1)S(1)} %broadcast_select_fusion.4), channel_id=1, source_target_pairs={{0,2},{1,3},{2,0},{3,1},{4,6},{5,7},{6,4},{7,5},{8,10},{9,11},{10,... | collective-permute-start | bytes 4423688 | tf_op jit(solution)/shard_map/ppermute | solution.py:466
  96.0 46.0 %collective-permute-start.22 = (bf16[512,768]{1,0:T(8,128)(2,1)}, bf16[512,768]{1,0:T(8,128)(2,1)}, u32[]{:S(2)}, u32[]{:S(2)}) collective-permute-start(bf16[512,768]{1,0:T(8,128)(2,1)} %dynamic-slice_bitcast_fusion.4), channel_id=1, source_target_pairs={{0,16},{16,0},{1,17},{17,1},{2,18},{18,2},{3,19},{19,3},{4,20},{20... | collective-permute-start | bytes 2359304 | tf_op jit(solution)/shard_map/ppermute | solution.py:556
  99.0 48.1 %collective-permute-start.25 = (bf16[4,2,96,768]{3,2,1,0:T(8,128)(2,1)S(1)}, bf16[4,2,96,768]{3,2,1,0:T(8,128)(2,1)}, u32[]{:S(2)}, u32[]{:S(2)}) collective-permute-start(bf16[4,2,96,768]{3,2,1,0:T(8,128)(2,1)S(1)} %broadcast_select_fusion.6), channel_id=1, source_target_pairs={{0,16},{1,17},{2,18},{3,19},{4,20},{5,21},{6,22},{7,23},{8,24},{9,... | collective-permute-start | bytes 3538952 | tf_op jit(solution)/shard_map/ppermute | solution.py:466
  146.9 14.2 %collective-permute-start.23 = (bf16[2,4,2,24,3840]{4,3,2,1,0:T(8,128)(2,1)S(1)}, bf16[2,4,2,24,3840]{4,3,2,1,0:T(8,128)(2,1)}, u32[]{:S(2)}, u32[]{:S(2)}) collective-permute-start(bf16[2,4,2,24,3840]{4,3,2,1,0:T(8,128)(2,1)S(1)} %broadcast_select_fusion), channel_id=1, source_target_pairs={{0,1},{1,0},{2,3},{3,2},{4,5},{5,4},{6,7},{7,6},{8,9},{9,8},{10,11... | collective-permute-start | bytes 8847368 | tf_op jit(solution)/shard_map/ppermute | solution.py:466
  213.1 36.2 %collective-permute-start.28 = (bf16[2,4,2,96,768]{4,3,1,0,2:T(8,128)(2,1)}, bf16[2,4,2,96,768]{4,3,1,0,2:T(8,128)(2,1)}, u32[]{:S(2)}, u32[]{:S(2)}) collective-permute-start(bf16[2,4,2,96,768]{4,3,1,0,2:T(8,128)(2,1)} %bitcast.191), channel_id=1, source_target_pairs={{0,1},{1,0},{2,3},{3,2},{4,5},{5,4},{6,7},{7,6},{8,9},{9,8},{10,11... | collective-permute-start | bytes 7077896 | tf_op jit(solution)/shard_map/ppermute | solution.py:466
  242.1 54.7 %collective-permute-start.29 = (bf16[2,4,2,24,3840]{4,3,1,0,2:T(8,128)(2,1)}, bf16[2,4,2,24,3840]{4,3,1,0,2:T(8,128)(2,1)}, u32[]{:S(2)}, u32[]{:S(2)}) collective-permute-start(bf16[2,4,2,24,3840]{4,3,1,0,2:T(8,128)(2,1)} %bitcast.190), channel_id=1, source_target_pairs={{0,1},{1,0},{2,3},{3,2},{4,5},{5,4},{6,7},{7,6},{8,9},{9,8},{10,11... | collective-permute-start | bytes 8847368 | tf_op jit(solution)/shard_map/ppermute | solution.py:466
  249.0 20.7 %collective-permute-start.27 = (bf16[512,768]{1,0:T(8,128)(2,1)}, bf16[512,768]{1,0:T(8,128)(2,1)}, u32[]{:S(2)}, u32[]{:S(2)}) collective-permute-start(bf16[512,768]{1,0:T(8,128)(2,1)} %get-tuple-element.113), channel_id=1, source_target_pairs={{0,16},{16,0},{1,17},{17,1},{2,18},{18,2},{3,19},{19,3},{4,20},{20... | collective-permute-start | bytes 2359304 | tf_op jit(solution)/shard_map/ppermute | solution.py:556
  254.0 38.6 %collective-permute-start.30 = (bf16[4,2,96,384]{3,2,0,1:T(8,128)(2,1)S(1)}, bf16[4,2,96,384]{3,2,0,1:T(8,128)(2,1)}, u32[]{:S(2)}, u32[]{:S(2)}) collective-permute-start(bf16[4,2,96,384]{3,2,0,1:T(8,128)(2,1)S(1)} %dynamic-slice_bitcast_fusion.10), channel_id=1, source_target_pairs={{0,16},{1,17},{2,18},{3,19},{4,20},{5,21},{6,22},{7,23},{8,24},{9,... | collective-permute-start | bytes 1769480 | tf_op jit(solution)/shard_map/ppermute | solution.py:466
  258.8 36.8 %collective-permute-start.31 = (bf16[2,4,96,384]{3,2,1,0:T(8,128)(2,1)S(1)}, bf16[2,4,96,384]{3,2,1,0:T(8,128)(2,1)S(1)}, u32[]{:S(2)}, u32[]{:S(2)}) collective-permute-start(bf16[2,4,96,384]{3,2,1,0:T(8,128)(2,1)S(1)} %dynamic-slice_bitcast_fusion.9), channel_id=1, source_target_pairs={{0,2},{1,3},{2,0},{3,1},{4,6},{5,7},{6,4},{7,5},{8,10},{9,11},{10,... | collective-permute-start | bytes 1769480 | tf_op jit(solution)/shard_map/ppermute | solution.py:466
  294.8 32.7 %collective-permute-start.32 = (bf16[4,96,384]{2,1,0:T(8,128)(2,1)}, bf16[4,96,384]{2,1,0:T(8,128)(2,1)S(1)}, u32[]{:S(2)}, u32[]{:S(2)}) collective-permute-start(bf16[4,96,384]{2,1,0:T(8,128)(2,1)} %dynamic-slice_bitcast_fusion.16), channel_id=1, source_target_pairs={{0,2},{1,3},{2,0},{3,1},{4,6},{5,7},{6,4},{7,5},{8,10},{9,11},{10,... | collective-permute-start | bytes 884744 | tf_op jit(solution)/shard_map/ppermute | solution.py:466
  296.5 31.1 %collective-permute-start.33 = (bf16[4,96,384]{2,1,0:T(8,128)(2,1)}, bf16[4,96,384]{2,1,0:T(8,128)(2,1)S(1)}, u32[]{:S(2)}, u32[]{:S(2)}) collective-permute-start(bf16[4,96,384]{2,1,0:T(8,128)(2,1)} %dynamic-slice_bitcast_fusion.15), channel_id=1, source_target_pairs={{0,16},{1,17},{2,18},{3,19},{4,20},{5,21},{6,22},{7,23},{8,24},{9,... | collective-permute-start | bytes 884744 | tf_op jit(solution)/shard_map/ppermute | solution.py:466
  324.5 16.6 %collective-permute-start.34 = (bf16[4,2,24,1920]{3,2,0,1:T(8,128)(2,1)S(1)}, bf16[4,2,24,1920]{3,2,0,1:T(8,128)(2,1)S(1)}, u32[]{:S(2)}, u32[]{:S(2)}) collective-permute-start(bf16[4,2,24,1920]{3,2,0,1:T(8,128)(2,1)S(1)} %dynamic-slice_bitcast_fusion.7), channel_id=1, source_target_pairs={{0,16},{1,17},{2,18},{3,19},{4,20},{5,21},{6,22},{7,23},{8,24},{9,... | collective-permute-start | bytes 2211848 | tf_op jit(solution)/shard_map/ppermute | solution.py:466
  326.2 16.3 %collective-permute-start.35 = (bf16[2,4,24,1920]{3,2,1,0:T(8,128)(2,1)S(1)}, bf16[2,4,24,1920]{3,2,1,0:T(8,128)(2,1)S(1)}, u32[]{:S(2)}, u32[]{:S(2)}) collective-permute-start(bf16[2,4,24,1920]{3,2,1,0:T(8,128)(2,1)S(1)} %dynamic-slice_bitcast_fusion.6), channel_id=1, source_target_pairs={{0,2},{1,3},{2,0},{3,1},{4,6},{5,7},{6,4},{7,5},{8,10},{9,11},{10,... | collective-permute-start | bytes 2211848 | tf_op jit(solution)/shard_map/ppermute | solution.py:466
  327.8 11.1 %collective-permute-start.52 = (bf16[96,768]{1,0:T(8,128)(2,1)S(1)}, bf16[96,768]{1,0:T(8,128)(2,1)S(1)}, u32[]{:S(2)}, u32[]{:S(2)}) collective-permute-start(bf16[96,768]{1,0:T(8,128)(2,1)S(1)} %get-tuple-element.120), channel_id=1, source_target_pairs={{0,8},{1,9},{2,10},{3,11},{4,12},{5,13},{6,14},{7,15},{8,0},{9,1},... | collective-permute-start | bytes 442376 | tf_op jit(solution)/shard_map/ppermute | solution.py:469
  362.7 12.0 %collective-permute-start.46 = (bf16[4,24,1920]{2,1,0:T(8,128)(2,1)}, bf16[4,24,1920]{2,1,0:T(8,128)(2,1)}, u32[]{:S(2)}, u32[]{:S(2)}) collective-permute-start(bf16[4,24,1920]{2,1,0:T(8,128)(2,1)} %dynamic-slice_bitcast_fusion.12), channel_id=1, source_target_pairs={{0,2},{1,3},{2,0},{3,1},{4,6},{5,7},{6,4},{7,5},{8,10},{9,11},{10,... | collective-permute-start | bytes 1105928 | tf_op jit(solution)/shard_map/ppermute | solution.py:466
  371.8 11.5 %collective-permute-start.47 = (bf16[4,24,1920]{2,1,0:T(8,128)(2,1)S(1)}, bf16[4,24,1920]{2,1,0:T(8,128)(2,1)S(1)}, u32[]{:S(2)}, u32[]{:S(2)}) collective-permute-start(bf16[4,24,1920]{2,1,0:T(8,128)(2,1)S(1)} %copy-done.23), channel_id=1, source_target_pairs={{0,16},{1,17},{2,18},{3,19},{4,20},{5,21},{6,22},{7,23},{8,24},{9,... | collective-permute-start | bytes 1105928 | tf_op jit(solution)/shard_map/ppermute | solution.py:466
  372.7 52.5 %collective-permute-start.36 = (bf16[512,768]{1,0:T(8,128)(2,1)S(1)}, bf16[512,768]{1,0:T(8,128)(2,1)S(1)}, u32[]{:S(2)}, u32[]{:S(2)}) collective-permute-start(bf16[512,768]{1,0:T(8,128)(2,1)S(1)} %copy-done.16), channel_id=1, source_target_pairs={{0,16},{16,0},{1,17},{17,1},{2,18},{18,2},{3,19},{19,3},{4,20},{20... | collective-permute-start | bytes 2359304 | tf_op jit(solution)/shard_map/ppermute | solution.py:556
  385.3 24.1 %collective-permute-start.38 = (bf16[4,2,24,1536]{3,2,0,1:T(8,128)(2,1)S(1)}, bf16[4,2,24,1536]{3,2,0,1:T(8,128)(2,1)S(1)}, u32[]{:S(2)}, u32[]{:S(2)}) collective-permute-start(bf16[4,2,24,1536]{3,2,0,1:T(8,128)(2,1)S(1)} %dynamic-slice_bitcast_fusion.8), channel_id=1, source_target_pairs={{0,16},{1,17},{2,18},{3,19},{4,20},{5,21},{6,22},{7,23},{8,24},{9,... | collective-permute-start | bytes 1769480 | tf_op jit(solution)/shard_map/ppermute | solution.py:466
  386.6 24.7 %collective-permute-start.48 = (bf16[24,3840]{1,0:T(8,128)(2,1)S(1)}, bf16[24,3840]{1,0:T(8,128)(2,1)S(1)}, u32[]{:S(2)}, u32[]{:S(2)}) collective-permute-start(bf16[24,3840]{1,0:T(8,128)(2,1)S(1)} %get-tuple-element.116), channel_id=1, source_target_pairs={{0,4},{1,5},{2,6},{3,7},{4,8},{5,9},{6,10},{7,11},{8,12},{9,13},{1... | collective-permute-start | bytes 552968 | tf_op jit(solution)/shard_map/ppermute | solution.py:469
  388.0 24.8 %collective-permute-start.49 = (bf16[24,3840]{1,0:T(8,128)(2,1)S(1)}, bf16[24,3840]{1,0:T(8,128)(2,1)S(1)}, u32[]{:S(2)}, u32[]{:S(2)}) collective-permute-start(bf16[24,3840]{1,0:T(8,128)(2,1)S(1)} %get-tuple-element.117), channel_id=1, source_target_pairs={{0,8},{1,9},{2,10},{3,11},{4,12},{5,13},{6,14},{7,15},{8,0},{9,1},... | collective-permute-start | bytes 552968 | tf_op jit(solution)/shard_map/ppermute | solution.py:469
  391.0 21.8 %collective-permute-start.50 = (bf16[24,3840]{1,0:T(8,128)(2,1)S(1)}, bf16[24,3840]{1,0:T(8,128)(2,1)S(1)}, u32[]{:S(2)}, u32[]{:S(2)}) collective-permute-start(bf16[24,3840]{1,0:T(8,128)(2,1)S(1)} %get-tuple-element.118), channel_id=1, source_target_pairs={{0,12},{1,13},{2,14},{3,15},{4,0},{5,1},{6,2},{7,3},{8,4},{9,5},{1... | collective-permute-start | bytes 552968 | tf_op jit(solution)/shard_map/ppermute | solution.py:469
  (56 other events, 430.5 us)

commit v2 on v1

v2 whole, which is shorter than its diff:
```python
import functools

import jax
import jax.numpy as jnp
from jax import lax
from jax.experimental import pallas as pl
from jax.experimental.pallas import tpu as pltpu
from jax.sharding import PartitionSpec as P

f32 = jnp.float32
bf16 = jnp.bfloat16
HD = 64
EPS = 1e-5
LOG2E = 1.4426950408889634
VMEM = 56 * 1024 * 1024
BOTH = ("seq", "rows")
WEIGHT = 0.02


def nn(a, b):
    return lax.dot_general(a, b, (((1,), (0,)), ((), ())), preferred_element_type=f32)


def nt(a, b):
    return lax.dot_general(a, b, (((1,), (1,)), ((), ())), preferred_element_type=f32)


def tn(a, b):
    return lax.dot_general(a, b, (((0,), (0,)), ((), ())), preferred_element_type=f32)


def sds(shape, dtype):
    return jax.ShapeDtypeStruct(shape, dtype)


def whole(*shape):
    return pl.BlockSpec(shape, lambda *_: (0,) * len(shape))


def params():
    return pltpu.CompilerParams(vmem_limit_bytes=VMEM, dimension_semantics=("arbitrary",))


def cost(flops, nbytes, trans=0):
    return pl.CostEstimate(
        flops=int(flops * WEIGHT), bytes_accessed=int(nbytes * WEIGHT), transcendentals=int(trans * WEIGHT)
    )


def norm_parts(v):
    c = v - jnp.mean(v, axis=1, keepdims=True)
    s = lax.rsqrt(jnp.mean(c * c, axis=1, keepdims=True) + EPS)
    return c * s, s


def norm_back(e, gain, xhat, s):
    f = e * gain
    return s * (
        f
        - jnp.mean(f, axis=1, keepdims=True)
        - xhat * jnp.mean(f * xhat, axis=1, keepdims=True)
    )


SHORT, SEQ, LAST_A, LAST_B, CORE = range(5)


def choose(flag, a, b):
    return jnp.where(flag == 0, a, b), jnp.where(flag == 0, b, a)


def weave_a(refs, at_ref):
    own, other, own_2, other_2 = [r[...].astype(f32) for r in refs]
    first, second = choose(at_ref[LAST_A], own, other)
    first_2, second_2 = choose(at_ref[LAST_A], own_2, other_2)
    quarters = choose(at_ref[CORE], first, first_2) + choose(at_ref[CORE], second, second_2)
    unit = own.shape[0] // 8
    return jnp.concatenate(
        [q[i * unit : (i + 1) * unit] for i in range(8) for q in quarters], axis=0
    ).astype(bf16)


def weave_b(refs, at_ref):
    own, other, own_2, other_2 = [r[...].astype(f32) for r in refs]
    halves = choose(at_ref[LAST_B], own, other)
    halves_2 = choose(at_ref[LAST_B], own_2, other_2)
    unit = own.shape[0] // 8
    out = []
    for half, half_2 in zip(halves, halves_2):
        even, odd = choose(at_ref[CORE], half, half_2)
        for i in range(8):
            out += [even[i * unit : (i + 1) * unit], odd[i * unit : (i + 1) * unit]]
    return jnp.concatenate(out, axis=0).astype(bf16)


def unweave(v, at_ref, unit):
    own, other = [], []
    for i in range(v.shape[0] // (2 * unit)):
        even, odd = v[2 * i * unit : (2 * i + 1) * unit], v[(2 * i + 1) * unit : (2 * i + 2) * unit]
        mine, theirs = choose(at_ref[CORE], even, odd)
        own.append(mine)
        other.append(theirs)
    return jnp.concatenate(own, axis=0), jnp.concatenate(other, axis=0)


def turn(v, at_ref):
    own, other = unweave(v.T.astype(f32), at_ref, v.shape[1] // 32)
    return own.astype(bf16), other.astype(bf16)


def call(kernel, name, grid, in_specs, out_specs, out_shape, scratch, estimate, at, args, aliases=None):
    return pl.pallas_call(
        kernel,
        grid_spec=pltpu.PrefetchScalarGridSpec(
            num_scalar_prefetch=1,
            grid=grid,
            in_specs=in_specs,
            out_specs=out_specs,
            scratch_shapes=scratch,
        ),
        out_shape=out_shape,
        compiler_params=params(),
        cost_estimate=estimate,
        input_output_aliases=aliases or {},
        name=name,
    )(at, *args)


def norm_one_kernel(at_ref, own_ref, other_ref, row_ref, x_ref, n_ref):
    ahead = pl.program_id(0) // (pl.num_programs(0) // 2) == at_ref[SEQ]
    x = jnp.where(ahead, own_ref[0].astype(f32), other_ref[...].astype(f32))
    x_ref[...] = x.astype(bf16)
    xhat, _ = norm_parts(x + row_ref[0:1, :])
    n_ref[...] = (xhat * row_ref[1:2, :] + row_ref[2:3, :]).astype(bf16)


def norm_one(at, both, other, rows, tb=256):
    half, d = other.shape
    t = 2 * half
    steps = half // tb
    tok = pl.BlockSpec((tb, d), lambda i, s: (i, 0))
    return call(
        norm_one_kernel, "norm_one", (2 * steps,),
        [
            pl.BlockSpec((1, tb, d), lambda i, s: (s[SEQ], i % steps, 0)),
            pl.BlockSpec((tb, d), lambda i, s: (i % steps, 0)),
            whole(*rows.shape),
        ],
        [tok, tok], [sds((t, d), bf16)] * 2, [],
        cost(10 * t * d, 4 * t * d), at, (both, other, rows),
    )


def weave_keys(refs, at_ref, w_ref):
    last = pl.program_id(0) == pl.num_programs(0) - 1

    @pl.when(jnp.logical_not(last))
    def _():
        w_ref[...] = weave_a(refs[:4], at_ref)

    @pl.when(last)
    def _():
        w_ref[...] = weave_b(refs[4:], at_ref)


def qkv_columns(w_a, w_b, width, groups):
    specs, args = [], []
    for pieces, column in (
        (w_a, lambda i, s: (0, i)),
        (w_a, lambda i, s: (0, groups + jnp.minimum(i, groups - 2))),
        (w_b, lambda i, s: (0, 0)),
        (w_b, lambda i, s: (0, 1 + i)),
    ):
        specs += [pl.BlockSpec((pieces[0].shape[0], width), column)] * 4
        args += pieces
    return specs, args


def attend_kernel(at_ref, n_ref, *refs, heads, qb):
    q_ref, k_ref, v_ref, o_ref, lse_ref, wk_ref = refs[16:]
    t = n_ref.shape[0]
    n = n_ref[...]
    weave_keys(refs[4:12], at_ref, wk_ref)
    q_ref[...] = nn(n, weave_a(refs[0:4], at_ref)).astype(bf16)
    k_ref[...] = nn(n, wk_ref[...]).astype(bf16)
    v_ref[...] = nn(n, weave_b(refs[12:16], at_ref)).astype(bf16)

    def run(parts):
        span = t // parts
        for h in range(heads):
            hs = slice(h * HD, (h + 1) * HD)
            for q0 in range(0, t, qb):
                k0 = (q0 // span) * span
                q = q_ref[q0 : q0 + qb, hs] * bf16(0.125)
                s = nt(k_ref[k0 : k0 + span, hs], q)
                top = jnp.max(s, axis=0, keepdims=True)
                p = jnp.exp2((s - top) * f32(LOG2E))
                total = jnp.sum(p, axis=0, keepdims=True)
                probs = (p * (1.0 / total)).astype(bf16)
                o_ref[q0 : q0 + qb, hs] = tn(probs, v_ref[k0 : k0 + span, hs]).astype(bf16)
                lse_ref[0, h : h + 1, q0 : q0 + qb] = top + jnp.log(total)

    short = at_ref[SHORT]

    @pl.when(short == 0)
    def _():
        run(1)

    @pl.when(short != 0)
    def _():
        run(2)


def attend(at, n, w_a, w_b, heads=4, qb=256):
    t, d = n.shape
    c = heads * HD
    groups = d // c
    specs, args = qkv_columns(w_a, w_b, c, groups)
    tok = pl.BlockSpec((t, c), lambda g, s: (0, g))
    return call(
        functools.partial(attend_kernel, heads=heads, qb=qb), "attend", (groups,),
        [whole(t, d)] + specs,
        [tok] * 4 + [pl.BlockSpec((1, heads, t), lambda g, s: (g, 0, 0))],
        [sds((t, d), bf16)] * 4 + [sds((groups, heads, t), f32)], [pltpu.VMEM((d, c), bf16)],
        cost(6 * t * d * d + 16 * t * t * d, 20 * t * d, t * t * d // HD),
        at, (n, *args),
    )


def attend_back_kernel(at_ref, q_ref, k_ref, v_ref, o_ref, do_ref, lse_ref, *refs, heads, qb):
    dq_ref, dk_ref, dv_ref = refs[-3:]
    t = q_ref.shape[0]

    def run(parts):
        span = t // parts
        k_turned = k_ref[...].T
        prod = (do_ref[...].astype(f32) * o_ref[...].astype(f32)).T
        for h in range(heads):
            hs = slice(h * HD, (h + 1) * HD)
            for b in range(parts):
                ks = slice(b * span, (b + 1) * span)
                k = k_ref[ks, hs]
                v = v_ref[ks, hs]
                dk = dv = None
                for q0 in range(b * span, (b + 1) * span, qb):
                    qs = slice(q0, q0 + qb)
                    q = q_ref[qs, hs] * bf16(0.125)
                    do = do_ref[qs, hs]
                    delta = jnp.sum(prod[hs, qs], axis=0, keepdims=True)
                    p = jnp.exp2((nt(k, q) - lse_ref[0, h : h + 1, qs]) * f32(LOG2E))
                    ds = (p * (nt(v, do) - delta)).astype(bf16)
                    dv_part = nn(p.astype(bf16), do)
                    dk_part = nn(ds, q)
                    dv = dv_part if dv is None else dv + dv_part
                    dk = dk_part if dk is None else dk + dk_part
                    dq_ref[qs, hs] = (nn(k_turned[hs, ks], ds) * f32(0.125)).T.astype(bf16)
                dk_ref[ks, hs] = dk.astype(bf16)
                dv_ref[ks, hs] = dv.astype(bf16)

    short = at_ref[SHORT]

    @pl.when(short == 0)
    def _():
        run(1)

    @pl.when(short != 0)
    def _():
        run(2)


def attend_back(at, q, k, v, o, do, lse, part, parts, before=(), heads=2, qb=256):
    t, d = q.shape
    c = heads * HD
    count = d // c // parts
    first = part * count
    tok = pl.BlockSpec((t, c), lambda g, s: (0, first + g))
    return call(
        functools.partial(attend_back_kernel, heads=heads, qb=qb), f"attend_back_{part}", (count,),
        [tok] * 5
        + [pl.BlockSpec((1, heads, t), lambda g, s: (first + g, 0, 0))]
        + [pl.BlockSpec(memory_space=pl.ANY)] * len(before),
        [tok] * 3, [sds((t, d), bf16)] * 3, [],
        cost(40 * t * t * d // parts, 16 * t * d // parts, t * t * d // HD // parts),
        at, (q, k, v, o, do, lse.reshape(-1, heads, t), *before),
        {7 + i: i for i in range(len(before))},
    )


def mix_kernel(
    at_ref, x_ref, o_ref, w0_ref, w1_ref, w2_ref, w3_ref, own_ref, other_ref, row_ref,
    mid_ref, n_ref, dy_ref, w_ref,
):
    @pl.when(pl.program_id(0) == 0)
    def _():
        w_ref[...] = weave_a((w0_ref, w1_ref, w2_ref, w3_ref), at_ref)

    ahead = pl.program_id(0) // (pl.num_programs(0) // 2) == at_ref[SEQ]
    dy_ref[...] = jnp.where(ahead, own_ref[0].astype(f32), other_ref[...].astype(f32)).astype(bf16)
    mid = x_ref[...].astype(f32) + row_ref[0:1, :] + nn(o_ref[...], w_ref[...])
    mid_ref[...] = mid
    xhat, _ = norm_parts(mid)
    n_ref[...] = (xhat * row_ref[3:4, :] + row_ref[4:5, :]).astype(bf16)


def mix(at, x, o, up_out, both, other, rows, tb=256):
    t, d = x.shape
    steps = other.shape[0] // tb
    tok = pl.BlockSpec((tb, d), lambda i, s: (i, 0))
    height, width = up_out[0].shape
    return call(
        mix_kernel, "mix", (t // tb,),
        [tok, tok]
        + [pl.BlockSpec((height, d), lambda i, s: (0, width // d - 1))] * 4
        + [
            pl.BlockSpec((1, tb, d), lambda i, s: (s[SEQ], i % steps, 0)),
            pl.BlockSpec((tb, d), lambda i, s: (i % steps, 0)),
            whole(*rows.shape),
        ],
        [tok] * 3, [sds((t, d), f32), sds((t, d), bf16), sds((t, d), bf16)],
        [pltpu.VMEM((d, d), bf16)], cost(2 * t * d * d, 12 * t * d), at, (x, o, *up_out, both, other, rows),
    )


def gelu_parts(u):
    e = jnp.exp(u * u * f32(-0.5))
    r = pl.reciprocal(1.0 + f32(0.3275911 * 0.7071067811865476) * jnp.abs(u))
    poly = f32(-1.453152027) + r * f32(1.061405429)
    poly = f32(1.421413741) + r * poly
    poly = f32(-0.284496736) + r * poly
    poly = r * (f32(0.254829592) + r * poly)
    tail = f32(0.5) * poly * e
    return jnp.where(u >= 0, 1.0 - tail, tail), e * f32(0.3989422804014327)


def ffn_kernel(at_ref, n_ref, dy_ref, mid_ref, *refs):
    ub_ref, row_ref, own_ref, send_ref, du_ref, keep_ref, give_ref, gub_ref, small_ref, acc, act = refs[8:]
    j = pl.program_id(0)

    @pl.when(j == 0)
    def _():
        acc[...] = mid_ref[...] + row_ref[5:6, :]

    wu = weave_a(refs[:4], at_ref)
    other = (j // (pl.num_programs(0) // 2)) != at_ref[LAST_B]
    even_odd = choose(
        at_ref[CORE],
        jnp.where(other, refs[5][...].astype(f32), refs[4][...].astype(f32)),
        jnp.where(other, refs[7][...].astype(f32), refs[6][...].astype(f32)),
    )
    short, d = refs[4].shape[0] // 4, dy_ref.shape[1]
    wd = jnp.concatenate(
        [
            v[i * short : (i + 1) * short, k * d : (k + 1) * d]
            for i in range(4)
            for v in even_odd
            for k in range(4)
        ],
        axis=0,
    ).astype(bf16)
    unit = 4 * short
    ub = ub_ref[...].astype(f32)
    t, fb = act.shape
    tb = t // 4
    gub = jnp.zeros((1, fb), f32)
    for i in range(4):
        sl = slice(i * tb, (i + 1) * tb)
        u = nn(n_ref[sl, :], wu) + ub
        da = nt(dy_ref[sl, :], wd)
        cdf, pdf = gelu_parts(u)
        active = (u * cdf).astype(bf16)
        act[sl, :] = active
        du = (da * (cdf + u * pdf)).astype(bf16)
        du_ref[sl, :] = du
        gub = gub + jnp.sum(du.astype(f32), axis=0, keepdims=True)
        acc[sl, :] += nn(active, wd)
    gub_ref[...] = gub
    own, theirs = unweave(tn(act[...], dy_ref[...]), at_ref, unit)
    keep_ref[...] = own.astype(bf16)
    give_ref[...] = theirs.astype(bf16)

    @pl.when(j == pl.num_programs(0) - 1)
    def _():
        half = t // 2
        own, theirs = choose(at_ref[SEQ], acc[:half, :], acc[half:, :])
        own_ref[...] = own.astype(bf16)
        send_ref[...] = theirs.astype(bf16)
        small_ref[...] = jnp.sum(dy_ref[...].astype(f32), axis=0, keepdims=True)


def ffn(at, n, dy, mid, up_out, down, up_bias, rows):
    t, d = n.shape
    ff = up_bias.shape[1]
    fb = ff // 4
    high, low = up_out[0].shape[0], down[0].shape[0]
    chunk = pl.BlockSpec((fb // 2, d), lambda j, s: (j, 0))
    return call(
        ffn_kernel, "ffn", (4,),
        [whole(t, d)] * 3
        + [pl.BlockSpec((high, fb), lambda j, s: (0, j))] * 4
        + [pl.BlockSpec((low // 2, 4 * d), lambda j, s: (j % 2, 0))] * 4
        + [pl.BlockSpec((1, fb), lambda j, s: (0, j)), whole(*rows.shape)],
        [whole(t // 2, d)] * 2
        + [pl.BlockSpec((t, fb), lambda j, s: (0, j)), chunk, chunk]
        + [pl.BlockSpec((1, fb), lambda j, s: (0, j)), whole(1, d)],
        [sds((t // 2, d), bf16)] * 2
        + [sds((t, ff), bf16)]
        + [sds((ff // 2, d), bf16)] * 2
        + [sds((1, ff), f32), sds((1, d), f32)],
        [pltpu.VMEM((t, d), f32), pltpu.VMEM((t, fb), bf16)],
        cost(8 * t * d * ff, 20 * t * d + 8 * d * ff, 2 * t * ff),
        at, (n, dy, mid, *up_out, *down, up_bias, rows),
    )


def unffn_kernel(at_ref, n_ref, dy_ref, mid_ref, du_ref, w0_ref, w1_ref, w2_ref, w3_ref, o_ref, row_ref, *refs):
    dmid_ref, do_ref, keep_ref, give_ref, small_ref, acc, turned, turned_2 = refs
    j = pl.program_id(0)
    last = pl.num_programs(0) - 1
    w = weave_a((w0_ref, w1_ref, w2_ref, w3_ref), at_ref)

    @pl.when(j == 0)
    def _():
        acc[...] = jnp.zeros_like(acc)
        turned[...], turned_2[...] = turn(n_ref[...], at_ref)

    @pl.when(j < last)
    def _():
        du = du_ref[...]
        keep_ref[...] = nn(turned[...], du).astype(bf16)
        give_ref[...] = nn(turned_2[...], du).astype(bf16)
        acc[...] += nt(du, w)

    @pl.when(j == last)
    def _():
        xhat, s = norm_parts(mid_ref[...])
        e = acc[...]
        small_ref[...] = jnp.concatenate(
            [jnp.sum(e * xhat, axis=0, keepdims=True), jnp.sum(e, axis=0, keepdims=True)], axis=0
        )
        dmid = dy_ref[...].astype(f32) + norm_back(e, row_ref[3:4, :], xhat, s)
        dmid_ref[...] = dmid
        db = dmid.astype(bf16)
        do_ref[...] = nt(db, w).astype(bf16)
        own, other = unweave(tn(o_ref[...], db), at_ref, w.shape[0] // 32)
        keep_ref[...] = own.astype(bf16)
        give_ref[...] = other.astype(bf16)


def unffn(at, n, dy, mid, du, up_out, o, rows):
    t, d = n.shape
    ff = du.shape[1]
    count = ff // d
    cols = pl.BlockSpec((d // 2, d), lambda j, s: (0, j))
    return call(
        unffn_kernel, "unffn", (count + 1,),
        [whole(t, d)] * 3
        + [pl.BlockSpec((t, d), lambda j, s: (0, jnp.minimum(j, count - 1)))]
        + [pl.BlockSpec((up_out[0].shape[0], d), lambda j, s: (0, j))] * 4
        + [whole(t, d), whole(*rows.shape)],
        [whole(t, d)] * 2 + [cols] * 2 + [whole(2, d)],
        [sds((t, d), f32), sds((t, d), bf16)] + [sds((d // 2, ff + d), bf16)] * 2 + [sds((2, d), f32)],
        [pltpu.VMEM((t, d), f32)] + [pltpu.VMEM((d // 2, t), bf16)] * 2,
        cost(4 * t * d * (ff + d), 20 * t * d + 8 * d * ff),
        at, (n, dy, mid, du, *up_out, o, rows),
    )


def grad_qkv_kernel(at_ref, n_ref, dq_ref, dk_ref, dv_ref, keep_ref, give_ref, turned, turned_2):
    @pl.when(pl.program_id(0) == 0)
    def _():
        turned[...], turned_2[...] = turn(n_ref[...], at_ref)

    for i, d_ref in enumerate((dq_ref, dk_ref, dv_ref)):
        keep_ref[i] = nn(turned[...], d_ref[...]).astype(bf16)
        give_ref[i] = nn(turned_2[...], d_ref[...]).astype(bf16)


def grad_qkv(at, n, dq, dk, dv, cb=256):
    t, d = n.shape
    tok = pl.BlockSpec((t, cb), lambda i, s: (0, i))
    out = pl.BlockSpec((3, d // 2, cb), lambda i, s: (0, 0, i))
    return call(
        grad_qkv_kernel, "grad_qkv", (d // cb,),
        [whole(t, d)] + [tok] * 3, [out] * 2, [sds((3, d // 2, d), bf16)] * 2,
        [pltpu.VMEM((d // 2, t), bf16)] * 2,
        cost(6 * t * d * d, 20 * t * d), at, (n, dq, dk, dv),
    )


def unqkv_kernel(at_ref, x_ref, row_ref, dmid_ref, *refs):
    dq_ref, dk_ref, dv_ref, own_ref, send_ref, small_ref, acc, wk_ref = refs[16:]
    i = pl.program_id(0)
    weave_keys(refs[4:12], at_ref, wk_ref)
    w = [weave_a(refs[0:4], at_ref), wk_ref[...], weave_b(refs[12:16], at_ref)]
    e = nt(
        jnp.concatenate([dq_ref[...], dk_ref[...], dv_ref[...]], axis=1),
        jnp.concatenate(w, axis=1),
    )

    @pl.when(i == 0)
    def _():
        acc[...] = e

    @pl.when(i > 0)
    def _():
        acc[...] += e

    @pl.when(i == pl.num_programs(0) - 1)
    def _():
        e = acc[...]
        xhat, s = norm_parts(x_ref[...].astype(f32) + row_ref[0:1, :])
        d_base = dmid_ref[...] + norm_back(e, row_ref[1:2, :], xhat, s)
        half = d_base.shape[0] // 2
        own, theirs = choose(at_ref[SEQ], d_base[:half], d_base[half:])
        own_ref[...] = own.astype(bf16)
        send_ref[...] = theirs.astype(bf16)
        small_ref[...] = jnp.concatenate(
            [
                jnp.sum(d_base, axis=0, keepdims=True),
                jnp.sum(e * xhat, axis=0, keepdims=True),
                jnp.sum(e, axis=0, keepdims=True),
                jnp.zeros((5, e.shape[1]), f32),
            ],
            axis=0,
        )


def unqkv(at, x, rows, dmid, w_a, w_b, dq, dk, dv, cb=256):
    t, d = x.shape
    count = d // cb
    specs, args = qkv_columns(w_a, w_b, cb, count)
    tok = pl.BlockSpec((t, cb), lambda i, s: (0, i))
    return call(
        unqkv_kernel, "unqkv", (count,),
        [whole(t, d), whole(*rows.shape), whole(t, d)] + specs + [tok] * 3,
        [whole(t // 2, d)] * 2 + [whole(8, d)],
        [sds((t // 2, d), bf16)] * 2 + [sds((8, d), f32)],
        [pltpu.VMEM((t, d), f32), pltpu.VMEM((d, cb), bf16)],
        cost(6 * t * d * d, 30 * t * d), at, (x, rows, dmid, *args, dq, dk, dv),
    )


class Grid:
    def __init__(self, seq, rows):
        self.seq, self.rows = seq, rows
        self.known = seq == 2 and rows == 16
        at = lax.axis_index("rows")
        self.x = lax.axis_index("seq")
        self.z, self.y, self.c = at // 4, (at // 2) % 2, at % 2

    def table(self, move):
        pairs = []
        for x in range(self.seq):
            for z in range(4):
                for y in range(2):
                    for c in range(2):
                        x2, z2, y2, c2 = move(x, z, y, c)
                        pairs.append((x * 16 + z * 4 + y * 2 + c, x2 * 16 + z2 * 4 + y2 * 2 + c2))
        return pairs

    def swap(self, v, axis):
        move = {
            "x": lambda x, z, y, c: (1 - x, z, y, c),
            "y": lambda x, z, y, c: (x, z, 1 - y, c),
            "c": lambda x, z, y, c: (x, z, y, 1 - c),
        }[axis]
        return lax.ppermute(v, BOTH, self.table(move))

    def cross(self, v, bit):
        return lax.ppermute(v, BOTH, self.table(lambda x, z, y, c: (x, z ^ bit, y, c)))

    def shift(self, v, by):
        return lax.ppermute(v, BOTH, self.table(lambda x, z, y, c: (x, (z + by) % 4, y, c)))


def tie(*values):
    return lax.optimization_barrier(values)


def after(v, *first):
    return lax.optimization_barrier((v, first))[0]


def spread(v, axis, count):
    return jnp.broadcast_to(jnp.expand_dims(v, axis), v.shape[:axis] + (count,) + v.shape[axis:])


def pair(own, other, at, axis):
    shape = own.shape[:axis] + (2,) + own.shape[axis:]
    here = lax.broadcasted_iota(jnp.int32, shape, axis) == at
    return jnp.where(here, spread(own, axis, 2), spread(other, axis, 2))


def arrange_z(g, v, shifts):
    out = spread(v, 0, 4)
    place = lax.broadcasted_iota(jnp.int32, out.shape, 0)
    for k, got in enumerate(shifts):
        out = jnp.where(place == (g.z - k - 1) % 4, spread(got, 0, 4), out)
    return out


def gather_z(g, v):
    return arrange_z(g, v, [g.shift(v, k) for k in range(1, 4)])


def flat(v):
    return v.reshape(-1, v.shape[-1])


def quarters(whole_array, kind):
    v = whole_array.reshape(2, 4, 2, 2, -1, whole_array.shape[1])
    pieces = []
    for core in range(2):
        for place in range(2):
            pieces.append(flat(v[:, :, place, core] if kind == "a" else v[place, :, :, core]))
    return pieces


def keep(v, at, axis):
    return lax.dynamic_index_in_dim(v, at, axis, keepdims=False)


def add(a, b):
    return (a.astype(f32) + b.astype(f32)).astype(bf16)


def split_plane(g, a, b):
    a = add(keep(a, g.x, -5), g.swap(keep(a, 1 - g.x, -5), "x"))
    b = add(keep(b, g.y, -3), g.swap(keep(b, 1 - g.y, -3), "y"))
    a, b = yield a, b
    got_a = g.swap(keep(a, 1 - g.y, -3), "y")
    got_b = g.swap(keep(b, 1 - g.x, -4), "x")
    got_a, got_b = yield got_a, got_b
    yield add(keep(a, g.y, -3), got_a), add(keep(b, g.x, -4), got_b)


def split_z(g, v):
    total = keep(v, g.z, -3).astype(f32)
    for k in range(1, 4):
        total = total + g.shift(keep(v, (g.z + k) % 4, -3), k).astype(f32)
    return total


def halve_z(g, v):
    v = v.reshape(*v.shape[:-3], 2, 2, *v.shape[-2:])
    high, low = g.z // 2, g.z % 2
    v = keep(v, low, -3).astype(f32) + g.cross(keep(v, 1 - low, -3), 1).astype(f32)
    got = yield g.cross(keep(v, 1 - high, -3).astype(bf16), 2)
    yield keep(v, high, -3) + got.astype(f32)


def scatter_plain(own, other):
    v = jnp.stack([own.reshape(16, -1, own.shape[1]), other.reshape(16, -1, own.shape[1])], axis=1)
    return lax.psum_scatter(flat(v).astype(f32), BOTH, scatter_dimension=0, tiled=True)


def swap_seq(v):
    return lax.ppermute(v, "seq", [(0, 1), (1, 0)])


def local(
    inputs, timesteps, boundary, step_table, w_qkv, w_out, w_up, w_down,
    norm1_gain, norm1_shift, norm2_gain, norm2_shift, up_bias, down_bias, cotangent,
):
    seq, row_blocks = lax.axis_size("seq"), lax.axis_size("rows")
    g = Grid(seq, row_blocks)
    devices = seq * row_blocks
    d = inputs.shape[2]
    shard = w_qkv.shape[0]
    ff = w_up.shape[1]
    steps = step_table.shape[0]
    wide = (ff // devices) // shard
    short = (g.x < boundary[0]).astype(jnp.int32)
    zero = jnp.zeros_like(short)
    at = jnp.stack([short, g.x] + ([g.y, g.x, g.c] if g.known else [zero] * 3))

    digits = jnp.concatenate([timesteps // 128, timesteps % 128]).astype(bf16)
    shorts = jnp.concatenate(
        [norm1_gain, norm1_shift, norm2_gain, norm2_shift, down_bias, up_bias, digits]
    )
    shorts = jnp.broadcast_to(shorts[None], (devices,) + shorts.shape)
    shorts = lax.all_to_all(shorts, BOTH, split_axis=0, concat_axis=0, tiled=True)
    x_other = swap_seq(keep(inputs, 1 - g.x, 0))
    unit = w_down.shape[0] // 4
    down_wide = w_down.reshape(4, unit, d).transpose(1, 0, 2).reshape(unit, -1)

    def look_up(shorts):
        digits = shorts[:, (5 + wide) * shard :].reshape(seq, row_blocks, 2, -1)[0].astype(jnp.int32)
        all_steps = digits[:, 0] * 128 + digits[:, 1]
        hot = all_steps.T.reshape(-1)[:, None] == jnp.arange(steps, dtype=jnp.int32)[None]
        found = nn(hot.astype(bf16), step_table).astype(bf16)
        found = lax.all_to_all(found, BOTH, split_axis=0, concat_axis=0, tiled=True)
        return all_steps.reshape(-1), found

    def norm_rows(shorts, found):
        rows = jnp.stack([found] + [shorts[:, i * shard : (i + 1) * shard] for i in range(5)])
        return jnp.pad(rows.reshape(6, d).astype(f32), ((0, 2), (0, 0)))

    if g.known:
        shifts = [g.shift(w_qkv, k) for k in range(1, 4)]
        rest = jnp.concatenate([w_up, w_out, down_wide], axis=1)
        rest_2 = g.cross(rest, 2)
        first = arrange_z(g, w_qkv, shifts)
        half = d + 2 * d // 3
        a, b = first[..., :half], first[..., half:]
        a = pair(a, g.swap(a, "x"), g.x, 0)
        b = pair(b, g.swap(b, "y"), g.y, 1)
        a, b, x_other, shorts, rest_2 = tie(a, b, x_other, shorts, rest_2)
        rest = pair(rest, rest_2, g.z // 2, 0)
        rest_1 = g.cross(rest, 1)
        all_steps, found = look_up(shorts)
        a_2, b_2 = g.swap(a, "y"), g.swap(b, "x")
        a_c, b_c = g.swap(a, "c"), g.swap(b, "c")
        w_a = [flat(v) for v in (a, a_2, a_c, g.swap(a_2, "c"))]
        w_b = [flat(v) for v in (b, b_2, b_c, g.swap(b_2, "c"))]
        rest, rest_1, found, a_2, b_2 = tie(rest, rest_1, found, a_2, b_2)
        rest = pair(rest, rest_1, g.z % 2, 1)
        rest = rest.reshape(4, *rest.shape[2:])
        rows = norm_rows(shorts, found)
        x, normed_one = norm_one(at, inputs, x_other, rows)
        a, b = rest[..., : ff + d], rest[..., ff + d :]
        a = pair(a, g.swap(a, "x"), g.x, 0)
        b = pair(b, g.swap(b, "y"), g.y, 1)
        a, b, normed_one = tie(a, b, normed_one)
        a_2, b_2 = g.swap(a, "y"), g.swap(b, "x")
        a_c, b_c = g.swap(a, "c"), g.swap(b, "c")
    else:
        half = d + 2 * d // 3
        w_a, w_b, up_out, down = [
            quarters(lax.all_gather(v, BOTH, axis=0, tiled=True), kind)
            for v, kind in (
                (w_qkv[:, :half], "a"),
                (w_qkv[:, half:], "b"),
                (jnp.concatenate([w_up, w_out], axis=1), "a"),
                (down_wide, "b"),
            )
        ]
        all_steps, found = look_up(shorts)
        rows = norm_rows(shorts, found)
        x, normed_one = norm_one(at, inputs, x_other, rows)

    up_row = shorts[:, 5 * shard : (5 + wide) * shard].reshape(1, ff)
    q, k, v, attended, lse = attend(at, normed_one, w_a, w_b)
    dy_other = swap_seq(keep(cotangent, 1 - g.x, 0))
    if g.known:
        a_2, b_2, attended, dy_other = tie(a_2, b_2, attended, dy_other)
        up_out = [flat(v) for v in (a, a_2, a_c, g.swap(a_2, "c"))]
        down = [flat(v) for v in (b, b_2, b_c, g.swap(b_2, "c"))]
    middle, normed_two, dy = mix(at, x, attended, up_out, cotangent, dy_other, rows)
    block_own, block_send, d_upper, keep_down, give_down, g_up_row, g_down_row = ffn(
        at, normed_two, dy, middle, up_out, down, up_row, rows
    )
    block_other = swap_seq(block_send)
    d_middle, d_attended, keep_up, give_up, small_two = unffn(
        at, normed_two, dy, middle, d_upper, up_out, attended, rows
    )
    six = (2, 4, 2)
    if g.known:
        d_middle, d_attended, keep_up, give_up, small_two, block_other = tie(
            d_middle, d_attended, keep_up, give_up, small_two, block_other
        )
        down = add(keep_down, g.swap(give_down, "c")).reshape(*six, -1, d)
        d_attended, down = tie(d_attended, down)
        down_plane = split_plane(g, down[..., : d // 2], down[..., d // 2 :])
    back = attend_back(at, q, k, v, attended, d_attended, lse, 0, 2)
    if g.known:
        cut = (ff + d) // 2
        up = add(keep_up, g.swap(give_up, "c")).reshape(*six, -1, ff + d)
        down_half = next(down_plane)
        d_attended, up, down_half, *back = tie(d_attended, up, down_half, *back)
        up_plane = split_plane(g, up[..., :cut], up[..., cut:])
        down_got = down_plane.send(down_half)
    dq, dk, dv = attend_back(at, q, k, v, attended, d_attended, lse, 1, 2, tuple(back))
    n = normed_one
    if g.known:
        up_half = next(up_plane)
        n, up_half, dq, down_got = tie(n, up_half, dq, down_got)
        up_got = up_plane.send(up_half)
        down = jnp.concatenate(down_plane.send(down_got), axis=-1)
        down_z = halve_z(g, down)
    keep_qkv, give_qkv = grad_qkv(at, n, dq, dk, dv)
    if g.known:
        qkv = add(keep_qkv, g.swap(give_qkv, "c")).reshape(3, *six, shard, d)
        up = jnp.concatenate(up_plane.send(up_got), axis=-1)
        d_middle, qkv, up = tie(d_middle, qkv, up)
        a = jnp.concatenate([qkv[0], qkv[1, ..., : d // 2]], axis=-1)
        b = jnp.concatenate([qkv[1, ..., d // 2 :], qkv[2]], axis=-1)
        plane = split_plane(g, a, b)
    d_own, d_send, small_one = unqkv(at, x, rows, d_middle, w_a, w_b, dq, dk, dv)
    if g.known:
        ready = next(plane)
        small_one, d_send, ready, down_got = tie(small_one, d_send, ready, next(down_z))
        sum_down = down_z.send(down_got)
        up_z = halve_z(g, up)
        got = plane.send(ready)
    d_other = swap_seq(d_send)

    small = jnp.concatenate([small_one[1:3], small_two, g_down_row, small_one[0:1]], axis=0)
    small = small.reshape(-1, devices, shard).transpose(1, 0, 2).reshape(devices, -1)
    small = jnp.concatenate([small, g_up_row.reshape(devices, -1)], axis=1)
    small = lax.all_to_all(small, BOTH, split_axis=0, concat_axis=0, tiled=True)
    row_sums = small[:, 5 * shard : 6 * shard].reshape(seq, row_blocks, shard).transpose(1, 0, 2)
    row_sums = row_sums.reshape(devices, shard)
    small = jnp.sum(small, axis=0)
    if g.known:
        sum_up = up_z.send(next(up_z))
        last = jnp.concatenate(plane.send(got), axis=-1)
        d_other, last = tie(d_other, split_z(g, last))
    else:
        sum_up, sum_down = scatter_plain(keep_up, give_up), scatter_plain(keep_down, give_down)
        last = [scatter_plain(keep_qkv[i], give_qkv[i]) for i in range(3)]
        last = jnp.concatenate(last, axis=1)
    block_out, grad_inputs = pair(block_own, block_other, g.x, 0), pair(d_own, d_other, g.x, 0)
    hot = (jnp.arange(steps, dtype=jnp.int32)[:, None] == all_steps[None]).astype(f32)
    g_table = lax.dot_general(
        hot, row_sums, (((1,), (0,)), ((), ())), precision=lax.Precision.HIGHEST,
        preferred_element_type=f32,
    )
    return (
        block_out,
        grad_inputs,
        g_table,
        last,
        sum_up[:, ff:],
        sum_up[:, :ff],
        sum_down,
        *[small[i * shard : (i + 1) * shard] for i in range(4)],
        small[6 * shard :],
        small[4 * shard : 5 * shard],
    )


def solution(mesh):
    tokens, weight, vector = P("rows", "seq", None), P(BOTH, None), P(BOTH)
    table = P(None, BOTH)
    in_specs = (
        (tokens, P("rows"), P("rows"), table) + (weight,) * 4 + (vector,) * 6 + (tokens,)
    )
    out_specs = (tokens, tokens, table) + (weight,) * 4 + (vector,) * 6
    return jax.shard_map(local, mesh=mesh, in_specs=in_specs, out_specs=out_specs, check_vma=False)
```

time: 441 us -> 346 us (0.78)
  waiting for transfers between devices: 102 us -> 57.4 us
  other arithmetic: 57.9 us -> 26 us
  local copies, waits for them, and re-layouts: 50 us -> 22.1 us
  Pallas kernels: 159 us -> 171 us
    ppermute x29 -> x31, waiting for transfers between devices: 61.4 us -> 27 us  [swap(): return lax.ppermute(v, BOTH, self.table(move))]
    ppermute x21 -> x6, waiting for transfers between devices: 30.6 us -> 3.22 us  [shift(): lax.ppermute(v, BOTH, self.table(lambda x, z, y, c: (x, (z + by) % 4, y,...]
    ppermute x21 -> x6, starting transfers between devices: 31.6 us -> 11.4 us  [shift(): lax.ppermute(v, BOTH, self.table(lambda x, z, y, c: (x, (z + by) % 4, y,...]
    all_to_all x0 -> x3, waiting for transfers between devices: none -> 20 us  [the longest x1 10.6 us: look_up(): found = lax.all_to_all(found, BOTH, split_axis=0, concat_axis=0, tiled=True)]
    select_n x15 -> x7, other arithmetic: 28.2 us -> 9.02 us  [pair(): return jnp.where(here, spread(own, axis, 2), spread(other, axis, 2))]
    concatenate x11 -> x4, other arithmetic: 12.5 us -> 0.2 us  [the longest x1 0.08 us: local(): small = jnp.concatenate([small, g_up_row.reshape(devices, -1)], axis=1)]
    pallas_call x8 -> x9, Pallas kernels: 159 us -> 171 us  [call(): pl.pallas_call(kernel, grid_spec=pltpu.PrefetchScalarGridSpec(num_scalar_...]
    all_to_all x0 -> x3, starting transfers between devices: none -> 10.6 us  [the longest x1 4.13 us: local(): lax.all_to_all(shorts, BOTH, split_axis=0, concat_axis=0, tiled=True)]
  transfers between devices with their start and end apart: 54 -> 50, of which waited for: 23 -> 16; matrix products, arithmetic and copies ran while one was open for 19% -> 10% of each run, Pallas kernels for 23% -> 40%
where the time goes in v2:
time: 346 us; the launch traced here: 341 us
  Pallas kernels  171 us (49%)
  starting transfers between devices  61 us (18%)
  waiting for transfers between devices  57.4 us (17%)
  other arithmetic  26 us (8%)
  local copies, waits for them, and re-layouts  22.1 us (6%)
    pallas_call x9, Pallas kernels, call(): pl.pallas_call(kernel, grid_spec=pltpu.PrefetchScalarGridSpec(num_scalar_...  171 us
    ppermute x31, waiting for transfers between devices, swap(): return lax.ppermute(v, BOTH, self.table(move))  27 us
    ppermute x31, starting transfers between devices, swap(): return lax.ppermute(v, BOTH, self.table(move))  26 us
    convert_element_type x15, other arithmetic, add(): return (a.astype(f32) + b.astype(f32)).astype(bf16)  11.7 us
    ppermute x6, starting transfers between devices, shift(): lax.ppermute(v, BOTH, self.table(lambda x, z, y, c: (x, (z + by) % 4, y,...  11.4 us
    all_to_all x1, waiting for transfers between devices, look_up(): found = lax.all_to_all(found, BOTH, split_axis=0, concat_axis=0, tiled=True)  10.6 us
    all_to_all x1, waiting for transfers between devices, local(): lax.all_to_all(shorts, BOTH, split_axis=0, concat_axis=0, tiled=True)  9.05 us
    select_n x7, other arithmetic, pair(): return jnp.where(here, spread(own, axis, 2), spread(other, axis, 2))  9.02 us
  transfers between devices with their start and end apart: 50, of which 16 were waited for; matrix products, arithmetic and copies ran while one was open for 10% of the time, Pallas kernels for 40%

profile of v2, /device:TPU:0, one launch (start us, length us, event | category | flops | bytes accessed | tf_op | source)
XLA Modules:
  0.0 341.0 jit_solution(2748540313829633412)
XLA Ops:
  0.8 5.1 %collective-permute-start = (bf16[24,2304]{1,0:T(8,128)(2,1)}, bf16[24,2304]{1,0:T(8,128)(2,1)S(1)}, u32[]{:S(2)}, u32[]{:S(2)}) collective-permute-start(bf16[24,2304]{1,0:T(8,128)(2,1)} %param.19), channel_id=1, source_target_pairs={{0,12},{1,13},{2,14},{3,15},{4,0},{5,1},{6,2},{7,3},{8,4},{9,5},{1... | collective-permute-start | bytes 331784 | tf_op jit(solution)/shard_map/ppermute | solution.py:573
  10.5 4.1 %all-to-all-start = ((bf16[32,1,220]{2,1,0:T(2,128)(2,1)}), bf16[32,1,220]{2,1,0:T(2,128)(2,1)S(1)}, u32[]{:S(2)}, u32[]{:S(2)}) async-start(bf16[32,1,220]{2,1,0:T(2,128)(2,1)} %broadcast_in_dim.54), calls=%async_computation | async-start | bytes 65536 | tf_op jit(solution)/shard_map/all_to_all | solution.py:682
  14.7 2.7 collective-permute-start.6
  20.8 9.0 %all-to-all-done = bf16[32,1,220]{2,1,0:T(2,128)(2,1)S(1)} async-done(((bf16[32,1,220]{2,1,0:T(2,128)(2,1)}), bf16[32,1,220]{2,1,0:T(2,128)(2,1)S(1)}, u32[]{:S(2)}, u32[]{:S(2)}) %all-to-all-start) | async-done | bytes 14112 | tf_op jit(solution)/shard_map/all_to_all | solution.py:682
  30.0 2.3 collective-permute-done.3
  34.5 2.5 collective-permute-start.7
  41.2 2.5 all-to-all-start.1
  43.8 10.6 %all-to-all-done.1 = bf16[32,1,24]{2,1,0:T(2,128)(2,1)S(1)} async-done(((bf16[32,1,24]{2,1,0:T(2,128)(2,1)}), bf16[32,1,24]{2,1,0:T(2,128)(2,1)S(1)}, u32[]{:S(2)}, u32[]{:S(2)}) %all-to-all-start.1) | async-done | bytes 1568 | tf_op jit(solution)/shard_map/all_to_all | solution.py:692
  61.2 5.2 %norm_one.1 = (bf16[1024,768]{1,0:T(8,128)(2,1)}, bf16[1024,768]{1,0:T(8,128)(2,1)}) custom-call(s32[5]{0:T(128)} %stack.45.at_ref, bf16[2,512,768]{2,1,0:T(8,128)(2,1)} %own_ref.2, bf16[512,768]{1,0:T(8,128)(2,1)} %copy-done.27, f32[8,768]{1,0:T(8,128)} %pad_convert_fusion.row_ref.refs_9_), custom_call_target="tpu_custom_call" | custom-call | flops 157286 | bytes 62914 | tf_op jit(solution)/shard_map/norm_one/pallas_call | solution.py:112
  66.4 6.3 %collective-permute-done.11 = bf16[4,24,3072]{2,1,0:T(8,128)(2,1)} collective-permute-done((bf16[4,24,3072]{2,1,0:T(8,128)(2,1)}, bf16[4,24,3072]{2,1,0:T(8,128)(2,1)}, u32[]{:S(2)}, u32[]{:S(2)}) %collective-permute-start.11) | collective-permute-done | bytes 589856 | tf_op jit(solution)/shard_map/ppermute | solution.py:567
  72.7 2.4 broadcast_select_fusion.3
  75.1 2.6 collective-permute-done.10
  85.8 33.1 %attend.1 = (bf16[1024,768]{1,0:T(8,128)(2,1)}, bf16[1024,768]{1,0:T(8,128)(2,1)}, bf16[1024,768]{1,0:T(8,128)(2,1)}, bf16[1024,768]{1,0:T(8,128)(2,1)}, f32[3,4,1024]{2,1,0:T(4,128)}) custom-call(s32[5]{0:T(128)} %stack.45.at_ref, bf16[1024,768]{1,0:T(8,128)(2,1)} %get-tuple-element.145.n_ref, bf16[192,1280]{1,0:T(8,128)(2,1)} %bitcast.176, ...), custom_call_target="tpu_custom_call" | custom-call | flops 330175616 | bytes 314572 | tf_op jit(solution)/shard_map/attend/pallas_call | solution.py:112
  118.9 3.9 %collective-permute-done.18.other_ref = bf16[512,768]{1,0:T(8,128)(2,1)S(1)} collective-permute-done((bf16[512,768]{1,0:T(8,128)(2,1)S(1)}, bf16[512,768]{1,0:T(8,128)(2,1)S(1)}, u32[]{:S(2)}, u32[]{:S(2)}) %collective-permute-start.18) | collective-permute-done | bytes 786464 | tf_op jit(solution)/shard_map/ppermute | solution.py:658
  125.0 4.2 %collective-permute-done.20 = bf16[2,4,24,3840]{3,2,1,0:T(8,128)(2,1)} collective-permute-done((bf16[2,4,24,3840]{3,2,1,0:T(8,128)(2,1)S(1)}, bf16[2,4,24,3840]{3,2,1,0:T(8,128)(2,1)}, u32[]{:S(2)}, u32[]{:S(2)}) %collective-permute-start.20) | collective-permute-done | bytes 1474592 | tf_op jit(solution)/shard_map/ppermute | solution.py:567
  129.2 8.3 %mix.1 = (f32[1024,768]{1,0:T(8,128)}, bf16[1024,768]{1,0:T(8,128)(2,1)}, bf16[1024,768]{1,0:T(8,128)(2,1)}) custom-call(s32[5]{0:T(128)} %stack.45.at_ref, bf16[1024,768]{1,0:T(8,128)(2,1)} %get-tuple-element.98.x_ref, bf16[1024,768]{1,0:T(8,128)(2,1)} %get-tuple-element.106.o_ref, bf16[192,3840]{1,0:T(8,128)(2,1)} %bitcast.168, ...), custom_call_target="tpu_custom_call" | custom-call | flops 24159192 | bytes 188743 | tf_op jit(solution)/shard_map/mix/pallas_call | solution.py:112
  137.5 34.8 %ffn.1 = (bf16[512,768]{1,0:T(8,128)(2,1)}, bf16[512,768]{1,0:T(8,128)(2,1)}, bf16[1024,3072]{1,0:T(8,128)(2,1)}, bf16[1536,768]{1,0:T(8,128)(2,1)}, bf16[1536,7...) custom-call(s32[5]{0:T(128)} %stack.45.at_ref, bf16[1024,768]{1,0:T(8,128)(2,1)} %get-tuple-element.109.n_ref, ...), custom_call_target="tpu_custom_call" | custom-call | flops 386547072 | bytes 692060 | tf_op jit(solution)/shard_map/ffn/pallas_call | solution.py:112
  173.0 27.2 %unffn.1 = (f32[1024,768]{1,0:T(8,128)}, bf16[1024,768]{1,0:T(8,128)(2,1)}, bf16[384,3840]{1,0:T(8,128)(2,1)}, bf16[384,3840]{1,0:T(8,128)(2,1)}, f32[2,768]{1,0:T(2,128)}) custom-call(s32[5]{0:T(128)} %stack.45.at_ref, bf16[1024,768]{1,0:T(8,128)(2,1)} %get-tuple-element.109.n_ref, bf16[1024,768]{1,0:T(8,128)(2,1)} %get-tuple-element.110.dy_ref, ...), custom_call_target="tpu_custom_call" | custom-call | flops 241591904 | bytes 692060 | tf_op jit(solution)/shard_map/unffn/pallas_call | solution.py:112
  200.4 2.3 add_convert_fusion.1
  207.0 19.6 %attend_back_0.1 = (bf16[1024,768]{1,0:T(8,128)(2,1)}, bf16[1024,768]{1,0:T(8,128)(2,1)}, bf16[1024,768]{1,0:T(8,128)(2,1)}) custom-call(s32[5]{0:T(128)} %stack.45.at_ref, bf16[1024,768]{1,0:T(8,128)(2,1)} %get-tuple-element.130.q_ref, bf16[1024,768]{1,0:T(8,128)(2,1)} %get-tuple-element.131.k_ref, bf16[1024,768]{1,0:T(8,128)(2,1)} %get-tuple-element.132.v_ref, ...), custom_call_target="tpu_custom_call" | custom-call | flops 322122560 | bytes 125829 | tf_op jit(solution)/shard_map/attend_back_0/pallas_call | solution.py:112
  226.6 2.2 fusion.2
  230.8 2.6 add_convert_fusion
  237.7 2.0 collective-permute-start.28
  242.0 19.6 %attend_back_1.1 = (bf16[1024,768]{1,0:T(8,128)(2,1)}, bf16[1024,768]{1,0:T(8,128)(2,1)}, bf16[1024,768]{1,0:T(8,128)(2,1)}) custom-call(s32[5]{0:T(128)} %stack.45.at_ref, bf16[1024,768]{1,0:T(8,128)(2,1)} %get-tuple-element.130.q_ref, bf16[1024,768]{1,0:T(8,128)(2,1)} %get-tuple-element.131.k_ref, ...), custom_call_target="tpu_custom_call", output_to_operand_aliasing={{0}: (7, {}), {1}: (8, {}), {2}: (9, {})} | custom-call | flops 322122560 | bytes 125829 | tf_op jit(solution)/shard_map/attend_back_1/pallas_call | solution.py:112
  265.6 9.0 %grad_qkv.1 = (bf16[3,384,768]{2,1,0:T(8,128)(2,1)}, bf16[3,384,768]{2,1,0:T(8,128)(2,1)}) custom-call(s32[5]{0:T(128)} %stack.45.at_ref, bf16[1024,768]{1,0:T(8,128)(2,1)} %get-tuple-element.145.n_ref, bf16[1024,768]{1,0:T(8,128)(2,1)} %get-tuple-element.146.dq_ref.refs_16_, bf16[1024,768]{1,0:T(8,128)(2,1)} %get-tuple-element.147.dk_ref.refs_17_, ...), custom_call_target="tpu_custom_call" | custom-call | flops 72477576 | bytes 314572 | tf_op jit(solution)/shard_map/grad_qkv/pallas_call | solution.py:112
  277.4 8.2 %collective-permute-done.34 = bf16[4,24,1920]{2,1,0:T(8,128)(2,1)S(1)} collective-permute-done((bf16[4,24,1920]{2,1,0:T(8,128)(2,1)S(1)}, bf16[4,24,1920]{2,1,0:T(8,128)(2,1)S(1)}, u32[]{:S(2)}, u32[]{:S(2)}) %collective-permute-start.34) | collective-permute-done | bytes 368672 | tf_op jit(solution)/shard_map/ppermute | solution.py:567
  289.7 13.8 %unqkv.1 = (bf16[512,768]{1,0:T(8,128)(2,1)}, bf16[512,768]{1,0:T(8,128)(2,1)}, f32[8,768]{1,0:T(8,128)}) custom-call(s32[5]{0:T(128)} %stack.45.at_ref, bf16[1024,768]{1,0:T(8,128)(2,1)} %get-tuple-element.98.x_ref, f32[8,768]{1,0:T(8,128)} %pad_convert_fusion.row_ref.refs_9_, f32[1024,768]{1,0:T(8,128)} %get-tuple-element.153.dmid_ref, ...), custom_call_target="tpu_custom_call" | custom-call | flops 72477576 | bytes 471859 | tf_op jit(solution)/shard_map/unqkv/pallas_call | solution.py:112
  307.8 4.0 %all-to-all-start.2 = ((f32[32,1,240]{2,1,0:T(1,128)}), f32[32,1,240]{2,1,0:T(1,128)S(1)}, u32[]{:S(2)}, u32[]{:S(2)}) async-start(f32[32,1,240]{2,1,0:T(1,128)} %all_to_all.27), calls=%async_computation.2 | async-start | bytes 65536 | tf_op jit(solution)/shard_map/all_to_all | solution.py:801
  324.1 2.4 collective-permute-start.43
  330.5 2.9 collective-permute-done.43
  334.1 3.3 collective-permute-done.39
  337.4 3.3 broadcast_select_fusion
  (289 shorter events, 76.2 us)
Async XLA Ops:
  0.8 16.7 %collective-permute-start = (bf16[24,2304]{1,0:T(8,128)(2,1)}, bf16[24,2304]{1,0:T(8,128)(2,1)S(1)}, u32[]{:S(2)}, u32[]{:S(2)}) collective-permute-start(bf16[24,2304]{1,0:T(8,128)(2,1)} %param.19), channel_id=1, source_target_pairs={{0,12},{1,13},{2,14},{3,15},{4,0},{5,1},{6,2},{7,3},{8,4},{9,5},{1... | collective-permute-start | bytes 331784 | tf_op jit(solution)/shard_map/ppermute | solution.py:573
  8.1 25.3 %collective-permute-start.5 = (bf16[512,768]{1,0:T(8,128)(2,1)S(1)}, bf16[512,768]{1,0:T(8,128)(2,1)S(1)}, u32[]{:S(2)}, u32[]{:S(2)}) collective-permute-start(bf16[512,768]{1,0:T(8,128)(2,1)S(1)} %dynamic-slice_bitcast_fusion.1), channel_id=1, source_target_pairs={{0,16},{16,0},{1,17},{17,1},{2,18},{18,2},{3,19},{19,3},{4,20},{20... | collective-permute-start | bytes 2359304 | tf_op jit(solution)/shard_map/ppermute | solution.py:658
  10.5 19.4 %all-to-all-start = ((bf16[32,1,220]{2,1,0:T(2,128)(2,1)}), bf16[32,1,220]{2,1,0:T(2,128)(2,1)S(1)}, u32[]{:S(2)}, u32[]{:S(2)}) async-start(bf16[32,1,220]{2,1,0:T(2,128)(2,1)} %broadcast_in_dim.54), calls=%async_computation | async-start | bytes 65536 | tf_op jit(solution)/shard_map/all_to_all | solution.py:682
  14.7 18.7 %collective-permute-start.6 = (bf16[24,6912]{1,0:T(8,128)(2,1)S(1)}, bf16[24,6912]{1,0:T(8,128)(2,1)S(1)}, u32[]{:S(2)}, u32[]{:S(2)}) collective-permute-start(bf16[24,6912]{1,0:T(8,128)(2,1)S(1)} %constant_dynamic-update-slice_fusion), channel_id=1, source_target_pairs={{0,8},{1,9},{2,10},{3,11},{4,12},{5,13},{6,14},{7,15},{8,0},{9,1},... | collective-permute-start | bytes 995336 | tf_op jit(solution)/shard_map/ppermute | solution.py:570
  34.5 20.1 %collective-permute-start.7 = (bf16[2,24,6912]{2,1,0:T(8,128)(2,1)S(1)}, bf16[2,24,6912]{2,1,0:T(8,128)(2,1)}, u32[]{:S(2)}, u32[]{:S(2)}) collective-permute-start(bf16[2,24,6912]{2,1,0:T(8,128)(2,1)S(1)} %broadcast_select_fusion.4), channel_id=1, source_target_pairs={{0,4},{1,5},{2,6},{3,7},{4,0},{5,1},{6,2},{7,3},{8,12},{9,13},{10,... | collective-permute-start | bytes 1990664 | tf_op jit(solution)/shard_map/ppermute | solution.py:570
  37.0 17.5 %collective-permute-start.8 = (bf16[2,4,24,1280]{3,2,1,0:T(8,128)(2,1)S(1)}, bf16[2,4,24,1280]{3,2,1,0:T(8,128)(2,1)S(1)}, u32[]{:S(2)}, u32[]{:S(2)}) collective-permute-start(bf16[2,4,24,1280]{3,2,1,0:T(8,128)(2,1)S(1)} %broadcast_select_fusion.5), channel_id=1, source_target_pairs={{0,2},{1,3},{2,0},{3,1},{4,6},{5,7},{6,4},{7,5},{8,10},{9,11},{10,... | collective-permute-start | bytes 1474568 | tf_op jit(solution)/shard_map/ppermute | solution.py:567
  38.6 16.0 %collective-permute-start.9 = (bf16[4,2,24,1024]{3,2,1,0:T(8,128)(2,1)S(1)}, bf16[4,2,24,1024]{3,2,1,0:T(8,128)(2,1)S(1)}, u32[]{:S(2)}, u32[]{:S(2)}) collective-permute-start(bf16[4,2,24,1024]{3,2,1,0:T(8,128)(2,1)S(1)} %broadcast_select_fusion.6), channel_id=1, source_target_pairs={{0,16},{1,17},{2,18},{3,19},{4,20},{5,21},{6,22},{7,23},{8,24},{9,... | collective-permute-start | bytes 1179656 | tf_op jit(solution)/shard_map/ppermute | solution.py:567
  41.2 13.3 %all-to-all-start.1 = ((bf16[32,1,24]{2,1,0:T(2,128)(2,1)}), bf16[32,1,24]{2,1,0:T(2,128)(2,1)S(1)}, u32[]{:S(2)}, u32[]{:S(2)}) async-start(bf16[32,1,24]{2,1,0:T(2,128)(2,1)} %copy.111), calls=%async_computation.1 | async-start | bytes 32768 | tf_op jit(solution)/shard_map/all_to_all | solution.py:692
  57.2 15.4 %collective-permute-start.11 = (bf16[4,24,3072]{2,1,0:T(8,128)(2,1)}, bf16[4,24,3072]{2,1,0:T(8,128)(2,1)}, u32[]{:S(2)}, u32[]{:S(2)}) collective-permute-start(bf16[4,24,3072]{2,1,0:T(8,128)(2,1)} %slice.137), channel_id=1, source_target_pairs={{0,2},{1,3},{2,0},{3,1},{4,6},{5,7},{6,4},{7,5},{8,10},{9,11},{10,... | collective-permute-start | bytes 1769480 | tf_op jit(solution)/shard_map/ppermute | solution.py:567
  59.7 18.0 %collective-permute-start.10 = (bf16[4,24,3840]{2,1,0:T(8,128)(2,1)S(1)}, bf16[4,24,3840]{2,1,0:T(8,128)(2,1)S(1)}, u32[]{:S(2)}, u32[]{:S(2)}) collective-permute-start(bf16[4,24,3840]{2,1,0:T(8,128)(2,1)S(1)} %slice.136), channel_id=1, source_target_pairs={{0,16},{1,17},{2,18},{3,19},{4,20},{5,21},{6,22},{7,23},{8,24},{9,... | collective-permute-start | bytes 2211848 | tf_op jit(solution)/shard_map/ppermute | solution.py:567
  77.9 44.9 %collective-permute-start.12 = (bf16[2,4,24,3840]{3,2,1,0:T(8,128)(2,1)S(1)}, bf16[2,4,24,3840]{3,2,1,0:T(8,128)(2,1)S(1)}, u32[]{:S(2)}, u32[]{:S(2)}) collective-permute-start(bf16[2,4,24,3840]{3,2,1,0:T(8,128)(2,1)S(1)} %broadcast_select_fusion.2), channel_id=1, source_target_pairs={{0,2},{1,3},{2,0},{3,1},{4,6},{5,7},{6,4},{7,5},{8,10},{9,11},{10,... | collective-permute-start | bytes 4423688 | tf_op jit(solution)/shard_map/ppermute | solution.py:567
  79.5 43.4 %collective-permute-start.13 = (bf16[4,2,24,3072]{3,2,1,0:T(8,128)(2,1)}, bf16[4,2,24,3072]{3,2,1,0:T(8,128)(2,1)}, u32[]{:S(2)}, u32[]{:S(2)}) collective-permute-start(bf16[4,2,24,3072]{3,2,1,0:T(8,128)(2,1)} %broadcast_select_fusion.3), channel_id=1, source_target_pairs={{0,16},{1,17},{2,18},{3,19},{4,20},{5,21},{6,22},{7,23},{8,24},{9,... | collective-permute-start | bytes 3538952 | tf_op jit(solution)/shard_map/ppermute | solution.py:567
  80.6 42.2 %collective-permute-start.18 = (bf16[512,768]{1,0:T(8,128)(2,1)S(1)}, bf16[512,768]{1,0:T(8,128)(2,1)S(1)}, u32[]{:S(2)}, u32[]{:S(2)}) collective-permute-start(bf16[512,768]{1,0:T(8,128)(2,1)S(1)} %dynamic-slice_bitcast_fusion), channel_id=1, source_target_pairs={{0,16},{16,0},{1,17},{17,1},{2,18},{18,2},{3,19},{19,3},{4,20},{20... | collective-permute-start | bytes 2359304 | tf_op jit(solution)/shard_map/ppermute | solution.py:658
  84.9 40.1 %collective-permute-start.19 = (bf16[2,4,24,3840]{3,2,1,0:T(8,128)(2,1)S(1)}, bf16[2,4,24,3840]{3,2,1,0:T(8,128)(2,1)}, u32[]{:S(2)}, u32[]{:S(2)}) collective-permute-start(bf16[2,4,24,3840]{3,2,1,0:T(8,128)(2,1)S(1)} %broadcast_select_fusion.2), channel_id=1, source_target_pairs={{0,1},{1,0},{2,3},{3,2},{4,5},{5,4},{6,7},{7,6},{8,9},{9,8},{10,11... | collective-permute-start | bytes 4423688 | tf_op jit(solution)/shard_map/ppermute | solution.py:567
  123.7 13.8 %collective-permute-start.21 = (bf16[4,2,24,3072]{3,2,1,0:T(8,128)(2,1)}, bf16[4,2,24,3072]{3,2,1,0:T(8,128)(2,1)}, u32[]{:S(2)}, u32[]{:S(2)}) collective-permute-start(bf16[4,2,24,3072]{3,2,1,0:T(8,128)(2,1)} %broadcast_select_fusion.3), channel_id=1, source_target_pairs={{0,1},{1,0},{2,3},{3,2},{4,5},{5,4},{6,7},{7,6},{8,9},{9,8},{10,11... | collective-permute-start | bytes 3538952 | tf_op jit(solution)/shard_map/ppermute | solution.py:567
  124.2 13.3 %collective-permute-start.22 = (bf16[4,2,24,3072]{3,2,1,0:T(8,128)(2,1)}, bf16[4,2,24,3072]{3,2,1,0:T(8,128)(2,1)}, u32[]{:S(2)}, u32[]{:S(2)}) collective-permute-start(bf16[4,2,24,3072]{3,2,1,0:T(8,128)(2,1)} %collective-permute-done.13), channel_id=1, source_target_pairs={{0,1},{1,0},{2,3},{3,2},{4,5},{5,4},{6,7},{7,6},{8,9},{9,8},{10,11... | collective-permute-start | bytes 3538952 | tf_op jit(solution)/shard_map/ppermute | solution.py:567
  172.3 28.1 %collective-permute-start.24 = (bf16[1536,768]{1,0:T(8,128)(2,1)}, bf16[1536,768]{1,0:T(8,128)(2,1)}, u32[]{:S(2)}, u32[]{:S(2)}) collective-permute-start(bf16[1536,768]{1,0:T(8,128)(2,1)} %get-tuple-element.125), channel_id=1, source_target_pairs={{0,1},{1,0},{2,3},{3,2},{4,5},{5,4},{6,7},{7,6},{8,9},{9,8},{10,11... | collective-permute-start | bytes 7077896 | tf_op jit(solution)/shard_map/ppermute | solution.py:567
  172.5 27.8 %collective-permute-start.23 = (bf16[512,768]{1,0:T(8,128)(2,1)}, bf16[512,768]{1,0:T(8,128)(2,1)}, u32[]{:S(2)}, u32[]{:S(2)}) collective-permute-start(bf16[512,768]{1,0:T(8,128)(2,1)} %get-tuple-element.120), channel_id=1, source_target_pairs={{0,16},{16,0},{1,17},{17,1},{2,18},{18,2},{3,19},{19,3},{4,20},{20... | collective-permute-start | bytes 2359304 | tf_op jit(solution)/shard_map/ppermute | solution.py:658
  200.2 30.6 %collective-permute-start.25 = (bf16[384,3840]{1,0:T(8,128)(2,1)}, bf16[384,3840]{1,0:T(8,128)(2,1)}, u32[]{:S(2)}, u32[]{:S(2)}) collective-permute-start(bf16[384,3840]{1,0:T(8,128)(2,1)} %get-tuple-element.128), channel_id=1, source_target_pairs={{0,1},{1,0},{2,3},{3,2},{4,5},{5,4},{6,7},{7,6},{8,9},{9,8},{10,11... | collective-permute-start | bytes 8847368 | tf_op jit(solution)/shard_map/ppermute | solution.py:567
  203.0 23.6 %collective-permute-start.27 = (bf16[2,4,96,384]{3,2,1,0:T(8,128)(2,1)S(1)}, bf16[2,4,96,384]{3,2,1,0:T(8,128)(2,1)}, u32[]{:S(2)}, u32[]{:S(2)}) collective-permute-start(bf16[2,4,96,384]{3,2,1,0:T(8,128)(2,1)S(1)} %dynamic-slice_bitcast_fusion.4), channel_id=1, source_target_pairs={{0,2},{1,3},{2,0},{3,1},{4,6},{5,7},{6,4},{7,5},{8,10},{9,11},{10,... | collective-permute-start | bytes 1769480 | tf_op jit(solution)/shard_map/ppermute | solution.py:567
  204.9 23.9 %collective-permute-start.26 = (bf16[4,2,96,384]{3,2,0,1:T(8,128)(2,1)}, bf16[4,2,96,384]{3,2,0,1:T(8,128)(2,1)}, u32[]{:S(2)}, u32[]{:S(2)}) collective-permute-start(bf16[4,2,96,384]{3,2,0,1:T(8,128)(2,1)} %dynamic-slice_bitcast_fusion.5), channel_id=1, source_target_pairs={{0,16},{1,17},{2,18},{3,19},{4,20},{5,21},{6,22},{7,23},{8,24},{9,... | collective-permute-start | bytes 1769480 | tf_op jit(solution)/shard_map/ppermute | solution.py:567
  235.8 25.8 %collective-permute-start.29 = (bf16[2,4,24,1920]{3,2,1,0:T(8,128)(2,1)}, bf16[2,4,24,1920]{3,2,1,0:T(8,128)(2,1)}, u32[]{:S(2)}, u32[]{:S(2)}) collective-permute-start(bf16[2,4,24,1920]{3,2,1,0:T(8,128)(2,1)} %dynamic-slice_bitcast_fusion.2), channel_id=1, source_target_pairs={{0,2},{1,3},{2,0},{3,1},{4,6},{5,7},{6,4},{7,5},{8,10},{9,11},{10,... | collective-permute-start | bytes 2211848 | tf_op jit(solution)/shard_map/ppermute | solution.py:567
  237.7 25.3 %collective-permute-start.28 = (bf16[4,2,24,1920]{3,2,0,1:T(8,128)(2,1)S(1)}, bf16[4,2,24,1920]{3,2,0,1:T(8,128)(2,1)S(1)}, u32[]{:S(2)}, u32[]{:S(2)}) collective-permute-start(bf16[4,2,24,1920]{3,2,0,1:T(8,128)(2,1)S(1)} %dynamic-slice_bitcast_fusion.3), channel_id=1, source_target_pairs={{0,16},{1,17},{2,18},{3,19},{4,20},{5,21},{6,22},{7,23},{8,24},{9,... | collective-permute-start | bytes 2211848 | tf_op jit(solution)/shard_map/ppermute | solution.py:567
  239.7 23.4 %collective-permute-start.30 = (bf16[4,96,384]{2,1,0:T(8,128)(2,1)S(1)}, bf16[4,96,384]{2,1,0:T(8,128)(2,1)S(1)}, u32[]{:S(2)}, u32[]{:S(2)}) collective-permute-start(bf16[4,96,384]{2,1,0:T(8,128)(2,1)S(1)} %dynamic-slice_bitcast_fusion.11), channel_id=1, source_target_pairs={{0,2},{1,3},{2,0},{3,1},{4,6},{5,7},{6,4},{7,5},{8,10},{9,11},{10,... | collective-permute-start | bytes 884744 | tf_op jit(solution)/shard_map/ppermute | solution.py:567
  240.7 22.6 %collective-permute-start.31 = (bf16[4,96,384]{2,1,0:T(8,128)(2,1)S(1)}, bf16[4,96,384]{2,1,0:T(8,128)(2,1)S(1)}, u32[]{:S(2)}, u32[]{:S(2)}) collective-permute-start(bf16[4,96,384]{2,1,0:T(8,128)(2,1)S(1)} %dynamic-slice_bitcast_fusion.10), channel_id=1, source_target_pairs={{0,16},{1,17},{2,18},{3,19},{4,20},{5,21},{6,22},{7,23},{8,24},{9,... | collective-permute-start | bytes 884744 | tf_op jit(solution)/shard_map/ppermute | solution.py:567
  263.9 13.4 %collective-permute-start.33 = (bf16[4,24,1920]{2,1,0:T(8,128)(2,1)S(1)}, bf16[4,24,1920]{2,1,0:T(8,128)(2,1)S(1)}, u32[]{:S(2)}, u32[]{:S(2)}) collective-permute-start(bf16[4,24,1920]{2,1,0:T(8,128)(2,1)S(1)} %dynamic-slice_bitcast_fusion.8), channel_id=1, source_target_pairs={{0,2},{1,3},{2,0},{3,1},{4,6},{5,7},{6,4},{7,5},{8,10},{9,11},{10,... | collective-permute-start | bytes 1105928 | tf_op jit(solution)/shard_map/ppermute | solution.py:567
  275.5 29.8 %collective-permute-start.38 = (bf16[96,768]{1,0:T(8,128)(2,1)S(1)}, bf16[96,768]{1,0:T(8,128)(2,1)}, u32[]{:S(2)}, u32[]{:S(2)}) collective-permute-start(bf16[96,768]{1,0:T(8,128)(2,1)S(1)} %fusion.26), channel_id=1, source_target_pairs={{0,8},{1,9},{2,10},{3,11},{4,12},{5,13},{6,14},{7,15},{8,0},{9,1},... | collective-permute-start | bytes 442376 | tf_op jit(solution)/shard_map/ppermute | solution.py:570
  286.4 17.1 %collective-permute-start.45 = (bf16[2,24,3840]{2,1,0:T(8,128)(2,1)S(1)}, bf16[2,24,3840]{2,1,0:T(8,128)(2,1)S(1)}, u32[]{:S(2)}, u32[]{:S(2)}) collective-permute-start(bf16[2,24,3840]{2,1,0:T(8,128)(2,1)S(1)} %dynamic-slice_bitcast_fusion.6), channel_id=1, source_target_pairs={{0,4},{1,5},{2,6},{3,7},{4,0},{5,1},{6,2},{7,3},{8,12},{9,13},{10,... | collective-permute-start | bytes 1105928 | tf_op jit(solution)/shard_map/ppermute | solution.py:570
  287.3 17.8 %collective-permute-start.36 = (bf16[2,4,24,1152]{3,2,1,0:T(8,128)(2,1)S(1)}, bf16[2,4,24,1152]{3,2,1,0:T(8,128)(2,1)S(1)}, u32[]{:S(2)}, u32[]{:S(2)}) collective-permute-start(bf16[2,4,24,1152]{3,2,1,0:T(8,128)(2,1)S(1)} %fusion.13), channel_id=1, source_target_pairs={{0,2},{1,3},{2,0},{3,1},{4,6},{5,7},{6,4},{7,5},{8,10},{9,11},{10,... | collective-permute-start | bytes 1327112 | tf_op jit(solution)/shard_map/ppermute | solution.py:567
  288.9 16.3 %collective-permute-start.35 = (bf16[4,2,24,1152]{3,2,0,1:T(8,128)(2,1)S(1)}, bf16[4,2,24,1152]{3,2,0,1:T(8,128)(2,1)S(1)}, u32[]{:S(2)}, u32[]{:S(2)}) collective-permute-start(bf16[4,2,24,1152]{3,2,0,1:T(8,128)(2,1)S(1)} %fusion.17), channel_id=1, source_target_pairs={{0,16},{1,17},{2,18},{3,19},{4,20},{5,21},{6,22},{7,23},{8,24},{9,... | collective-permute-start | bytes 1327112 | tf_op jit(solution)/shard_map/ppermute | solution.py:567
  304.3 23.6 %collective-permute-start.46 = (bf16[24,3840]{1,0:T(8,128)(2,1)}, bf16[24,3840]{1,0:T(8,128)(2,1)}, u32[]{:S(2)}, u32[]{:S(2)}) collective-permute-start(bf16[24,3840]{1,0:T(8,128)(2,1)} %fusion.25), channel_id=1, source_target_pairs={{0,8},{1,9},{2,10},{3,11},{4,12},{5,13},{6,14},{7,15},{8,0},{9,1},... | collective-permute-start | bytes 552968 | tf_op jit(solution)/shard_map/ppermute | solution.py:570
  316.4 21.0 %collective-permute-start.39 = (bf16[512,768]{1,0:T(8,128)(2,1)}, bf16[512,768]{1,0:T(8,128)(2,1)S(1)}, u32[]{:S(2)}, u32[]{:S(2)}) collective-permute-start(bf16[512,768]{1,0:T(8,128)(2,1)} %get-tuple-element.160), channel_id=1, source_target_pairs={{0,16},{16,0},{1,17},{17,1},{2,18},{18,2},{3,19},{19,3},{4,20},{20... | collective-permute-start | bytes 2359304 | tf_op jit(solution)/shard_map/ppermute | solution.py:658
  (61 other events, 602.1 us)

commit v3 on v2

--- a/solution.py
+++ b/solution.py
@@ -187,18 +187,26 @@
 
     def run(parts):
         span = t // parts
-        for h in range(heads):
+        blocks = [(h, q0) for h in range(heads) for q0 in range(0, t, qb)]
+
+        def scores(h, q0):
             hs = slice(h * HD, (h + 1) * HD)
-            for q0 in range(0, t, qb):
-                k0 = (q0 // span) * span
-                q = q_ref[q0 : q0 + qb, hs] * bf16(0.125)
-                s = nt(k_ref[k0 : k0 + span, hs], q)
-                top = jnp.max(s, axis=0, keepdims=True)
-                p = jnp.exp2((s - top) * f32(LOG2E))
-                total = jnp.sum(p, axis=0, keepdims=True)
-                probs = (p * (1.0 / total)).astype(bf16)
-                o_ref[q0 : q0 + qb, hs] = tn(probs, v_ref[k0 : k0 + span, hs]).astype(bf16)
-                lse_ref[0, h : h + 1, q0 : q0 + qb] = top + jnp.log(total)
+            k0 = (q0 // span) * span
+            return nt(k_ref[k0 : k0 + span, hs], q_ref[q0 : q0 + qb, hs] * bf16(0.125))
+
+        ahead = scores(*blocks[0])
+        for i, (h, q0) in enumerate(blocks):
+            s = ahead
+            if i + 1 < len(blocks):
+                ahead = scores(*blocks[i + 1])
+            hs = slice(h * HD, (h + 1) * HD)
+            k0 = (q0 // span) * span
+            top = jnp.max(s, axis=0, keepdims=True)
+            p = jnp.exp2((s - top) * f32(LOG2E))
+            total = jnp.sum(p, axis=0, keepdims=True)
+            probs = (p * (1.0 / total)).astype(bf16)
+            o_ref[q0 : q0 + qb, hs] = tn(probs, v_ref[k0 : k0 + span, hs]).astype(bf16)
+            lse_ref[0, h : h + 1, q0 : q0 + qb] = top + jnp.log(total)
 
     short = at_ref[SHORT]
 
@@ -211,7 +219,7 @@
         run(2)
 
 
-def attend(at, n, w_a, w_b, heads=4, qb=256):
+def attend(at, n, w_a, w_b, heads=4, qb=512):
     t, d = n.shape
     c = heads * HD
     groups = d // c
@@ -287,37 +295,33 @@
 
 
 def mix_kernel(
-    at_ref, x_ref, o_ref, w0_ref, w1_ref, w2_ref, w3_ref, own_ref, other_ref, row_ref,
-    mid_ref, n_ref, dy_ref, w_ref,
+    at_ref, x_ref, o_ref, w0_ref, w1_ref, w2_ref, w3_ref, row_ref, mid_ref, n_ref, w_ref,
 ):
     @pl.when(pl.program_id(0) == 0)
     def _():
         w_ref[...] = weave_a((w0_ref, w1_ref, w2_ref, w3_ref), at_ref)
 
-    ahead = pl.program_id(0) // (pl.num_programs(0) // 2) == at_ref[SEQ]
-    dy_ref[...] = jnp.where(ahead, own_ref[0].astype(f32), other_ref[...].astype(f32)).astype(bf16)
     mid = x_ref[...].astype(f32) + row_ref[0:1, :] + nn(o_ref[...], w_ref[...])
     mid_ref[...] = mid
     xhat, _ = norm_parts(mid)
     n_ref[...] = (xhat * row_ref[3:4, :] + row_ref[4:5, :]).astype(bf16)
 
 
-def mix(at, x, o, up_out, both, other, rows, tb=256):
+def last_columns(pieces, width):
+    return [
+        pl.BlockSpec((p.shape[0], width), (lambda k: lambda i, s: (0, k))(p.shape[1] // width - 1))
+        for p in pieces
+    ]
+
+
+def mix(at, x, o, out, rows, tb=256):
     t, d = x.shape
-    steps = other.shape[0] // tb
     tok = pl.BlockSpec((tb, d), lambda i, s: (i, 0))
-    height, width = up_out[0].shape
     return call(
         mix_kernel, "mix", (t // tb,),
-        [tok, tok]
-        + [pl.BlockSpec((height, d), lambda i, s: (0, width // d - 1))] * 4
-        + [
-            pl.BlockSpec((1, tb, d), lambda i, s: (s[SEQ], i % steps, 0)),
-            pl.BlockSpec((tb, d), lambda i, s: (i % steps, 0)),
-            whole(*rows.shape),
-        ],
-        [tok] * 3, [sds((t, d), f32), sds((t, d), bf16), sds((t, d), bf16)],
-        [pltpu.VMEM((d, d), bf16)], cost(2 * t * d * d, 12 * t * d), at, (x, o, *up_out, both, other, rows),
+        [tok, tok] + last_columns(out, d) + [whole(*rows.shape)],
+        [tok] * 2, [sds((t, d), f32), sds((t, d), bf16)],
+        [pltpu.VMEM((d, d), bf16)], cost(2 * t * d * d, 12 * t * d), at, (x, o, *out, rows),
     )
 
 
@@ -332,13 +336,18 @@
     return jnp.where(u >= 0, 1.0 - tail, tail), e * f32(0.3989422804014327)
 
 
-def ffn_kernel(at_ref, n_ref, dy_ref, mid_ref, *refs):
-    ub_ref, row_ref, own_ref, send_ref, du_ref, keep_ref, give_ref, gub_ref, small_ref, acc, act = refs[8:]
+def ffn_kernel(at_ref, n_ref, here_ref, there_ref, there_2_ref, mid_ref, *refs):
+    ub_ref, row_ref, own_ref, send_ref, du_ref, keep_ref, give_ref, gub_ref, small_ref, dy_ref, acc, act = refs[8:]
     j = pl.program_id(0)
 
     @pl.when(j == 0)
     def _():
         acc[...] = mid_ref[...] + row_ref[5:6, :]
+        there = jnp.concatenate([there_ref[...].astype(f32), there_2_ref[...].astype(f32)], axis=0)
+        halves = choose(at_ref[SEQ], here_ref[0].astype(f32), there)
+        half = there.shape[0]
+        dy_ref[:half, :] = halves[0].astype(bf16)
+        dy_ref[half:, :] = halves[1].astype(bf16)
 
     wu = weave_a(refs[:4], at_ref)
     other = (j // (pl.num_programs(0) // 2)) != at_ref[LAST_B]
@@ -387,7 +396,7 @@
         small_ref[...] = jnp.sum(dy_ref[...].astype(f32), axis=0, keepdims=True)
 
 
-def ffn(at, n, dy, mid, up_out, down, up_bias, rows):
+def ffn(at, n, both, other, mid, up_out, down, up_bias, rows):
     t, d = n.shape
     ff = up_bias.shape[1]
     fb = ff // 4
@@ -395,28 +404,28 @@
     chunk = pl.BlockSpec((fb // 2, d), lambda j, s: (j, 0))
     return call(
         ffn_kernel, "ffn", (4,),
-        [whole(t, d)] * 3
+        [whole(t, d), pl.BlockSpec((1, t // 2, d), lambda j, s: (s[SEQ], 0, 0)), whole(t // 4, d), whole(t // 4, d)]
+        + [whole(t, d)]
         + [pl.BlockSpec((high, fb), lambda j, s: (0, j))] * 4
         + [pl.BlockSpec((low // 2, 4 * d), lambda j, s: (j % 2, 0))] * 4
         + [pl.BlockSpec((1, fb), lambda j, s: (0, j)), whole(*rows.shape)],
         [whole(t // 2, d)] * 2
         + [pl.BlockSpec((t, fb), lambda j, s: (0, j)), chunk, chunk]
-        + [pl.BlockSpec((1, fb), lambda j, s: (0, j)), whole(1, d)],
+        + [pl.BlockSpec((1, fb), lambda j, s: (0, j)), whole(1, d), whole(t, d)],
         [sds((t // 2, d), bf16)] * 2
         + [sds((t, ff), bf16)]
         + [sds((ff // 2, d), bf16)] * 2
-        + [sds((1, ff), f32), sds((1, d), f32)],
+        + [sds((1, ff), f32), sds((1, d), f32), sds((t, d), bf16)],
         [pltpu.VMEM((t, d), f32), pltpu.VMEM((t, fb), bf16)],
         cost(8 * t * d * ff, 20 * t * d + 8 * d * ff, 2 * t * ff),
-        at, (n, dy, mid, *up_out, *down, up_bias, rows),
-    )
-
-
-def unffn_kernel(at_ref, n_ref, dy_ref, mid_ref, du_ref, w0_ref, w1_ref, w2_ref, w3_ref, o_ref, row_ref, *refs):
-    dmid_ref, do_ref, keep_ref, give_ref, small_ref, acc, turned, turned_2 = refs
+        at, (n, both, *other, mid, *up_out, *down, up_bias, rows),
+    )
+
+
+def unffn_kernel(at_ref, n_ref, dy_ref, mid_ref, du_ref, o_ref, row_ref, *refs):
+    dmid_ref, do_ref, keep_ref, give_ref, small_ref, acc, turned, turned_2 = refs[8:]
     j = pl.program_id(0)
     last = pl.num_programs(0) - 1
-    w = weave_a((w0_ref, w1_ref, w2_ref, w3_ref), at_ref)
 
     @pl.when(j == 0)
     def _():
@@ -426,6 +435,7 @@
     @pl.when(j < last)
     def _():
         du = du_ref[...]
+        w = weave_a(refs[:4], at_ref)
         keep_ref[...] = nn(turned[...], du).astype(bf16)
         give_ref[...] = nn(turned_2[...], du).astype(bf16)
         acc[...] += nt(du, w)
@@ -440,13 +450,13 @@
         dmid = dy_ref[...].astype(f32) + norm_back(e, row_ref[3:4, :], xhat, s)
         dmid_ref[...] = dmid
         db = dmid.astype(bf16)
-        do_ref[...] = nt(db, w).astype(bf16)
-        own, other = unweave(tn(o_ref[...], db), at_ref, w.shape[0] // 32)
+        do_ref[...] = nt(db, weave_a(refs[4:8], at_ref)).astype(bf16)
+        own, other = unweave(tn(o_ref[...], db), at_ref, db.shape[1] // 32)
         keep_ref[...] = own.astype(bf16)
         give_ref[...] = other.astype(bf16)
 
 
-def unffn(at, n, dy, mid, du, up_out, o, rows):
+def unffn(at, n, dy, mid, du, up, out, o, rows):
     t, d = n.shape
     ff = du.shape[1]
     count = ff // d
@@ -455,13 +465,14 @@
         unffn_kernel, "unffn", (count + 1,),
         [whole(t, d)] * 3
         + [pl.BlockSpec((t, d), lambda j, s: (0, jnp.minimum(j, count - 1)))]
-        + [pl.BlockSpec((up_out[0].shape[0], d), lambda j, s: (0, j))] * 4
-        + [whole(t, d), whole(*rows.shape)],
+        + [whole(t, d), whole(*rows.shape)]
+        + [pl.BlockSpec((p.shape[0], d), lambda j, s: (0, jnp.minimum(j, count - 1))) for p in up]
+        + last_columns(out, d),
         [whole(t, d)] * 2 + [cols] * 2 + [whole(2, d)],
         [sds((t, d), f32), sds((t, d), bf16)] + [sds((d // 2, ff + d), bf16)] * 2 + [sds((2, d), f32)],
         [pltpu.VMEM((t, d), f32)] + [pltpu.VMEM((d // 2, t), bf16)] * 2,
         cost(4 * t * d * (ff + d), 20 * t * d + 8 * d * ff),
-        at, (n, dy, mid, du, *up_out, o, rows),
+        at, (n, dy, mid, du, o, rows, *up, *out),
     )
 
 
@@ -741,18 +752,23 @@
 
     up_row = shorts[:, 5 * shard : (5 + wide) * shard].reshape(1, ff)
     q, k, v, attended, lse = attend(at, normed_one, w_a, w_b)
-    dy_other = swap_seq(keep(cotangent, 1 - g.x, 0))
+    dy_send = keep(cotangent, 1 - g.x, 0)
+    dy_other = [swap_seq(v) for v in jnp.split(dy_send, 2)]
     if g.known:
-        a_2, b_2, attended, dy_other = tie(a_2, b_2, attended, dy_other)
+        q, k, v, lse, attended, dy_other[0] = tie(q, k, v, lse, attended, dy_other[0])
+        a_2, b_2, attended = tie(a_2, b_2, attended)
+        out = [flat(v) for v in (a, a_2, a_c, g.swap(a_2[..., ff:], "c"))]
         up_out = [flat(v) for v in (a, a_2, a_c, g.swap(a_2, "c"))]
         down = [flat(v) for v in (b, b_2, b_c, g.swap(b_2, "c"))]
-    middle, normed_two, dy = mix(at, x, attended, up_out, cotangent, dy_other, rows)
-    block_own, block_send, d_upper, keep_down, give_down, g_up_row, g_down_row = ffn(
-        at, normed_two, dy, middle, up_out, down, up_row, rows
+    else:
+        out = up_out
+    middle, normed_two = mix(at, x, attended, out, rows)
+    block_own, block_send, d_upper, keep_down, give_down, g_up_row, g_down_row, dy = ffn(
+        at, normed_two, cotangent, dy_other, middle, up_out, down, up_row, rows
     )
     block_other = swap_seq(block_send)
     d_middle, d_attended, keep_up, give_up, small_two = unffn(
-        at, normed_two, dy, middle, d_upper, up_out, attended, rows
+        at, normed_two, dy, middle, d_upper, up_out, out, attended, rows
     )
     six = (2, 4, 2)
     if g.known:
@@ -760,7 +776,8 @@
             d_middle, d_attended, keep_up, give_up, small_two, block_other
         )
         down = add(keep_down, g.swap(give_down, "c")).reshape(*six, -1, d)
-        d_attended, down = tie(d_attended, down)
+        block_out = pair(block_own, block_other, g.x, 0)
+        d_attended, down, block_out = tie(d_attended, down, block_out)
         down_plane = split_plane(g, down[..., : d // 2], down[..., d // 2 :])
     back = attend_back(at, q, k, v, attended, d_attended, lse, 0, 2)
     if g.known:
@@ -780,6 +797,7 @@
         down_z = halve_z(g, down)
     keep_qkv, give_qkv = grad_qkv(at, n, dq, dk, dv)
     if g.known:
+        keep_qkv, up_got = tie(keep_qkv, up_got)
         qkv = add(keep_qkv, g.swap(give_qkv, "c")).reshape(3, *six, shard, d)
         up = jnp.concatenate(up_plane.send(up_got), axis=-1)
         d_middle, qkv, up = tie(d_middle, qkv, up)
@@ -810,7 +828,8 @@
         sum_up, sum_down = scatter_plain(keep_up, give_up), scatter_plain(keep_down, give_down)
         last = [scatter_plain(keep_qkv[i], give_qkv[i]) for i in range(3)]
         last = jnp.concatenate(last, axis=1)
-    block_out, grad_inputs = pair(block_own, block_other, g.x, 0), pair(d_own, d_other, g.x, 0)
+        block_out = pair(block_own, block_other, g.x, 0)
+    grad_inputs = pair(d_own, d_other, g.x, 0)
     hot = (jnp.arange(steps, dtype=jnp.int32)[:, None] == all_steps[None]).astype(f32)
     g_table = lax.dot_general(
         hot, row_sums, (((1,), (0,)), ((), ())), precision=lax.Precision.HIGHEST,

time: 346 us -> 335 us (0.968)
  Pallas kernels: 171 us -> 141 us
  starting transfers between devices: 61 us -> 73.1 us
  other arithmetic: 26 us -> 31.5 us
    pallas_call x9, Pallas kernels: 171 us -> 141 us  [call(): pl.pallas_call(kernel, grid_spec=pltpu.PrefetchScalarGridSpec(num_scalar_...]
    ppermute x31 -> x32, waiting for transfers between devices: 27 us -> 19.7 us  [swap(): return lax.ppermute(v, BOTH, self.table(move))]
    ppermute x31 -> x32, starting transfers between devices: 26 us -> 32.1 us  [swap(): return lax.ppermute(v, BOTH, self.table(move))]
    ppermute x4 -> x5, starting transfers between devices: 4.16 us -> 8.29 us  [swap_seq(): return lax.ppermute(v, 'seq', [(0, 1), (1, 0)])]
    ppermute x4 -> x5, waiting for transfers between devices: 7.16 us -> 10.5 us  [swap_seq(): return lax.ppermute(v, 'seq', [(0, 1), (1, 0)])]
    select_n x7 -> x8, other arithmetic: 9.02 us -> 11.5 us  [pair(): return jnp.where(here, spread(own, axis, 2), spread(other, axis, 2))]
  transfers between devices with their start and end apart: 50 -> 52, of which waited for: 16 -> 16; matrix products, arithmetic and copies ran while one was open for 10% -> 13% of each run, Pallas kernels for 40% -> 32%
where the time goes in v3:
time: 335 us; the launch traced here: 330 us
  Pallas kernels  141 us (42%)
  starting transfers between devices  73.1 us (22%)
  waiting for transfers between devices  55.7 us (17%)
  other arithmetic  31.5 us (9%)
  local copies, waits for them, and re-layouts  24.7 us (7%)
    pallas_call x9, Pallas kernels, call(): pl.pallas_call(kernel, grid_spec=pltpu.PrefetchScalarGridSpec(num_scalar_...  141 us
    ppermute x32, starting transfers between devices, swap(): return lax.ppermute(v, BOTH, self.table(move))  32.1 us
    ppermute x32, waiting for transfers between devices, swap(): return lax.ppermute(v, BOTH, self.table(move))  19.7 us
    convert_element_type x15, other arithmetic, add(): return (a.astype(f32) + b.astype(f32)).astype(bf16)  13.6 us
    all_to_all x1, waiting for transfers between devices, look_up(): found = lax.all_to_all(found, BOTH, split_axis=0, concat_axis=0, tiled=True)  11.7 us
    select_n x8, other arithmetic, pair(): return jnp.where(here, spread(own, axis, 2), spread(other, axis, 2))  11.5 us
    ppermute x6, starting transfers between devices, shift(): lax.ppermute(v, BOTH, self.table(lambda x, z, y, c: (x, (z + by) % 4, y,...  11.4 us
    ppermute x5, waiting for transfers between devices, swap_seq(): return lax.ppermute(v, 'seq', [(0, 1), (1, 0)])  10.5 us
  transfers between devices with their start and end apart: 52, of which 16 were waited for; matrix products, arithmetic and copies ran while one was open for 13% of the time, Pallas kernels for 32%

profile of v3, /device:TPU:0, one launch (start us, length us, event | category | flops | bytes accessed | tf_op | source)
XLA Modules:
  0.0 329.9 jit_solution(9914906761615595219)
XLA Ops:
  0.8 5.1 %collective-permute-start = (bf16[24,2304]{1,0:T(8,128)(2,1)}, bf16[24,2304]{1,0:T(8,128)(2,1)S(1)}, u32[]{:S(2)}, u32[]{:S(2)}) collective-permute-start(bf16[24,2304]{1,0:T(8,128)(2,1)} %param.19), channel_id=1, source_target_pairs={{0,12},{1,13},{2,14},{3,15},{4,0},{5,1},{6,2},{7,3},{8,4},{9,5},{1... | collective-permute-start | bytes 331784 | tf_op jit(solution)/shard_map/ppermute | solution.py:584
  10.5 4.1 %all-to-all-start = ((bf16[32,1,220]{2,1,0:T(2,128)(2,1)}), bf16[32,1,220]{2,1,0:T(2,128)(2,1)S(1)}, u32[]{:S(2)}, u32[]{:S(2)}) async-start(bf16[32,1,220]{2,1,0:T(2,128)(2,1)} %broadcast_in_dim.54), calls=%async_computation | async-start | bytes 65536 | tf_op jit(solution)/shard_map/all_to_all | solution.py:693
  14.7 2.7 collective-permute-start.6
  20.8 9.0 %all-to-all-done = bf16[32,1,220]{2,1,0:T(2,128)(2,1)S(1)} async-done(((bf16[32,1,220]{2,1,0:T(2,128)(2,1)}), bf16[32,1,220]{2,1,0:T(2,128)(2,1)S(1)}, u32[]{:S(2)}, u32[]{:S(2)}) %all-to-all-start) | async-done | bytes 14112 | tf_op jit(solution)/shard_map/all_to_all | solution.py:693
  40.4 2.5 all-to-all-start.1
  43.1 11.7 %all-to-all-done.1 = bf16[32,1,24]{2,1,0:T(2,128)(2,1)S(1)} async-done(((bf16[32,1,24]{2,1,0:T(2,128)(2,1)}), bf16[32,1,24]{2,1,0:T(2,128)(2,1)S(1)}, u32[]{:S(2)}, u32[]{:S(2)}) %all-to-all-start.1) | async-done | bytes 1568 | tf_op jit(solution)/shard_map/all_to_all | solution.py:703
  61.2 5.2 %norm_one.1 = (bf16[1024,768]{1,0:T(8,128)(2,1)}, bf16[1024,768]{1,0:T(8,128)(2,1)}) custom-call(s32[5]{0:T(128)} %stack.45.at_ref, bf16[2,512,768]{2,1,0:T(8,128)(2,1)} %own_ref.1, bf16[512,768]{1,0:T(8,128)(2,1)} %copy-done.17, f32[8,768]{1,0:T(8,128)} %pad_convert_fusion.row_ref.refs_9_), custom_call_target="tpu_custom_call" | custom-call | flops 157286 | bytes 62914 | tf_op jit(solution)/shard_map/norm_one/pallas_call | solution.py:112
  66.5 6.2 %collective-permute-done.11 = bf16[4,24,3072]{2,1,0:T(8,128)(2,1)} collective-permute-done((bf16[4,24,3072]{2,1,0:T(8,128)(2,1)}, bf16[4,24,3072]{2,1,0:T(8,128)(2,1)}, u32[]{:S(2)}, u32[]{:S(2)}) %collective-permute-start.11) | collective-permute-done | bytes 589856 | tf_op jit(solution)/shard_map/ppermute | solution.py:578
  72.7 2.4 broadcast_select_fusion.3
  75.2 2.6 collective-permute-done.10
  81.7 2.0 collective-permute-done.16
  83.9 1.9 dynamic-slice_bitcast_fusion.5
  88.2 20.2 %attend.1 = (bf16[1024,768]{1,0:T(8,128)(2,1)}, bf16[1024,768]{1,0:T(8,128)(2,1)}, bf16[1024,768]{1,0:T(8,128)(2,1)}, bf16[1024,768]{1,0:T(8,128)(2,1)}, f32[3,4,1024]{2,1,0:T(4,128)}) custom-call(s32[5]{0:T(128)} %stack.45.at_ref, bf16[1024,768]{1,0:T(8,128)(2,1)} %get-tuple-element.160.n_ref, bf16[192,1280]{1,0:T(8,128)(2,1)} %bitcast.185, ...), custom_call_target="tpu_custom_call" | custom-call | flops 330175616 | bytes 314572 | tf_op jit(solution)/shard_map/attend/pallas_call | solution.py:112
  108.4 7.2 %collective-permute-done.18.there_ref = bf16[256,768]{1,0:T(8,128)(2,1)S(1)} collective-permute-done((bf16[256,768]{1,0:T(8,128)(2,1)S(1)}, bf16[256,768]{1,0:T(8,128)(2,1)S(1)}, u32[]{:S(2)}, u32[]{:S(2)}) %collective-permute-start.18) | collective-permute-done | bytes 393248 | tf_op jit(solution)/shard_map/ppermute | solution.py:669
  116.3 3.2 collective-permute-start.21
  123.8 6.8 %mix.1 = (f32[1024,768]{1,0:T(8,128)}, bf16[1024,768]{1,0:T(8,128)(2,1)}) custom-call(s32[5]{0:T(128)} %stack.45.at_ref, bf16[1024,768]{1,0:T(8,128)(2,1)} %get-tuple-element.107.x_ref, bf16[1024,768]{1,0:T(8,128)(2,1)} %get-tuple-element.120.o_ref, bf16[192,3840]{1,0:T(8,128)(2,1)} %bitcast.169, bf16[192,3840]{1,0:T(8,128)(2,1)} %bitcast.175, ...), custom_call_target="tpu_custom_call" | custom-call | flops 24159192 | bytes 188743 | tf_op jit(solution)/shard_map/mix/pallas_call | solution.py:112
  130.7 35.7 %ffn.1 = (bf16[512,768]{1,0:T(8,128)(2,1)}, bf16[512,768]{1,0:T(8,128)(2,1)}, bf16[1024,3072]{1,0:T(8,128)(2,1)}, bf16[1536,768]{1,0:T(8,128)(2,1)}, bf16[1536,7...) custom-call(s32[5]{0:T(128)} %stack.45.at_ref, ...), custom_call_target="tpu_custom_call" | custom-call | flops 386547072 | bytes 692060 | tf_op jit(solution)/shard_map/ffn/pallas_call | solution.py:112
  168.1 24.3 %unffn.1 = (f32[1024,768]{1,0:T(8,128)}, bf16[1024,768]{1,0:T(8,128)(2,1)}, bf16[384,3840]{1,0:T(8,128)(2,1)}, bf16[384,3840]{1,0:T(8,128)(2,1)}, f32[2,768]{1,0:T(2,128)}) custom-call(s32[5]{0:T(128)} %stack.45.at_ref, bf16[1024,768]{1,0:T(8,128)(2,1)} %get-tuple-element.122.n_ref, bf16[1024,768]{1,0:T(8,128)(2,1)} %get-tuple-element.126.dy_ref, ...), custom_call_target="tpu_custom_call" | custom-call | flops 241591904 | bytes 692060 | tf_op jit(solution)/shard_map/unffn/pallas_call | solution.py:112
  192.6 2.6 broadcast_select_fusion.1
  200.3 13.0 %attend_back_0.1 = (bf16[1024,768]{1,0:T(8,128)(2,1)}, bf16[1024,768]{1,0:T(8,128)(2,1)}, bf16[1024,768]{1,0:T(8,128)(2,1)}) custom-call(s32[5]{0:T(128)} %stack.45.at_ref, bf16[1024,768]{1,0:T(8,128)(2,1)} %get-tuple-element.145.q_ref, bf16[1024,768]{1,0:T(8,128)(2,1)} %get-tuple-element.146.k_ref, bf16[1024,768]{1,0:T(8,128)(2,1)} %get-tuple-element.147.v_ref, ...), custom_call_target="tpu_custom_call" | custom-call | flops 322122560 | bytes 125829 | tf_op jit(solution)/shard_map/attend_back_0/pallas_call | solution.py:112
  213.3 2.2 fusion.2
  215.4 2.0 fusion.3
  217.5 2.6 add_convert_fusion
  222.4 7.1 %collective-permute-start.31 = (bf16[2,4,24,1920]{3,2,1,0:T(8,128)(2,1)}, bf16[2,4,24,1920]{3,2,1,0:T(8,128)(2,1)}, u32[]{:S(2)}, u32[]{:S(2)}) collective-permute-start(bf16[2,4,24,1920]{3,2,1,0:T(8,128)(2,1)} %dynamic-slice_bitcast_fusion.1), channel_id=1, source_target_pairs={{0,2},{1,3},{2,0},{3,1},{4,6},{5,7},{6,4},{7,5},{8,10},{9,11},{10,... | collective-permute-start | bytes 2211848 | tf_op jit(solution)/shard_map/ppermute | solution.py:578
  234.3 13.0 %attend_back_1.1 = (bf16[1024,768]{1,0:T(8,128)(2,1)}, bf16[1024,768]{1,0:T(8,128)(2,1)}, bf16[1024,768]{1,0:T(8,128)(2,1)}) custom-call(s32[5]{0:T(128)} %stack.45.at_ref, bf16[1024,768]{1,0:T(8,128)(2,1)} %get-tuple-element.145.q_ref, bf16[1024,768]{1,0:T(8,128)(2,1)} %get-tuple-element.146.k_ref, ...), custom_call_target="tpu_custom_call", output_to_operand_aliasing={{0}: (7, {}), {1}: (8, {}), {2}: (9, {})} | custom-call | flops 322122560 | bytes 125829 | tf_op jit(solution)/shard_map/attend_back_1/pallas_call | solution.py:112
  249.6 4.5 %collective-permute-done.33 = bf16[4,96,384]{2,1,0:T(8,128)(2,1)S(1)} collective-permute-done((bf16[4,96,384]{2,1,0:T(8,128)(2,1)S(1)}, bf16[4,96,384]{2,1,0:T(8,128)(2,1)S(1)}, u32[]{:S(2)}, u32[]{:S(2)}) %collective-permute-start.33) | collective-permute-done | bytes 294944 | tf_op jit(solution)/shard_map/ppermute | solution.py:578
  259.3 9.3 %grad_qkv.1 = (bf16[3,384,768]{2,1,0:T(8,128)(2,1)}, bf16[3,384,768]{2,1,0:T(8,128)(2,1)}) custom-call(s32[5]{0:T(128)} %stack.45.at_ref, bf16[1024,768]{1,0:T(8,128)(2,1)} %get-tuple-element.160.n_ref, bf16[1024,768]{1,0:T(8,128)(2,1)} %get-tuple-element.161.dq_ref.refs_16_, bf16[1024,768]{1,0:T(8,128)(2,1)} %get-tuple-element.162.dk_ref.refs_17_, ...), custom_call_target="tpu_custom_call" | custom-call | flops 72477576 | bytes 314572 | tf_op jit(solution)/shard_map/grad_qkv/pallas_call | solution.py:112
  279.1 13.6 %unqkv.1 = (bf16[512,768]{1,0:T(8,128)(2,1)}, bf16[512,768]{1,0:T(8,128)(2,1)}, f32[8,768]{1,0:T(8,128)}) custom-call(s32[5]{0:T(128)} %stack.45.at_ref, bf16[1024,768]{1,0:T(8,128)(2,1)} %get-tuple-element.107.x_ref, f32[8,768]{1,0:T(8,128)} %pad_convert_fusion.row_ref.refs_9_, f32[1024,768]{1,0:T(8,128)} %get-tuple-element.171.dmid_ref, ...), custom_call_target="tpu_custom_call" | custom-call | flops 72477576 | bytes 471859 | tf_op jit(solution)/shard_map/unqkv/pallas_call | solution.py:112
  298.3 4.4 %all-to-all-start.2 = ((f32[32,1,240]{2,1,0:T(1,128)}), f32[32,1,240]{2,1,0:T(1,128)S(1)}, u32[]{:S(2)}, u32[]{:S(2)}) async-start(f32[32,1,240]{2,1,0:T(1,128)} %all_to_all.27), calls=%async_computation.2 | async-start | bytes 65536 | tf_op jit(solution)/shard_map/all_to_all | solution.py:819
  314.9 2.4 collective-permute-start.45
  321.4 2.9 collective-permute-done.45
  325.0 3.3 collective-permute-done.41
  (283 shorter events, 91.2 us)
Async XLA Ops:
  0.8 16.7 %collective-permute-start = (bf16[24,2304]{1,0:T(8,128)(2,1)}, bf16[24,2304]{1,0:T(8,128)(2,1)S(1)}, u32[]{:S(2)}, u32[]{:S(2)}) collective-permute-start(bf16[24,2304]{1,0:T(8,128)(2,1)} %param.19), channel_id=1, source_target_pairs={{0,12},{1,13},{2,14},{3,15},{4,0},{5,1},{6,2},{7,3},{8,4},{9,5},{1... | collective-permute-start | bytes 331784 | tf_op jit(solution)/shard_map/ppermute | solution.py:584
  8.1 25.3 %collective-permute-start.5 = (bf16[512,768]{1,0:T(8,128)(2,1)S(1)}, bf16[512,768]{1,0:T(8,128)(2,1)S(1)}, u32[]{:S(2)}, u32[]{:S(2)}) collective-permute-start(bf16[512,768]{1,0:T(8,128)(2,1)S(1)} %dynamic-slice_bitcast_fusion), channel_id=1, source_target_pairs={{0,16},{16,0},{1,17},{17,1},{2,18},{18,2},{3,19},{19,3},{4,20},{20... | collective-permute-start | bytes 2359304 | tf_op jit(solution)/shard_map/ppermute | solution.py:669
  10.5 19.4 %all-to-all-start = ((bf16[32,1,220]{2,1,0:T(2,128)(2,1)}), bf16[32,1,220]{2,1,0:T(2,128)(2,1)S(1)}, u32[]{:S(2)}, u32[]{:S(2)}) async-start(bf16[32,1,220]{2,1,0:T(2,128)(2,1)} %broadcast_in_dim.54), calls=%async_computation | async-start | bytes 65536 | tf_op jit(solution)/shard_map/all_to_all | solution.py:693
  14.7 18.7 %collective-permute-start.6 = (bf16[24,6912]{1,0:T(8,128)(2,1)S(1)}, bf16[24,6912]{1,0:T(8,128)(2,1)}, u32[]{:S(2)}, u32[]{:S(2)}) collective-permute-start(bf16[24,6912]{1,0:T(8,128)(2,1)S(1)} %constant_dynamic-update-slice_fusion), channel_id=1, source_target_pairs={{0,8},{1,9},{2,10},{3,11},{4,12},{5,13},{6,14},{7,15},{8,0},{9,1},... | collective-permute-start | bytes 995336 | tf_op jit(solution)/shard_map/ppermute | solution.py:581
  34.7 20.2 %collective-permute-start.7 = (bf16[2,24,6912]{2,1,0:T(8,128)(2,1)S(1)}, bf16[2,24,6912]{2,1,0:T(8,128)(2,1)}, u32[]{:S(2)}, u32[]{:S(2)}) collective-permute-start(bf16[2,24,6912]{2,1,0:T(8,128)(2,1)S(1)} %broadcast_select_fusion.4), channel_id=1, source_target_pairs={{0,4},{1,5},{2,6},{3,7},{4,0},{5,1},{6,2},{7,3},{8,12},{9,13},{10,... | collective-permute-start | bytes 1990664 | tf_op jit(solution)/shard_map/ppermute | solution.py:581
  36.3 18.6 %collective-permute-start.8 = (bf16[2,4,24,1280]{3,2,1,0:T(8,128)(2,1)S(1)}, bf16[2,4,24,1280]{3,2,1,0:T(8,128)(2,1)S(1)}, u32[]{:S(2)}, u32[]{:S(2)}) collective-permute-start(bf16[2,4,24,1280]{3,2,1,0:T(8,128)(2,1)S(1)} %broadcast_select_fusion.5), channel_id=1, source_target_pairs={{0,2},{1,3},{2,0},{3,1},{4,6},{5,7},{6,4},{7,5},{8,10},{9,11},{10,... | collective-permute-start | bytes 1474568 | tf_op jit(solution)/shard_map/ppermute | solution.py:578
  37.8 17.1 %collective-permute-start.9 = (bf16[4,2,24,1024]{3,2,1,0:T(8,128)(2,1)}, bf16[4,2,24,1024]{3,2,1,0:T(8,128)(2,1)}, u32[]{:S(2)}, u32[]{:S(2)}) collective-permute-start(bf16[4,2,24,1024]{3,2,1,0:T(8,128)(2,1)} %broadcast_select_fusion.6), channel_id=1, source_target_pairs={{0,16},{1,17},{2,18},{3,19},{4,20},{5,21},{6,22},{7,23},{8,24},{9,... | collective-permute-start | bytes 1179656 | tf_op jit(solution)/shard_map/ppermute | solution.py:578
  57.3 15.4 %collective-permute-start.11 = (bf16[4,24,3072]{2,1,0:T(8,128)(2,1)}, bf16[4,24,3072]{2,1,0:T(8,128)(2,1)}, u32[]{:S(2)}, u32[]{:S(2)}) collective-permute-start(bf16[4,24,3072]{2,1,0:T(8,128)(2,1)} %slice.143), channel_id=1, source_target_pairs={{0,2},{1,3},{2,0},{3,1},{4,6},{5,7},{6,4},{7,5},{8,10},{9,11},{10,... | collective-permute-start | bytes 1769480 | tf_op jit(solution)/shard_map/ppermute | solution.py:578
  59.7 18.0 %collective-permute-start.10 = (bf16[4,24,3840]{2,1,0:T(8,128)(2,1)S(1)}, bf16[4,24,3840]{2,1,0:T(8,128)(2,1)S(1)}, u32[]{:S(2)}, u32[]{:S(2)}) collective-permute-start(bf16[4,24,3840]{2,1,0:T(8,128)(2,1)S(1)} %slice.142), channel_id=1, source_target_pairs={{0,16},{1,17},{2,18},{3,19},{4,20},{5,21},{6,22},{7,23},{8,24},{9,... | collective-permute-start | bytes 2211848 | tf_op jit(solution)/shard_map/ppermute | solution.py:578
  79.1 36.5 %collective-permute-start.12 = (bf16[2,4,24,3840]{3,2,1,0:T(8,128)(2,1)S(1)}, bf16[2,4,24,3840]{3,2,1,0:T(8,128)(2,1)S(1)}, u32[]{:S(2)}, u32[]{:S(2)}) collective-permute-start(bf16[2,4,24,3840]{3,2,1,0:T(8,128)(2,1)S(1)} %broadcast_select_fusion.2), channel_id=1, source_target_pairs={{0,2},{1,3},{2,0},{3,1},{4,6},{5,7},{6,4},{7,5},{8,10},{9,11},{10,... | collective-permute-start | bytes 4423688 | tf_op jit(solution)/shard_map/ppermute | solution.py:578
  80.7 34.9 %collective-permute-start.13 = (bf16[4,2,24,3072]{3,2,1,0:T(8,128)(2,1)}, bf16[4,2,24,3072]{3,2,1,0:T(8,128)(2,1)}, u32[]{:S(2)}, u32[]{:S(2)}) collective-permute-start(bf16[4,2,24,3072]{3,2,1,0:T(8,128)(2,1)} %broadcast_select_fusion.3), channel_id=1, source_target_pairs={{0,16},{1,17},{2,18},{3,19},{4,20},{5,21},{6,22},{7,23},{8,24},{9,... | collective-permute-start | bytes 3538952 | tf_op jit(solution)/shard_map/ppermute | solution.py:578
  85.9 29.7 %collective-permute-start.18 = (bf16[256,768]{1,0:T(8,128)(2,1)S(1)}, bf16[256,768]{1,0:T(8,128)(2,1)S(1)}, u32[]{:S(2)}, u32[]{:S(2)}) collective-permute-start(bf16[256,768]{1,0:T(8,128)(2,1)S(1)} %get-tuple-element.190), channel_id=1, source_target_pairs={{0,16},{16,0},{1,17},{17,1},{2,18},{18,2},{3,19},{19,3},{4,20},{20... | collective-permute-start | bytes 1179656 | tf_op jit(solution)/shard_map/ppermute | solution.py:669
  87.4 32.9 %collective-permute-start.19 = (bf16[2,4,24,3840]{3,2,1,0:T(8,128)(2,1)S(1)}, bf16[2,4,24,3840]{3,2,1,0:T(8,128)(2,1)S(1)}, u32[]{:S(2)}, u32[]{:S(2)}) collective-permute-start(bf16[2,4,24,3840]{3,2,1,0:T(8,128)(2,1)S(1)} %broadcast_select_fusion.2), channel_id=1, source_target_pairs={{0,1},{1,0},{2,3},{3,2},{4,5},{5,4},{6,7},{7,6},{8,9},{9,8},{10,11... | collective-permute-start | bytes 4423688 | tf_op jit(solution)/shard_map/ppermute | solution.py:578
  115.6 15.0 %collective-permute-start.22 = (bf16[2,4,24,3840]{3,2,1,0:T(8,128)(2,1)S(1)}, bf16[2,4,24,3840]{3,2,1,0:T(8,128)(2,1)}, u32[]{:S(2)}, u32[]{:S(2)}) collective-permute-start(bf16[2,4,24,3840]{3,2,1,0:T(8,128)(2,1)S(1)} %collective-permute-done.12), channel_id=1, source_target_pairs={{0,1},{1,0},{2,3},{3,2},{4,5},{5,4},{6,7},{7,6},{8,9},{9,8},{10,11... | collective-permute-start | bytes 4423688 | tf_op jit(solution)/shard_map/ppermute | solution.py:578
  166.4 28.8 %collective-permute-start.26 = (bf16[1536,768]{1,0:T(8,128)(2,1)}, bf16[1536,768]{1,0:T(8,128)(2,1)S(1)}, u32[]{:S(2)}, u32[]{:S(2)}) collective-permute-start(bf16[1536,768]{1,0:T(8,128)(2,1)} %get-tuple-element.136), channel_id=1, source_target_pairs={{0,1},{1,0},{2,3},{3,2},{4,5},{5,4},{6,7},{7,6},{8,9},{9,8},{10,11... | collective-permute-start | bytes 7077896 | tf_op jit(solution)/shard_map/ppermute | solution.py:578
  166.6 25.8 %collective-permute-start.25 = (bf16[512,768]{1,0:T(8,128)(2,1)}, bf16[512,768]{1,0:T(8,128)(2,1)}, u32[]{:S(2)}, u32[]{:S(2)}) collective-permute-start(bf16[512,768]{1,0:T(8,128)(2,1)} %get-tuple-element.133), channel_id=1, source_target_pairs={{0,16},{16,0},{1,17},{17,1},{2,18},{18,2},{3,19},{19,3},{4,20},{20... | collective-permute-start | bytes 2359304 | tf_op jit(solution)/shard_map/ppermute | solution.py:669
  192.4 25.0 %collective-permute-start.27 = (bf16[384,3840]{1,0:T(8,128)(2,1)}, bf16[384,3840]{1,0:T(8,128)(2,1)}, u32[]{:S(2)}, u32[]{:S(2)}) collective-permute-start(bf16[384,3840]{1,0:T(8,128)(2,1)} %get-tuple-element.143), channel_id=1, source_target_pairs={{0,1},{1,0},{2,3},{3,2},{4,5},{5,4},{6,7},{7,6},{8,9},{9,8},{10,11... | collective-permute-start | bytes 8847368 | tf_op jit(solution)/shard_map/ppermute | solution.py:578
  196.2 17.1 %collective-permute-start.29 = (bf16[2,4,96,384]{3,2,1,0:T(8,128)(2,1)S(1)}, bf16[2,4,96,384]{3,2,1,0:T(8,128)(2,1)}, u32[]{:S(2)}, u32[]{:S(2)}) collective-permute-start(bf16[2,4,96,384]{3,2,1,0:T(8,128)(2,1)S(1)} %dynamic-slice_bitcast_fusion.3), channel_id=1, source_target_pairs={{0,2},{1,3},{2,0},{3,1},{4,6},{5,7},{6,4},{7,5},{8,10},{9,11},{10,... | collective-permute-start | bytes 1769480 | tf_op jit(solution)/shard_map/ppermute | solution.py:578
  199.3 16.1 %collective-permute-start.28 = (bf16[4,2,96,384]{3,2,0,1:T(8,128)(2,1)}, bf16[4,2,96,384]{3,2,0,1:T(8,128)(2,1)}, u32[]{:S(2)}, u32[]{:S(2)}) collective-permute-start(bf16[4,2,96,384]{3,2,0,1:T(8,128)(2,1)} %dynamic-slice_bitcast_fusion.4), channel_id=1, source_target_pairs={{0,16},{1,17},{2,18},{3,19},{4,20},{5,21},{6,22},{7,23},{8,24},{9,... | collective-permute-start | bytes 1769480 | tf_op jit(solution)/shard_map/ppermute | solution.py:578
  222.4 24.9 %collective-permute-start.31 = (bf16[2,4,24,1920]{3,2,1,0:T(8,128)(2,1)}, bf16[2,4,24,1920]{3,2,1,0:T(8,128)(2,1)}, u32[]{:S(2)}, u32[]{:S(2)}) collective-permute-start(bf16[2,4,24,1920]{3,2,1,0:T(8,128)(2,1)} %dynamic-slice_bitcast_fusion.1), channel_id=1, source_target_pairs={{0,2},{1,3},{2,0},{3,1},{4,6},{5,7},{6,4},{7,5},{8,10},{9,11},{10,... | collective-permute-start | bytes 2211848 | tf_op jit(solution)/shard_map/ppermute | solution.py:578
  229.9 19.5 %collective-permute-start.30 = (bf16[4,2,24,1920]{3,2,0,1:T(8,128)(2,1)S(1)}, bf16[4,2,24,1920]{3,2,0,1:T(8,128)(2,1)S(1)}, u32[]{:S(2)}, u32[]{:S(2)}) collective-permute-start(bf16[4,2,24,1920]{3,2,0,1:T(8,128)(2,1)S(1)} %dynamic-slice_bitcast_fusion.2), channel_id=1, source_target_pairs={{0,16},{1,17},{2,18},{3,19},{4,20},{5,21},{6,22},{7,23},{8,24},{9,... | collective-permute-start | bytes 2211848 | tf_op jit(solution)/shard_map/ppermute | solution.py:578
  231.5 18.1 %collective-permute-start.32 = (bf16[4,96,384]{2,1,0:T(8,128)(2,1)S(1)}, bf16[4,96,384]{2,1,0:T(8,128)(2,1)S(1)}, u32[]{:S(2)}, u32[]{:S(2)}) collective-permute-start(bf16[4,96,384]{2,1,0:T(8,128)(2,1)S(1)} %dynamic-slice_bitcast_fusion.12), channel_id=1, source_target_pairs={{0,2},{1,3},{2,0},{3,1},{4,6},{5,7},{6,4},{7,5},{8,10},{9,11},{10,... | collective-permute-start | bytes 884744 | tf_op jit(solution)/shard_map/ppermute | solution.py:578
  233.4 20.7 %collective-permute-start.33 = (bf16[4,96,384]{2,1,0:T(8,128)(2,1)S(1)}, bf16[4,96,384]{2,1,0:T(8,128)(2,1)S(1)}, u32[]{:S(2)}, u32[]{:S(2)}) collective-permute-start(bf16[4,96,384]{2,1,0:T(8,128)(2,1)S(1)} %dynamic-slice_bitcast_fusion.11), channel_id=1, source_target_pairs={{0,16},{1,17},{2,18},{3,19},{4,20},{5,21},{6,22},{7,23},{8,24},{9,... | collective-permute-start | bytes 884744 | tf_op jit(solution)/shard_map/ppermute | solution.py:578
  254.4 15.7 %collective-permute-start.39 = (bf16[2,96,768]{2,1,0:T(8,128)(2,1)S(1)}, bf16[2,96,768]{2,1,0:T(8,128)(2,1)}, u32[]{:S(2)}, u32[]{:S(2)}) collective-permute-start(bf16[2,96,768]{2,1,0:T(8,128)(2,1)S(1)} %dynamic-slice_bitcast_fusion.10), channel_id=1, source_target_pairs={{0,4},{1,5},{2,6},{3,7},{4,0},{5,1},{6,2},{7,3},{8,12},{9,13},{10,... | collective-permute-start | bytes 884744 | tf_op jit(solution)/shard_map/ppermute | solution.py:581
  256.4 16.7 %collective-permute-start.34 = (bf16[4,24,1920]{2,1,0:T(8,128)(2,1)S(1)}, bf16[4,24,1920]{2,1,0:T(8,128)(2,1)}, u32[]{:S(2)}, u32[]{:S(2)}) collective-permute-start(bf16[4,24,1920]{2,1,0:T(8,128)(2,1)S(1)} %dynamic-slice_bitcast_fusion.9), channel_id=1, source_target_pairs={{0,2},{1,3},{2,0},{3,1},{4,6},{5,7},{6,4},{7,5},{8,10},{9,11},{10,... | collective-permute-start | bytes 1105928 | tf_op jit(solution)/shard_map/ppermute | solution.py:578
  258.0 15.1 %collective-permute-start.35 = (bf16[4,24,1920]{2,1,0:T(8,128)(2,1)S(1)}, bf16[4,24,1920]{2,1,0:T(8,128)(2,1)}, u32[]{:S(2)}, u32[]{:S(2)}) collective-permute-start(bf16[4,24,1920]{2,1,0:T(8,128)(2,1)S(1)} %dynamic-slice_bitcast_fusion.8), channel_id=1, source_target_pairs={{0,16},{1,17},{2,18},{3,19},{4,20},{5,21},{6,22},{7,23},{8,24},{9,... | collective-permute-start | bytes 1105928 | tf_op jit(solution)/shard_map/ppermute | solution.py:578
  271.2 24.5 %collective-permute-start.40 = (bf16[96,768]{1,0:T(8,128)(2,1)S(1)}, bf16[96,768]{1,0:T(8,128)(2,1)S(1)}, u32[]{:S(2)}, u32[]{:S(2)}) collective-permute-start(bf16[96,768]{1,0:T(8,128)(2,1)S(1)} %fusion.26), channel_id=1, source_target_pairs={{0,8},{1,9},{2,10},{3,11},{4,12},{5,13},{6,14},{7,15},{8,0},{9,1},... | collective-permute-start | bytes 442376 | tf_op jit(solution)/shard_map/ppermute | solution.py:581
  277.5 15.2 %collective-permute-start.47 = (bf16[2,24,3840]{2,1,0:T(8,128)(2,1)S(1)}, bf16[2,24,3840]{2,1,0:T(8,128)(2,1)S(1)}, u32[]{:S(2)}, u32[]{:S(2)}) collective-permute-start(bf16[2,24,3840]{2,1,0:T(8,128)(2,1)S(1)} %dynamic-slice_bitcast_fusion.7), channel_id=1, source_target_pairs={{0,4},{1,5},{2,6},{3,7},{4,0},{5,1},{6,2},{7,3},{8,12},{9,13},{10,... | collective-permute-start | bytes 1105928 | tf_op jit(solution)/shard_map/ppermute | solution.py:581
  277.8 17.6 %collective-permute-start.38 = (bf16[2,4,24,1152]{3,2,1,0:T(8,128)(2,1)S(1)}, bf16[2,4,24,1152]{3,2,1,0:T(8,128)(2,1)S(1)}, u32[]{:S(2)}, u32[]{:S(2)}) collective-permute-start(bf16[2,4,24,1152]{3,2,1,0:T(8,128)(2,1)S(1)} %fusion.13), channel_id=1, source_target_pairs={{0,2},{1,3},{2,0},{3,1},{4,6},{5,7},{6,4},{7,5},{8,10},{9,11},{10,... | collective-permute-start | bytes 1327112 | tf_op jit(solution)/shard_map/ppermute | solution.py:578
  278.9 16.7 %collective-permute-start.37 = (bf16[4,2,24,1152]{3,2,0,1:T(8,128)(2,1)S(1)}, bf16[4,2,24,1152]{3,2,0,1:T(8,128)(2,1)S(1)}, u32[]{:S(2)}, u32[]{:S(2)}) collective-permute-start(bf16[4,2,24,1152]{3,2,0,1:T(8,128)(2,1)S(1)} %fusion.17), channel_id=1, source_target_pairs={{0,16},{1,17},{2,18},{3,19},{4,20},{5,21},{6,22},{7,23},{8,24},{9,... | collective-permute-start | bytes 1327112 | tf_op jit(solution)/shard_map/ppermute | solution.py:578
  293.5 25.2 %collective-permute-start.48 = (bf16[24,3840]{1,0:T(8,128)(2,1)}, bf16[24,3840]{1,0:T(8,128)(2,1)}, u32[]{:S(2)}, u32[]{:S(2)}) collective-permute-start(bf16[24,3840]{1,0:T(8,128)(2,1)} %fusion.25), channel_id=1, source_target_pairs={{0,8},{1,9},{2,10},{3,11},{4,12},{5,13},{6,14},{7,15},{8,0},{9,1},... | collective-permute-start | bytes 552968 | tf_op jit(solution)/shard_map/ppermute | solution.py:581
  307.3 21.0 %collective-permute-start.41 = (bf16[512,768]{1,0:T(8,128)(2,1)}, bf16[512,768]{1,0:T(8,128)(2,1)S(1)}, u32[]{:S(2)}, u32[]{:S(2)}) collective-permute-start(bf16[512,768]{1,0:T(8,128)(2,1)} %get-tuple-element.178), channel_id=1, source_target_pairs={{0,16},{16,0},{1,17},{17,1},{2,18},{18,2},{3,19},{19,3},{4,20},{20... | collective-permute-start | bytes 2359304 | tf_op jit(solution)/shard_map/ppermute | solution.py:669
  (57 other events, 577.3 us)

commit v4 on v3

--- a/solution.py
+++ b/solution.py
@@ -206,7 +206,7 @@
             total = jnp.sum(p, axis=0, keepdims=True)
             probs = (p * (1.0 / total)).astype(bf16)
             o_ref[q0 : q0 + qb, hs] = tn(probs, v_ref[k0 : k0 + span, hs]).astype(bf16)
-            lse_ref[0, h : h + 1, q0 : q0 + qb] = top + jnp.log(total)
+            lse_ref[h // 2, h % 2 : h % 2 + 1, q0 : q0 + qb] = top + jnp.log(total)
 
     short = at_ref[SHORT]
 
@@ -228,8 +228,8 @@
     return call(
         functools.partial(attend_kernel, heads=heads, qb=qb), "attend", (groups,),
         [whole(t, d)] + specs,
-        [tok] * 4 + [pl.BlockSpec((1, heads, t), lambda g, s: (g, 0, 0))],
-        [sds((t, d), bf16)] * 4 + [sds((groups, heads, t), f32)], [pltpu.VMEM((d, c), bf16)],
+        [tok] * 4 + [pl.BlockSpec((heads // 2, 2, t), lambda g, s: (g, 0, 0))],
+        [sds((t, d), bf16)] * 4 + [sds((groups * heads // 2, 2, t), f32)], [pltpu.VMEM((d, c), bf16)],
         cost(6 * t * d * d + 16 * t * t * d, 20 * t * d, t * t * d // HD),
         at, (n, *args),
     )
@@ -289,7 +289,7 @@
         + [pl.BlockSpec(memory_space=pl.ANY)] * len(before),
         [tok] * 3, [sds((t, d), bf16)] * 3, [],
         cost(40 * t * t * d // parts, 16 * t * d // parts, t * t * d // HD // parts),
-        at, (q, k, v, o, do, lse.reshape(-1, heads, t), *before),
+        at, (q, k, v, o, do, lse, *before),
         {7 + i: i for i in range(len(before))},
     )
 
@@ -336,13 +336,16 @@
     return jnp.where(u >= 0, 1.0 - tail, tail), e * f32(0.3989422804014327)
 
 
-def ffn_kernel(at_ref, n_ref, here_ref, there_ref, there_2_ref, mid_ref, *refs):
-    ub_ref, row_ref, own_ref, send_ref, du_ref, keep_ref, give_ref, gub_ref, small_ref, dy_ref, acc, act = refs[8:]
+def ffn_kernel(at_ref, n_ref, here_ref, there_ref, there_2_ref, mid_any, *refs):
+    ub_ref, row_ref, own_ref, send_ref, du_ref, keep_ref, give_ref, gub_ref, small_ref, dy_ref = refs[8:18]
+    acc, act, mid_ref, mid_sem = refs[18:]
     j = pl.program_id(0)
+    late = pltpu.make_async_copy(mid_any, mid_ref, mid_sem)
 
     @pl.when(j == 0)
     def _():
-        acc[...] = mid_ref[...] + row_ref[5:6, :]
+        late.start()
+        acc[...] = jnp.zeros_like(acc)
         there = jnp.concatenate([there_ref[...].astype(f32), there_2_ref[...].astype(f32)], axis=0)
         halves = choose(at_ref[SEQ], here_ref[0].astype(f32), there)
         half = there.shape[0]
@@ -390,7 +393,9 @@
     @pl.when(j == pl.num_programs(0) - 1)
     def _():
         half = t // 2
-        own, theirs = choose(at_ref[SEQ], acc[:half, :], acc[half:, :])
+        late.wait()
+        result = acc[...] + mid_ref[...] + row_ref[5:6, :]
+        own, theirs = choose(at_ref[SEQ], result[:half, :], result[half:, :])
         own_ref[...] = own.astype(bf16)
         send_ref[...] = theirs.astype(bf16)
         small_ref[...] = jnp.sum(dy_ref[...].astype(f32), axis=0, keepdims=True)
@@ -405,7 +410,7 @@
     return call(
         ffn_kernel, "ffn", (4,),
         [whole(t, d), pl.BlockSpec((1, t // 2, d), lambda j, s: (s[SEQ], 0, 0)), whole(t // 4, d), whole(t // 4, d)]
-        + [whole(t, d)]
+        + [pl.BlockSpec(memory_space=pl.ANY)]
         + [pl.BlockSpec((high, fb), lambda j, s: (0, j))] * 4
         + [pl.BlockSpec((low // 2, 4 * d), lambda j, s: (j % 2, 0))] * 4
         + [pl.BlockSpec((1, fb), lambda j, s: (0, j)), whole(*rows.shape)],
@@ -416,19 +421,26 @@
         + [sds((t, ff), bf16)]
         + [sds((ff // 2, d), bf16)] * 2
         + [sds((1, ff), f32), sds((1, d), f32), sds((t, d), bf16)],
-        [pltpu.VMEM((t, d), f32), pltpu.VMEM((t, fb), bf16)],
+        [pltpu.VMEM((t, d), f32), pltpu.VMEM((t, fb), bf16), pltpu.VMEM((t, d), f32), pltpu.SemaphoreType.DMA],
         cost(8 * t * d * ff, 20 * t * d + 8 * d * ff, 2 * t * ff),
         at, (n, both, *other, mid, *up_out, *down, up_bias, rows),
     )
 
 
-def unffn_kernel(at_ref, n_ref, dy_ref, mid_ref, du_ref, o_ref, row_ref, *refs):
-    dmid_ref, do_ref, keep_ref, give_ref, small_ref, acc, turned, turned_2 = refs[8:]
+def unffn_kernel(at_ref, n_ref, dy_any, mid_any, du_ref, o_any, row_ref, *refs):
+    dmid_ref, do_ref, keep_ref, give_ref, small_ref, acc, turned, turned_2 = refs[8:16]
+    dy_ref, mid_ref, o_ref, dy_sem, mid_sem, o_sem = refs[16:]
+    late = [
+        pltpu.make_async_copy(*pair_of)
+        for pair_of in ((dy_any, dy_ref, dy_sem), (mid_any, mid_ref, mid_sem), (o_any, o_ref, o_sem))
+    ]
     j = pl.program_id(0)
     last = pl.num_programs(0) - 1
 
     @pl.when(j == 0)
     def _():
+        for copy in late:
+            copy.start()
         acc[...] = jnp.zeros_like(acc)
         turned[...], turned_2[...] = turn(n_ref[...], at_ref)
 
@@ -442,6 +454,8 @@
 
     @pl.when(j == last)
     def _():
+        for copy in late:
+            copy.wait()
         xhat, s = norm_parts(mid_ref[...])
         e = acc[...]
         small_ref[...] = jnp.concatenate(
@@ -463,14 +477,16 @@
     cols = pl.BlockSpec((d // 2, d), lambda j, s: (0, j))
     return call(
         unffn_kernel, "unffn", (count + 1,),
-        [whole(t, d)] * 3
+        [whole(t, d)] + [pl.BlockSpec(memory_space=pl.ANY)] * 2
         + [pl.BlockSpec((t, d), lambda j, s: (0, jnp.minimum(j, count - 1)))]
-        + [whole(t, d), whole(*rows.shape)]
+        + [pl.BlockSpec(memory_space=pl.ANY), whole(*rows.shape)]
         + [pl.BlockSpec((p.shape[0], d), lambda j, s: (0, jnp.minimum(j, count - 1))) for p in up]
         + last_columns(out, d),
         [whole(t, d)] * 2 + [cols] * 2 + [whole(2, d)],
         [sds((t, d), f32), sds((t, d), bf16)] + [sds((d // 2, ff + d), bf16)] * 2 + [sds((2, d), f32)],
-        [pltpu.VMEM((t, d), f32)] + [pltpu.VMEM((d // 2, t), bf16)] * 2,
+        [pltpu.VMEM((t, d), f32)] + [pltpu.VMEM((d // 2, t), bf16)] * 2
+        + [pltpu.VMEM((t, d), bf16), pltpu.VMEM((t, d), f32), pltpu.VMEM((t, d), bf16)]
+        + [pltpu.SemaphoreType.DMA] * 3,
         cost(4 * t * d * (ff + d), 20 * t * d + 8 * d * ff),
         at, (n, dy, mid, du, o, rows, *up, *out),
     )
@@ -498,9 +514,19 @@
     )
 
 
-def unqkv_kernel(at_ref, x_ref, row_ref, dmid_ref, *refs):
-    dq_ref, dk_ref, dv_ref, own_ref, send_ref, small_ref, acc, wk_ref = refs[16:]
+def unqkv_kernel(at_ref, x_any, row_ref, dmid_any, *refs):
+    dq_ref, dk_ref, dv_ref, own_ref, send_ref, small_ref, acc, wk_ref = refs[16:24]
+    x_ref, dmid_ref, x_sem, dmid_sem = refs[24:]
     i = pl.program_id(0)
+    late = [
+        pltpu.make_async_copy(x_any, x_ref, x_sem), pltpu.make_async_copy(dmid_any, dmid_ref, dmid_sem)
+    ]
+
+    @pl.when(i == 0)
+    def _():
+        for copy in late:
+            copy.start()
+
     weave_keys(refs[4:12], at_ref, wk_ref)
     w = [weave_a(refs[0:4], at_ref), wk_ref[...], weave_b(refs[12:16], at_ref)]
     e = nt(
@@ -518,6 +544,8 @@
 
     @pl.when(i == pl.num_programs(0) - 1)
     def _():
+        for copy in late:
+            copy.wait()
         e = acc[...]
         xhat, s = norm_parts(x_ref[...].astype(f32) + row_ref[0:1, :])
         d_base = dmid_ref[...] + norm_back(e, row_ref[1:2, :], xhat, s)
@@ -527,10 +555,9 @@
         send_ref[...] = theirs.astype(bf16)
         small_ref[...] = jnp.concatenate(
             [
-                jnp.sum(d_base, axis=0, keepdims=True),
                 jnp.sum(e * xhat, axis=0, keepdims=True),
                 jnp.sum(e, axis=0, keepdims=True),
-                jnp.zeros((5, e.shape[1]), f32),
+                jnp.sum(d_base, axis=0, keepdims=True),
             ],
             axis=0,
         )
@@ -543,10 +570,12 @@
     tok = pl.BlockSpec((t, cb), lambda i, s: (0, i))
     return call(
         unqkv_kernel, "unqkv", (count,),
-        [whole(t, d), whole(*rows.shape), whole(t, d)] + specs + [tok] * 3,
-        [whole(t // 2, d)] * 2 + [whole(8, d)],
-        [sds((t // 2, d), bf16)] * 2 + [sds((8, d), f32)],
-        [pltpu.VMEM((t, d), f32), pltpu.VMEM((d, cb), bf16)],
+        [pl.BlockSpec(memory_space=pl.ANY), whole(*rows.shape), pl.BlockSpec(memory_space=pl.ANY)]
+        + specs + [tok] * 3,
+        [whole(t // 2, d)] * 2 + [whole(3, d)],
+        [sds((t // 2, d), bf16)] * 2 + [sds((3, d), f32)],
+        [pltpu.VMEM((t, d), f32), pltpu.VMEM((d, cb), bf16), pltpu.VMEM((t, d), bf16), pltpu.VMEM((t, d), f32)]
+        + [pltpu.SemaphoreType.DMA] * 2,
         cost(6 * t * d * d, 30 * t * d), at, (x, rows, dmid, *args, dq, dk, dv),
     )
 
@@ -776,8 +805,7 @@
             d_middle, d_attended, keep_up, give_up, small_two, block_other
         )
         down = add(keep_down, g.swap(give_down, "c")).reshape(*six, -1, d)
-        block_out = pair(block_own, block_other, g.x, 0)
-        d_attended, down, block_out = tie(d_attended, down, block_out)
+        d_attended, down = tie(d_attended, down)
         down_plane = split_plane(g, down[..., : d // 2], down[..., d // 2 :])
     back = attend_back(at, q, k, v, attended, d_attended, lse, 0, 2)
     if g.known:
@@ -813,7 +841,7 @@
         got = plane.send(ready)
     d_other = swap_seq(d_send)
 
-    small = jnp.concatenate([small_one[1:3], small_two, g_down_row, small_one[0:1]], axis=0)
+    small = jnp.concatenate([small_two, g_down_row, small_one], axis=0)
     small = small.reshape(-1, devices, shard).transpose(1, 0, 2).reshape(devices, -1)
     small = jnp.concatenate([small, g_up_row.reshape(devices, -1)], axis=1)
     small = lax.all_to_all(small, BOTH, split_axis=0, concat_axis=0, tiled=True)
@@ -823,7 +851,8 @@
     if g.known:
         sum_up = up_z.send(next(up_z))
         last = jnp.concatenate(plane.send(got), axis=-1)
-        d_other, last = tie(d_other, split_z(g, last))
+        block_out = pair(block_own, block_other, g.x, 0)
+        d_other, last, block_out = tie(d_other, split_z(g, last), block_out)
     else:
         sum_up, sum_down = scatter_plain(keep_up, give_up), scatter_plain(keep_down, give_down)
         last = [scatter_plain(keep_qkv[i], give_qkv[i]) for i in range(3)]
@@ -843,9 +872,9 @@
         sum_up[:, ff:],
         sum_up[:, :ff],
         sum_down,
-        *[small[i * shard : (i + 1) * shard] for i in range(4)],
+        *[small[i * shard : (i + 1) * shard] for i in (3, 4, 0, 1)],
         small[6 * shard :],
-        small[4 * shard : 5 * shard],
+        small[2 * shard : 3 * shard],
     )
 
 

time: 335 us -> 328 us (0.979)
  Pallas kernels: 141 us -> 160 us
  waiting for transfers between devices: 55.7 us -> 44.1 us
  starting transfers between devices: 73.1 us -> 62.2 us
    pallas_call x9, Pallas kernels: 141 us -> 160 us  [call(): pl.pallas_call(kernel, grid_spec=pltpu.PrefetchScalarGridSpec(num_scalar_...]
    ppermute x32, starting transfers between devices: 32.1 us -> 24.6 us  [swap(): return lax.ppermute(v, BOTH, self.table(move))]
    ppermute x5, waiting for transfers between devices: 10.5 us -> 3.28 us  [swap_seq(): return lax.ppermute(v, 'seq', [(0, 1), (1, 0)])]
    ppermute x32, waiting for transfers between devices: 19.7 us -> 15.4 us  [swap(): return lax.ppermute(v, BOTH, self.table(move))]
  transfers between devices with their start and end apart: 52 -> 52, of which waited for: 16 -> 13; matrix products, arithmetic and copies ran while one was open for 13% -> 12% of each run, Pallas kernels for 32% -> 39%
where the time goes in v4:
time: 328 us; the launch traced here: 323 us
  Pallas kernels  160 us (49%)
  starting transfers between devices  62.2 us (19%)
  waiting for transfers between devices  44.1 us (13%)
  other arithmetic  28.4 us (9%)
  local copies, waits for them, and re-layouts  24.4 us (7%)
    pallas_call x9, Pallas kernels, call(): pl.pallas_call(kernel, grid_spec=pltpu.PrefetchScalarGridSpec(num_scalar_...  160 us
    ppermute x32, starting transfers between devices, swap(): return lax.ppermute(v, BOTH, self.table(move))  24.6 us
    ppermute x32, waiting for transfers between devices, swap(): return lax.ppermute(v, BOTH, self.table(move))  15.4 us
    all_to_all x1, waiting for transfers between devices, look_up(): found = lax.all_to_all(found, BOTH, split_axis=0, concat_axis=0, tiled=True)  11.7 us
    convert_element_type x15, other arithmetic, add(): return (a.astype(f32) + b.astype(f32)).astype(bf16)  11.7 us
    ppermute x6, starting transfers between devices, shift(): lax.ppermute(v, BOTH, self.table(lambda x, z, y, c: (x, (z + by) % 4, y,...  11.4 us
    select_n x8, other arithmetic, pair(): return jnp.where(here, spread(own, axis, 2), spread(other, axis, 2))  11.3 us
    ppermute x6, starting transfers between devices, cross(): lax.ppermute(v, BOTH, self.table(lambda x, z, y, c: (x, z ^ bit, y, c)))  9.53 us
  transfers between devices with their start and end apart: 52, of which 13 were waited for; matrix products, arithmetic and copies ran while one was open for 12% of the time, Pallas kernels for 39%

profile of v4, /device:TPU:0, one launch (start us, length us, event | category | flops | bytes accessed | tf_op | source)
XLA Modules:
  0.0 322.8 jit_solution(16766833582103120585)
XLA Ops:
  0.8 5.1 %collective-permute-start = (bf16[24,2304]{1,0:T(8,128)(2,1)}, bf16[24,2304]{1,0:T(8,128)(2,1)S(1)}, u32[]{:S(2)}, u32[]{:S(2)}) collective-permute-start(bf16[24,2304]{1,0:T(8,128)(2,1)} %param.19), channel_id=1, source_target_pairs={{0,12},{1,13},{2,14},{3,15},{4,0},{5,1},{6,2},{7,3},{8,4},{9,5},{1... | collective-permute-start | bytes 331784 | tf_op jit(solution)/shard_map/ppermute | solution.py:613
  10.5 4.1 %all-to-all-start = ((bf16[32,1,220]{2,1,0:T(2,128)(2,1)}), bf16[32,1,220]{2,1,0:T(2,128)(2,1)S(1)}, u32[]{:S(2)}, u32[]{:S(2)}) async-start(bf16[32,1,220]{2,1,0:T(2,128)(2,1)} %broadcast_in_dim.54), calls=%async_computation | async-start | bytes 65536 | tf_op jit(solution)/shard_map/all_to_all | solution.py:722
  14.7 2.7 collective-permute-start.6
  20.8 9.0 %all-to-all-done = bf16[32,1,220]{2,1,0:T(2,128)(2,1)S(1)} async-done(((bf16[32,1,220]{2,1,0:T(2,128)(2,1)}), bf16[32,1,220]{2,1,0:T(2,128)(2,1)S(1)}, u32[]{:S(2)}, u32[]{:S(2)}) %all-to-all-start) | async-done | bytes 14112 | tf_op jit(solution)/shard_map/all_to_all | solution.py:722
  40.4 2.5 all-to-all-start.1
  43.1 11.7 %all-to-all-done.1 = bf16[32,1,24]{2,1,0:T(2,128)(2,1)S(1)} async-done(((bf16[32,1,24]{2,1,0:T(2,128)(2,1)}), bf16[32,1,24]{2,1,0:T(2,128)(2,1)S(1)}, u32[]{:S(2)}, u32[]{:S(2)}) %all-to-all-start.1) | async-done | bytes 1568 | tf_op jit(solution)/shard_map/all_to_all | solution.py:732
  61.2 5.2 %norm_one.1 = (bf16[1024,768]{1,0:T(8,128)(2,1)}, bf16[1024,768]{1,0:T(8,128)(2,1)}) custom-call(s32[5]{0:T(128)} %stack.45.at_ref, bf16[2,512,768]{2,1,0:T(8,128)(2,1)} %own_ref.1, bf16[512,768]{1,0:T(8,128)(2,1)} %copy-done.17, f32[8,768]{1,0:T(8,128)} %pad_convert_fusion.row_ref.refs_9_), custom_call_target="tpu_custom_call" | custom-call | flops 157286 | bytes 62914 | tf_op jit(solution)/shard_map/norm_one/pallas_call | solution.py:112
  66.4 6.3 %collective-permute-done.11 = bf16[4,24,3072]{2,1,0:T(8,128)(2,1)} collective-permute-done((bf16[4,24,3072]{2,1,0:T(8,128)(2,1)}, bf16[4,24,3072]{2,1,0:T(8,128)(2,1)}, u32[]{:S(2)}, u32[]{:S(2)}) %collective-permute-start.11) | collective-permute-done | bytes 589856 | tf_op jit(solution)/shard_map/ppermute | solution.py:607
  72.7 2.4 broadcast_select_fusion.3
  75.1 2.6 collective-permute-done.10
  81.7 2.0 collective-permute-done.16
  83.9 1.9 dynamic-slice_bitcast_fusion.5
  88.2 29.6 %attend.1 = (bf16[1024,768]{1,0:T(8,128)(2,1)}, bf16[1024,768]{1,0:T(8,128)(2,1)}, bf16[1024,768]{1,0:T(8,128)(2,1)}, bf16[1024,768]{1,0:T(8,128)(2,1)}, f32[6,2,1024]{2,1,0:T(2,128)}) custom-call(s32[5]{0:T(128)} %stack.45.at_ref, bf16[1024,768]{1,0:T(8,128)(2,1)} %get-tuple-element.157.n_ref, bf16[192,1280]{1,0:T(8,128)(2,1)} %bitcast.185, ...), custom_call_target="tpu_custom_call" | custom-call | flops 330175616 | bytes 314572 | tf_op jit(solution)/shard_map/attend/pallas_call | solution.py:112
  124.7 6.8 %mix.1 = (f32[1024,768]{1,0:T(8,128)}, bf16[1024,768]{1,0:T(8,128)(2,1)}) custom-call(s32[5]{0:T(128)} %stack.45.at_ref, bf16[1024,768]{1,0:T(8,128)(2,1)} %get-tuple-element.107.x_ref.x_any, bf16[1024,768]{1,0:T(8,128)(2,1)} %get-tuple-element.120.o_ref.o_any, bf16[192,3840]{1,0:T(8,128)(2,1)} %bitcast.169, bf16[192,3840]{1,0:T(8,128)(2,1)} %bitcast.175, ...), custom_call_target="tpu_custom_call" | custom-call | flops 24159192 | bytes 188743 | tf_op jit(solution)/shard_map/mix/pallas_call | solution.py:112
  131.5 35.0 %ffn.1 = (bf16[512,768]{1,0:T(8,128)(2,1)}, bf16[512,768]{1,0:T(8,128)(2,1)}, bf16[1024,3072]{1,0:T(8,128)(2,1)}, bf16[1536,768]{1,0:T(8,128)(2,1)}, bf16[1536,7...) custom-call(s32[5]{0:T(128)} %stack.45.at_ref, ...), custom_call_target="tpu_custom_call" | custom-call | flops 386547072 | bytes 692060 | tf_op jit(solution)/shard_map/ffn/pallas_call | solution.py:112
  166.7 2.2 collective-permute-start.25
  168.9 22.6 %unffn.1 = (f32[1024,768]{1,0:T(8,128)}, bf16[1024,768]{1,0:T(8,128)(2,1)}, bf16[384,3840]{1,0:T(8,128)(2,1)}, bf16[384,3840]{1,0:T(8,128)(2,1)}, f32[2,768]{1,0:T(2,128)}) custom-call(s32[5]{0:T(128)} %stack.45.at_ref, bf16[1024,768]{1,0:T(8,128)(2,1)} %get-tuple-element.122.n_ref, bf16[1024,768]{1,0:T(8,128)(2,1)} %get-tuple-element.126.dy_any, ...), custom_call_target="tpu_custom_call" | custom-call | flops 241591904 | bytes 692060 | tf_op jit(solution)/shard_map/unffn/pallas_call | solution.py:112
  191.6 2.3 add_convert_fusion.1
  196.2 19.6 %attend_back_0.1 = (bf16[1024,768]{1,0:T(8,128)(2,1)}, bf16[1024,768]{1,0:T(8,128)(2,1)}, bf16[1024,768]{1,0:T(8,128)(2,1)}) custom-call(s32[5]{0:T(128)} %stack.45.at_ref, bf16[1024,768]{1,0:T(8,128)(2,1)} %get-tuple-element.142.q_ref, bf16[1024,768]{1,0:T(8,128)(2,1)} %get-tuple-element.143.k_ref, bf16[1024,768]{1,0:T(8,128)(2,1)} %get-tuple-element.144.v_ref, ...), custom_call_target="tpu_custom_call" | custom-call | flops 322122560 | bytes 125829 | tf_op jit(solution)/shard_map/attend_back_0/pallas_call | solution.py:112
  215.8 2.2 fusion.2
  217.9 2.0 fusion.3
  220.0 2.6 add_convert_fusion
  228.3 2.0 collective-permute-start.30
  231.8 19.7 %attend_back_1.1 = (bf16[1024,768]{1,0:T(8,128)(2,1)}, bf16[1024,768]{1,0:T(8,128)(2,1)}, bf16[1024,768]{1,0:T(8,128)(2,1)}) custom-call(s32[5]{0:T(128)} %stack.45.at_ref, bf16[1024,768]{1,0:T(8,128)(2,1)} %get-tuple-element.142.q_ref, bf16[1024,768]{1,0:T(8,128)(2,1)} %get-tuple-element.143.k_ref, ...), custom_call_target="tpu_custom_call", output_to_operand_aliasing={{0}: (7, {}), {1}: (8, {}), {2}: (9, {})} | custom-call | flops 322122560 | bytes 125829 | tf_op jit(solution)/shard_map/attend_back_1/pallas_call | solution.py:112
  256.8 9.3 %grad_qkv.1 = (bf16[3,384,768]{2,1,0:T(8,128)(2,1)}, bf16[3,384,768]{2,1,0:T(8,128)(2,1)}) custom-call(s32[5]{0:T(128)} %stack.45.at_ref, bf16[1024,768]{1,0:T(8,128)(2,1)} %get-tuple-element.157.n_ref, bf16[1024,768]{1,0:T(8,128)(2,1)} %get-tuple-element.158.dq_ref.refs_16_, bf16[1024,768]{1,0:T(8,128)(2,1)} %get-tuple-element.159.dk_ref.refs_17_, ...), custom_call_target="tpu_custom_call" | custom-call | flops 72477576 | bytes 314572 | tf_op jit(solution)/shard_map/grad_qkv/pallas_call | solution.py:112
  266.2 2.5 broadcast_select_fusion.1
  274.2 12.1 %unqkv.1 = (bf16[512,768]{1,0:T(8,128)(2,1)}, bf16[512,768]{1,0:T(8,128)(2,1)}, f32[3,768]{1,0:T(4,128)}) custom-call(s32[5]{0:T(128)} %stack.45.at_ref, bf16[1024,768]{1,0:T(8,128)(2,1)} %get-tuple-element.107.x_ref.x_any, f32[8,768]{1,0:T(8,128)} %pad_convert_fusion.row_ref.refs_9_, f32[1024,768]{1,0:T(8,128)} %get-tuple-element.168.dmid_any, ...), custom_call_target="tpu_custom_call" | custom-call | flops 72477576 | bytes 471859 | tf_op jit(solution)/shard_map/unqkv/pallas_call | solution.py:112
  287.1 2.8 collective-permute-start.48
  291.8 3.7 %all-to-all-start.2 = ((f32[32,1,240]{2,1,0:T(1,128)}), f32[32,1,240]{2,1,0:T(1,128)S(1)}, u32[]{:S(2)}, u32[]{:S(2)}) async-start(f32[32,1,240]{2,1,0:T(1,128)} %all_to_all.27), calls=%async_computation.2 | async-start | bytes 65536 | tf_op jit(solution)/shard_map/all_to_all | solution.py:847
  307.8 2.4 collective-permute-start.45
  314.3 2.9 collective-permute-done.45
  317.9 3.3 %collective-permute-done.41 = bf16[512,768]{1,0:T(8,128)(2,1)S(1)} collective-permute-done((bf16[512,768]{1,0:T(8,128)(2,1)}, bf16[512,768]{1,0:T(8,128)(2,1)S(1)}, u32[]{:S(2)}, u32[]{:S(2)}) %collective-permute-start.41) | collective-permute-done | bytes 786464 | tf_op jit(solution)/shard_map/ppermute | solution.py:698
  (280 shorter events, 79.0 us)
Async XLA Ops:
  0.8 16.7 %collective-permute-start = (bf16[24,2304]{1,0:T(8,128)(2,1)}, bf16[24,2304]{1,0:T(8,128)(2,1)S(1)}, u32[]{:S(2)}, u32[]{:S(2)}) collective-permute-start(bf16[24,2304]{1,0:T(8,128)(2,1)} %param.19), channel_id=1, source_target_pairs={{0,12},{1,13},{2,14},{3,15},{4,0},{5,1},{6,2},{7,3},{8,4},{9,5},{1... | collective-permute-start | bytes 331784 | tf_op jit(solution)/shard_map/ppermute | solution.py:613
  8.1 25.3 %collective-permute-start.5 = (bf16[512,768]{1,0:T(8,128)(2,1)S(1)}, bf16[512,768]{1,0:T(8,128)(2,1)S(1)}, u32[]{:S(2)}, u32[]{:S(2)}) collective-permute-start(bf16[512,768]{1,0:T(8,128)(2,1)S(1)} %dynamic-slice_bitcast_fusion), channel_id=1, source_target_pairs={{0,16},{16,0},{1,17},{17,1},{2,18},{18,2},{3,19},{19,3},{4,20},{20... | collective-permute-start | bytes 2359304 | tf_op jit(solution)/shard_map/ppermute | solution.py:698
  10.5 19.4 %all-to-all-start = ((bf16[32,1,220]{2,1,0:T(2,128)(2,1)}), bf16[32,1,220]{2,1,0:T(2,128)(2,1)S(1)}, u32[]{:S(2)}, u32[]{:S(2)}) async-start(bf16[32,1,220]{2,1,0:T(2,128)(2,1)} %broadcast_in_dim.54), calls=%async_computation | async-start | bytes 65536 | tf_op jit(solution)/shard_map/all_to_all | solution.py:722
  14.7 18.7 %collective-permute-start.6 = (bf16[24,6912]{1,0:T(8,128)(2,1)S(1)}, bf16[24,6912]{1,0:T(8,128)(2,1)}, u32[]{:S(2)}, u32[]{:S(2)}) collective-permute-start(bf16[24,6912]{1,0:T(8,128)(2,1)S(1)} %constant_dynamic-update-slice_fusion), channel_id=1, source_target_pairs={{0,8},{1,9},{2,10},{3,11},{4,12},{5,13},{6,14},{7,15},{8,0},{9,1},... | collective-permute-start | bytes 995336 | tf_op jit(solution)/shard_map/ppermute | solution.py:610
  34.7 20.2 %collective-permute-start.7 = (bf16[2,24,6912]{2,1,0:T(8,128)(2,1)S(1)}, bf16[2,24,6912]{2,1,0:T(8,128)(2,1)}, u32[]{:S(2)}, u32[]{:S(2)}) collective-permute-start(bf16[2,24,6912]{2,1,0:T(8,128)(2,1)S(1)} %broadcast_select_fusion.4), channel_id=1, source_target_pairs={{0,4},{1,5},{2,6},{3,7},{4,0},{5,1},{6,2},{7,3},{8,12},{9,13},{10,... | collective-permute-start | bytes 1990664 | tf_op jit(solution)/shard_map/ppermute | solution.py:610
  36.3 18.7 %collective-permute-start.8 = (bf16[2,4,24,1280]{3,2,1,0:T(8,128)(2,1)S(1)}, bf16[2,4,24,1280]{3,2,1,0:T(8,128)(2,1)S(1)}, u32[]{:S(2)}, u32[]{:S(2)}) collective-permute-start(bf16[2,4,24,1280]{3,2,1,0:T(8,128)(2,1)S(1)} %broadcast_select_fusion.5), channel_id=1, source_target_pairs={{0,2},{1,3},{2,0},{3,1},{4,6},{5,7},{6,4},{7,5},{8,10},{9,11},{10,... | collective-permute-start | bytes 1474568 | tf_op jit(solution)/shard_map/ppermute | solution.py:607
  37.8 17.1 %collective-permute-start.9 = (bf16[4,2,24,1024]{3,2,1,0:T(8,128)(2,1)}, bf16[4,2,24,1024]{3,2,1,0:T(8,128)(2,1)}, u32[]{:S(2)}, u32[]{:S(2)}) collective-permute-start(bf16[4,2,24,1024]{3,2,1,0:T(8,128)(2,1)} %broadcast_select_fusion.6), channel_id=1, source_target_pairs={{0,16},{1,17},{2,18},{3,19},{4,20},{5,21},{6,22},{7,23},{8,24},{9,... | collective-permute-start | bytes 1179656 | tf_op jit(solution)/shard_map/ppermute | solution.py:607
  40.4 14.4 %all-to-all-start.1 = ((bf16[32,1,24]{2,1,0:T(2,128)(2,1)}), bf16[32,1,24]{2,1,0:T(2,128)(2,1)S(1)}, u32[]{:S(2)}, u32[]{:S(2)}) async-start(bf16[32,1,24]{2,1,0:T(2,128)(2,1)} %copy.111), calls=%async_computation.1 | async-start | bytes 32768 | tf_op jit(solution)/shard_map/all_to_all | solution.py:732
  57.3 15.4 %collective-permute-start.11 = (bf16[4,24,3072]{2,1,0:T(8,128)(2,1)}, bf16[4,24,3072]{2,1,0:T(8,128)(2,1)}, u32[]{:S(2)}, u32[]{:S(2)}) collective-permute-start(bf16[4,24,3072]{2,1,0:T(8,128)(2,1)} %slice.135), channel_id=1, source_target_pairs={{0,2},{1,3},{2,0},{3,1},{4,6},{5,7},{6,4},{7,5},{8,10},{9,11},{10,... | collective-permute-start | bytes 1769480 | tf_op jit(solution)/shard_map/ppermute | solution.py:607
  59.7 18.0 %collective-permute-start.10 = (bf16[4,24,3840]{2,1,0:T(8,128)(2,1)S(1)}, bf16[4,24,3840]{2,1,0:T(8,128)(2,1)S(1)}, u32[]{:S(2)}, u32[]{:S(2)}) collective-permute-start(bf16[4,24,3840]{2,1,0:T(8,128)(2,1)S(1)} %slice.134), channel_id=1, source_target_pairs={{0,16},{1,17},{2,18},{3,19},{4,20},{5,21},{6,22},{7,23},{8,24},{9,... | collective-permute-start | bytes 2211848 | tf_op jit(solution)/shard_map/ppermute | solution.py:607
  79.1 38.8 %collective-permute-start.12 = (bf16[2,4,24,3840]{3,2,1,0:T(8,128)(2,1)S(1)}, bf16[2,4,24,3840]{3,2,1,0:T(8,128)(2,1)S(1)}, u32[]{:S(2)}, u32[]{:S(2)}) collective-permute-start(bf16[2,4,24,3840]{3,2,1,0:T(8,128)(2,1)S(1)} %broadcast_select_fusion.2), channel_id=1, source_target_pairs={{0,2},{1,3},{2,0},{3,1},{4,6},{5,7},{6,4},{7,5},{8,10},{9,11},{10,... | collective-permute-start | bytes 4423688 | tf_op jit(solution)/shard_map/ppermute | solution.py:607
  80.6 37.2 %collective-permute-start.13 = (bf16[4,2,24,3072]{3,2,1,0:T(8,128)(2,1)}, bf16[4,2,24,3072]{3,2,1,0:T(8,128)(2,1)}, u32[]{:S(2)}, u32[]{:S(2)}) collective-permute-start(bf16[4,2,24,3072]{3,2,1,0:T(8,128)(2,1)} %broadcast_select_fusion.3), channel_id=1, source_target_pairs={{0,16},{1,17},{2,18},{3,19},{4,20},{5,21},{6,22},{7,23},{8,24},{9,... | collective-permute-start | bytes 3538952 | tf_op jit(solution)/shard_map/ppermute | solution.py:607
  85.8 32.0 %collective-permute-start.18 = (bf16[256,768]{1,0:T(8,128)(2,1)S(1)}, bf16[256,768]{1,0:T(8,128)(2,1)S(1)}, u32[]{:S(2)}, u32[]{:S(2)}) collective-permute-start(bf16[256,768]{1,0:T(8,128)(2,1)S(1)} %get-tuple-element.190), channel_id=1, source_target_pairs={{0,16},{16,0},{1,17},{17,1},{2,18},{18,2},{3,19},{19,3},{4,20},{20... | collective-permute-start | bytes 1179656 | tf_op jit(solution)/shard_map/ppermute | solution.py:698
  87.3 32.9 %collective-permute-start.19 = (bf16[2,4,24,3840]{3,2,1,0:T(8,128)(2,1)S(1)}, bf16[2,4,24,3840]{3,2,1,0:T(8,128)(2,1)S(1)}, u32[]{:S(2)}, u32[]{:S(2)}) collective-permute-start(bf16[2,4,24,3840]{3,2,1,0:T(8,128)(2,1)S(1)} %broadcast_select_fusion.2), channel_id=1, source_target_pairs={{0,1},{1,0},{2,3},{3,2},{4,5},{5,4},{6,7},{7,6},{8,9},{9,8},{10,11... | collective-permute-start | bytes 4423688 | tf_op jit(solution)/shard_map/ppermute | solution.py:607
  117.9 13.6 %collective-permute-start.22 = (bf16[2,4,24,3840]{3,2,1,0:T(8,128)(2,1)S(1)}, bf16[2,4,24,3840]{3,2,1,0:T(8,128)(2,1)}, u32[]{:S(2)}, u32[]{:S(2)}) collective-permute-start(bf16[2,4,24,3840]{3,2,1,0:T(8,128)(2,1)S(1)} %collective-permute-done.12), channel_id=1, source_target_pairs={{0,1},{1,0},{2,3},{3,2},{4,5},{5,4},{6,7},{7,6},{8,9},{9,8},{10,11... | collective-permute-start | bytes 4423688 | tf_op jit(solution)/shard_map/ppermute | solution.py:607
  166.5 25.1 %collective-permute-start.26 = (bf16[1536,768]{1,0:T(8,128)(2,1)}, bf16[1536,768]{1,0:T(8,128)(2,1)}, u32[]{:S(2)}, u32[]{:S(2)}) collective-permute-start(bf16[1536,768]{1,0:T(8,128)(2,1)} %get-tuple-element.137), channel_id=1, source_target_pairs={{0,1},{1,0},{2,3},{3,2},{4,5},{5,4},{6,7},{7,6},{8,9},{9,8},{10,11... | collective-permute-start | bytes 7077896 | tf_op jit(solution)/shard_map/ppermute | solution.py:607
  166.7 24.8 %collective-permute-start.25 = (bf16[512,768]{1,0:T(8,128)(2,1)}, bf16[512,768]{1,0:T(8,128)(2,1)}, u32[]{:S(2)}, u32[]{:S(2)}) collective-permute-start(bf16[512,768]{1,0:T(8,128)(2,1)} %get-tuple-element.133), channel_id=1, source_target_pairs={{0,16},{16,0},{1,17},{17,1},{2,18},{18,2},{3,19},{19,3},{4,20},{20... | collective-permute-start | bytes 2359304 | tf_op jit(solution)/shard_map/ppermute | solution.py:698
  191.5 28.5 %collective-permute-start.27 = (bf16[384,3840]{1,0:T(8,128)(2,1)}, bf16[384,3840]{1,0:T(8,128)(2,1)}, u32[]{:S(2)}, u32[]{:S(2)}) collective-permute-start(bf16[384,3840]{1,0:T(8,128)(2,1)} %get-tuple-element.140), channel_id=1, source_target_pairs={{0,1},{1,0},{2,3},{3,2},{4,5},{5,4},{6,7},{7,6},{8,9},{9,8},{10,11... | collective-permute-start | bytes 8847368 | tf_op jit(solution)/shard_map/ppermute | solution.py:607
  194.3 21.5 %collective-permute-start.29 = (bf16[2,4,96,384]{3,2,1,0:T(8,128)(2,1)S(1)}, bf16[2,4,96,384]{3,2,1,0:T(8,128)(2,1)}, u32[]{:S(2)}, u32[]{:S(2)}) collective-permute-start(bf16[2,4,96,384]{3,2,1,0:T(8,128)(2,1)S(1)} %dynamic-slice_bitcast_fusion.3), channel_id=1, source_target_pairs={{0,2},{1,3},{2,0},{3,1},{4,6},{5,7},{6,4},{7,5},{8,10},{9,11},{10,... | collective-permute-start | bytes 1769480 | tf_op jit(solution)/shard_map/ppermute | solution.py:607
  196.1 21.9 %collective-permute-start.28 = (bf16[4,2,96,384]{3,2,0,1:T(8,128)(2,1)}, bf16[4,2,96,384]{3,2,0,1:T(8,128)(2,1)}, u32[]{:S(2)}, u32[]{:S(2)}) collective-permute-start(bf16[4,2,96,384]{3,2,0,1:T(8,128)(2,1)} %dynamic-slice_bitcast_fusion.4), channel_id=1, source_target_pairs={{0,16},{1,17},{2,18},{3,19},{4,20},{5,21},{6,22},{7,23},{8,24},{9,... | collective-permute-start | bytes 1769480 | tf_op jit(solution)/shard_map/ppermute | solution.py:607
  225.0 26.5 %collective-permute-start.31 = (bf16[2,4,24,1920]{3,2,1,0:T(8,128)(2,1)}, bf16[2,4,24,1920]{3,2,1,0:T(8,128)(2,1)}, u32[]{:S(2)}, u32[]{:S(2)}) collective-permute-start(bf16[2,4,24,1920]{3,2,1,0:T(8,128)(2,1)} %dynamic-slice_bitcast_fusion.1), channel_id=1, source_target_pairs={{0,2},{1,3},{2,0},{3,1},{4,6},{5,7},{6,4},{7,5},{8,10},{9,11},{10,... | collective-permute-start | bytes 2211848 | tf_op jit(solution)/shard_map/ppermute | solution.py:607
  228.3 24.5 %collective-permute-start.30 = (bf16[4,2,24,1920]{3,2,0,1:T(8,128)(2,1)S(1)}, bf16[4,2,24,1920]{3,2,0,1:T(8,128)(2,1)S(1)}, u32[]{:S(2)}, u32[]{:S(2)}) collective-permute-start(bf16[4,2,24,1920]{3,2,0,1:T(8,128)(2,1)S(1)} %dynamic-slice_bitcast_fusion.2), channel_id=1, source_target_pairs={{0,16},{1,17},{2,18},{3,19},{4,20},{5,21},{6,22},{7,23},{8,24},{9,... | collective-permute-start | bytes 2211848 | tf_op jit(solution)/shard_map/ppermute | solution.py:607
  230.3 22.7 %collective-permute-start.32 = (bf16[4,96,384]{2,1,0:T(8,128)(2,1)S(1)}, bf16[4,96,384]{2,1,0:T(8,128)(2,1)S(1)}, u32[]{:S(2)}, u32[]{:S(2)}) collective-permute-start(bf16[4,96,384]{2,1,0:T(8,128)(2,1)S(1)} %dynamic-slice_bitcast_fusion.12), channel_id=1, source_target_pairs={{0,2},{1,3},{2,0},{3,1},{4,6},{5,7},{6,4},{7,5},{8,10},{9,11},{10,... | collective-permute-start | bytes 884744 | tf_op jit(solution)/shard_map/ppermute | solution.py:607
  231.0 22.0 %collective-permute-start.33 = (bf16[4,96,384]{2,1,0:T(8,128)(2,1)S(1)}, bf16[4,96,384]{2,1,0:T(8,128)(2,1)S(1)}, u32[]{:S(2)}, u32[]{:S(2)}) collective-permute-start(bf16[4,96,384]{2,1,0:T(8,128)(2,1)S(1)} %dynamic-slice_bitcast_fusion.11), channel_id=1, source_target_pairs={{0,16},{1,17},{2,18},{3,19},{4,20},{5,21},{6,22},{7,23},{8,24},{9,... | collective-permute-start | bytes 884744 | tf_op jit(solution)/shard_map/ppermute | solution.py:607
  253.3 15.4 %collective-permute-start.39 = (bf16[2,96,768]{2,1,0:T(8,128)(2,1)S(1)}, bf16[2,96,768]{2,1,0:T(8,128)(2,1)S(1)}, u32[]{:S(2)}, u32[]{:S(2)}) collective-permute-start(bf16[2,96,768]{2,1,0:T(8,128)(2,1)S(1)} %dynamic-slice_bitcast_fusion.10), channel_id=1, source_target_pairs={{0,4},{1,5},{2,6},{3,7},{4,0},{5,1},{6,2},{7,3},{8,12},{9,13},{10,... | collective-permute-start | bytes 884744 | tf_op jit(solution)/shard_map/ppermute | solution.py:610
  253.9 16.7 %collective-permute-start.34 = (bf16[4,24,1920]{2,1,0:T(8,128)(2,1)S(1)}, bf16[4,24,1920]{2,1,0:T(8,128)(2,1)S(1)}, u32[]{:S(2)}, u32[]{:S(2)}) collective-permute-start(bf16[4,24,1920]{2,1,0:T(8,128)(2,1)S(1)} %dynamic-slice_bitcast_fusion.9), channel_id=1, source_target_pairs={{0,2},{1,3},{2,0},{3,1},{4,6},{5,7},{6,4},{7,5},{8,10},{9,11},{10,... | collective-permute-start | bytes 1105928 | tf_op jit(solution)/shard_map/ppermute | solution.py:607
  255.0 15.6 %collective-permute-start.35 = (bf16[4,24,1920]{2,1,0:T(8,128)(2,1)S(1)}, bf16[4,24,1920]{2,1,0:T(8,128)(2,1)S(1)}, u32[]{:S(2)}, u32[]{:S(2)}) collective-permute-start(bf16[4,24,1920]{2,1,0:T(8,128)(2,1)S(1)} %dynamic-slice_bitcast_fusion.8), channel_id=1, source_target_pairs={{0,16},{1,17},{2,18},{3,19},{4,20},{5,21},{6,22},{7,23},{8,24},{9,... | collective-permute-start | bytes 1105928 | tf_op jit(solution)/shard_map/ppermute | solution.py:607
  268.8 21.4 %collective-permute-start.40 = (bf16[96,768]{1,0:T(8,128)(2,1)S(1)}, bf16[96,768]{1,0:T(8,128)(2,1)S(1)}, u32[]{:S(2)}, u32[]{:S(2)}) collective-permute-start(bf16[96,768]{1,0:T(8,128)(2,1)S(1)} %fusion.26), channel_id=1, source_target_pairs={{0,8},{1,9},{2,10},{3,11},{4,12},{5,13},{6,14},{7,15},{8,0},{9,1},... | collective-permute-start | bytes 442376 | tf_op jit(solution)/shard_map/ppermute | solution.py:610
  272.9 17.0 %collective-permute-start.38 = (bf16[2,4,24,1152]{3,2,1,0:T(8,128)(2,1)S(1)}, bf16[2,4,24,1152]{3,2,1,0:T(8,128)(2,1)S(1)}, u32[]{:S(2)}, u32[]{:S(2)}) collective-permute-start(bf16[2,4,24,1152]{3,2,1,0:T(8,128)(2,1)S(1)} %fusion.13), channel_id=1, source_target_pairs={{0,2},{1,3},{2,0},{3,1},{4,6},{5,7},{6,4},{7,5},{8,10},{9,11},{10,... | collective-permute-start | bytes 1327112 | tf_op jit(solution)/shard_map/ppermute | solution.py:607
  273.9 16.1 %collective-permute-start.37 = (bf16[4,2,24,1152]{3,2,0,1:T(8,128)(2,1)S(1)}, bf16[4,2,24,1152]{3,2,0,1:T(8,128)(2,1)S(1)}, u32[]{:S(2)}, u32[]{:S(2)}) collective-permute-start(bf16[4,2,24,1152]{3,2,0,1:T(8,128)(2,1)S(1)} %fusion.17), channel_id=1, source_target_pairs={{0,16},{1,17},{2,18},{3,19},{4,20},{5,21},{6,22},{7,23},{8,24},{9,... | collective-permute-start | bytes 1327112 | tf_op jit(solution)/shard_map/ppermute | solution.py:607
  287.1 24.5 %collective-permute-start.48 = (bf16[24,3840]{1,0:T(8,128)(2,1)}, bf16[24,3840]{1,0:T(8,128)(2,1)}, u32[]{:S(2)}, u32[]{:S(2)}) collective-permute-start(bf16[24,3840]{1,0:T(8,128)(2,1)} %fusion.25), channel_id=1, source_target_pairs={{0,8},{1,9},{2,10},{3,11},{4,12},{5,13},{6,14},{7,15},{8,0},{9,1},... | collective-permute-start | bytes 552968 | tf_op jit(solution)/shard_map/ppermute | solution.py:610
  300.2 21.0 %collective-permute-start.41 = (bf16[512,768]{1,0:T(8,128)(2,1)}, bf16[512,768]{1,0:T(8,128)(2,1)S(1)}, u32[]{:S(2)}, u32[]{:S(2)}) collective-permute-start(bf16[512,768]{1,0:T(8,128)(2,1)} %get-tuple-element.174), channel_id=1, source_target_pairs={{0,16},{16,0},{1,17},{17,1},{2,18},{18,2},{3,19},{19,3},{4,20},{20... | collective-permute-start | bytes 2359304 | tf_op jit(solution)/shard_map/ppermute | solution.py:698
  (57 other events, 582.4 us)

commit v5 on v4

--- a/solution.py
+++ b/solution.py
@@ -838,7 +838,9 @@
         small_one, d_send, ready, down_got = tie(small_one, d_send, ready, next(down_z))
         sum_down = down_z.send(down_got)
         up_z = halve_z(g, up)
-        got = plane.send(ready)
+        got_a, got_b = plane.send(ready)
+        small_one, got_a = tie(small_one, got_a)
+        got = (got_a, got_b)
     d_other = swap_seq(d_send)
 
     small = jnp.concatenate([small_two, g_down_row, small_one], axis=0)

time: 328 us -> 324 us (0.988)
  Pallas kernels: 160 us -> 137 us
  waiting for transfers between devices: 44.1 us -> 58.1 us
  starting transfers between devices: 62.2 us -> 71.5 us
    pallas_call x9, Pallas kernels: 160 us -> 137 us  [call(): pl.pallas_call(kernel, grid_spec=pltpu.PrefetchScalarGridSpec(num_scalar_...]
    ppermute x32, starting transfers between devices: 24.6 us -> 33.3 us  [swap(): return lax.ppermute(v, BOTH, self.table(move))]
    ppermute x6, waiting for transfers between devices: 1.07 us -> 6.24 us  [cross(): lax.ppermute(v, BOTH, self.table(lambda x, z, y, c: (x, z ^ bit, y, c)))]
    all_to_all x1, waiting for transfers between devices: 0.39 us -> 4.6 us  [local(): small = lax.all_to_all(small, BOTH, split_axis=0, concat_axis=0, tiled=True)]
    ppermute x32, waiting for transfers between devices: 15.4 us -> 19.3 us  [swap(): return lax.ppermute(v, BOTH, self.table(move))]
    ppermute x5, waiting for transfers between devices: 3.28 us -> 7.08 us  [swap_seq(): return lax.ppermute(v, 'seq', [(0, 1), (1, 0)])]
  transfers between devices with their start and end apart: 52 -> 52, of which waited for: 13 -> 15; matrix products, arithmetic and copies ran while one was open for 12% -> 10% of each run, Pallas kernels for 39% -> 32%
where the time goes in v5:
time: 324 us; the launch traced here: 319 us
  Pallas kernels  137 us (42%)
  starting transfers between devices  71.5 us (22%)
  waiting for transfers between devices  58.1 us (18%)
  other arithmetic  26.6 us (8%)
  local copies, waits for them, and re-layouts  21.7 us (7%)
    pallas_call x9, Pallas kernels, call(): pl.pallas_call(kernel, grid_spec=pltpu.PrefetchScalarGridSpec(num_scalar_...  137 us
    ppermute x32, starting transfers between devices, swap(): return lax.ppermute(v, BOTH, self.table(move))  33.3 us
    ppermute x32, waiting for transfers between devices, swap(): return lax.ppermute(v, BOTH, self.table(move))  19.3 us
    ppermute x6, starting transfers between devices, shift(): lax.ppermute(v, BOTH, self.table(lambda x, z, y, c: (x, (z + by) % 4, y,...  11.8 us
    all_to_all x1, waiting for transfers between devices, look_up(): found = lax.all_to_all(found, BOTH, split_axis=0, concat_axis=0, tiled=True)  11.7 us
    convert_element_type x15, other arithmetic, add(): return (a.astype(f32) + b.astype(f32)).astype(bf16)  11.7 us
    select_n x8, other arithmetic, pair(): return jnp.where(here, spread(own, axis, 2), spread(other, axis, 2))  11.3 us
    all_to_all x1, waiting for transfers between devices, local(): lax.all_to_all(shorts, BOTH, split_axis=0, concat_axis=0, tiled=True)  9.04 us
  transfers between devices with their start and end apart: 52, of which 15 were waited for; matrix products, arithmetic and copies ran while one was open for 10% of the time, Pallas kernels for 32%

profile of v5, /device:TPU:0, one launch (start us, length us, event | category | flops | bytes accessed | tf_op | source)
XLA Modules:
  0.0 319.1 jit_solution(8516980340824177937)
XLA Ops:
  0.8 5.1 %collective-permute-start = (bf16[24,2304]{1,0:T(8,128)(2,1)}, bf16[24,2304]{1,0:T(8,128)(2,1)S(1)}, u32[]{:S(2)}, u32[]{:S(2)}) collective-permute-start(bf16[24,2304]{1,0:T(8,128)(2,1)} %param.19), channel_id=1, source_target_pairs={{0,12},{1,13},{2,14},{3,15},{4,0},{5,1},{6,2},{7,3},{8,4},{9,5},{1... | collective-permute-start | bytes 331784 | tf_op jit(solution)/shard_map/ppermute | solution.py:613
  10.5 4.1 %all-to-all-start = ((bf16[32,1,220]{2,1,0:T(2,128)(2,1)}), bf16[32,1,220]{2,1,0:T(2,128)(2,1)S(1)}, u32[]{:S(2)}, u32[]{:S(2)}) async-start(bf16[32,1,220]{2,1,0:T(2,128)(2,1)} %broadcast_in_dim.54), calls=%async_computation | async-start | bytes 65536 | tf_op jit(solution)/shard_map/all_to_all | solution.py:722
  14.7 2.7 collective-permute-start.6
  20.8 9.0 %all-to-all-done = bf16[32,1,220]{2,1,0:T(2,128)(2,1)S(1)} async-done(((bf16[32,1,220]{2,1,0:T(2,128)(2,1)}), bf16[32,1,220]{2,1,0:T(2,128)(2,1)S(1)}, u32[]{:S(2)}, u32[]{:S(2)}) %all-to-all-start) | async-done | bytes 14112 | tf_op jit(solution)/shard_map/all_to_all | solution.py:722
  40.4 2.5 all-to-all-start.1
  43.1 11.7 %all-to-all-done.1 = bf16[32,1,24]{2,1,0:T(2,128)(2,1)S(1)} async-done(((bf16[32,1,24]{2,1,0:T(2,128)(2,1)}), bf16[32,1,24]{2,1,0:T(2,128)(2,1)S(1)}, u32[]{:S(2)}, u32[]{:S(2)}) %all-to-all-start.1) | async-done | bytes 1568 | tf_op jit(solution)/shard_map/all_to_all | solution.py:732
  61.2 5.2 %norm_one.1 = (bf16[1024,768]{1,0:T(8,128)(2,1)}, bf16[1024,768]{1,0:T(8,128)(2,1)}) custom-call(s32[5]{0:T(128)} %stack.45.at_ref, bf16[2,512,768]{2,1,0:T(8,128)(2,1)} %own_ref.1, bf16[512,768]{1,0:T(8,128)(2,1)} %copy-done.17, f32[8,768]{1,0:T(8,128)} %pad_convert_fusion.row_ref.refs_9_), custom_call_target="tpu_custom_call" | custom-call | flops 157286 | bytes 62914 | tf_op jit(solution)/shard_map/norm_one/pallas_call | solution.py:112
  66.4 6.3 %collective-permute-done.11 = bf16[4,24,3072]{2,1,0:T(8,128)(2,1)} collective-permute-done((bf16[4,24,3072]{2,1,0:T(8,128)(2,1)}, bf16[4,24,3072]{2,1,0:T(8,128)(2,1)}, u32[]{:S(2)}, u32[]{:S(2)}) %collective-permute-start.11) | collective-permute-done | bytes 589856 | tf_op jit(solution)/shard_map/ppermute | solution.py:607
  72.7 2.4 broadcast_select_fusion.3
  75.1 2.6 collective-permute-done.10
  88.2 20.3 %attend.1 = (bf16[1024,768]{1,0:T(8,128)(2,1)}, bf16[1024,768]{1,0:T(8,128)(2,1)}, bf16[1024,768]{1,0:T(8,128)(2,1)}, bf16[1024,768]{1,0:T(8,128)(2,1)}, f32[6,2,1024]{2,1,0:T(2,128)}) custom-call(s32[5]{0:T(128)} %stack.45.at_ref, bf16[1024,768]{1,0:T(8,128)(2,1)} %get-tuple-element.159.n_ref, bf16[192,1280]{1,0:T(8,128)(2,1)} %bitcast.185, ...), custom_call_target="tpu_custom_call" | custom-call | flops 330175616 | bytes 314572 | tf_op jit(solution)/shard_map/attend/pallas_call | solution.py:112
  108.5 7.1 %collective-permute-done.18.there_ref = bf16[256,768]{1,0:T(8,128)(2,1)S(1)} collective-permute-done((bf16[256,768]{1,0:T(8,128)(2,1)S(1)}, bf16[256,768]{1,0:T(8,128)(2,1)S(1)}, u32[]{:S(2)}, u32[]{:S(2)}) %collective-permute-start.18) | collective-permute-done | bytes 393248 | tf_op jit(solution)/shard_map/ppermute | solution.py:698
  116.2 3.4 %collective-permute-start.21 = (bf16[256,768]{1,0:T(8,128)(2,1)}, bf16[256,768]{1,0:T(8,128)(2,1)}, u32[]{:S(2)}, u32[]{:S(2)}) collective-permute-start(bf16[256,768]{1,0:T(8,128)(2,1)} %get-tuple-element.193), channel_id=1, source_target_pairs={{0,16},{16,0},{1,17},{17,1},{2,18},{18,2},{3,19},{19,3},{4,20},{20... | collective-permute-start | bytes 1179656 | tf_op jit(solution)/shard_map/ppermute | solution.py:698
  124.0 6.8 %mix.1 = (f32[1024,768]{1,0:T(8,128)}, bf16[1024,768]{1,0:T(8,128)(2,1)}) custom-call(s32[5]{0:T(128)} %stack.45.at_ref, bf16[1024,768]{1,0:T(8,128)(2,1)} %get-tuple-element.109.x_ref.x_any, bf16[1024,768]{1,0:T(8,128)(2,1)} %get-tuple-element.122.o_ref.o_any, bf16[192,3840]{1,0:T(8,128)(2,1)} %bitcast.169, bf16[192,3840]{1,0:T(8,128)(2,1)} %bitcast.175, ...), custom_call_target="tpu_custom_call" | custom-call | flops 24159192 | bytes 188743 | tf_op jit(solution)/shard_map/mix/pallas_call | solution.py:112
  130.9 34.9 %ffn.1 = (bf16[512,768]{1,0:T(8,128)(2,1)}, bf16[512,768]{1,0:T(8,128)(2,1)}, bf16[1024,3072]{1,0:T(8,128)(2,1)}, bf16[1536,768]{1,0:T(8,128)(2,1)}, bf16[1536,7...) custom-call(s32[5]{0:T(128)} %stack.45.at_ref, ...), custom_call_target="tpu_custom_call" | custom-call | flops 386547072 | bytes 692060 | tf_op jit(solution)/shard_map/ffn/pallas_call | solution.py:112
  167.4 22.7 %unffn.1 = (f32[1024,768]{1,0:T(8,128)}, bf16[1024,768]{1,0:T(8,128)(2,1)}, bf16[384,3840]{1,0:T(8,128)(2,1)}, bf16[384,3840]{1,0:T(8,128)(2,1)}, f32[2,768]{1,0:T(2,128)}) custom-call(s32[5]{0:T(128)} %stack.45.at_ref, bf16[1024,768]{1,0:T(8,128)(2,1)} %get-tuple-element.124.n_ref, bf16[1024,768]{1,0:T(8,128)(2,1)} %get-tuple-element.128.dy_any, ...), custom_call_target="tpu_custom_call" | custom-call | flops 241591904 | bytes 692060 | tf_op jit(solution)/shard_map/unffn/pallas_call | solution.py:112
  190.3 2.3 add_convert_fusion.1
  192.9 2.1 collective-permute-start.29
  196.3 13.0 %attend_back_0.1 = (bf16[1024,768]{1,0:T(8,128)(2,1)}, bf16[1024,768]{1,0:T(8,128)(2,1)}, bf16[1024,768]{1,0:T(8,128)(2,1)}) custom-call(s32[5]{0:T(128)} %stack.45.at_ref, bf16[1024,768]{1,0:T(8,128)(2,1)} %get-tuple-element.144.q_ref, bf16[1024,768]{1,0:T(8,128)(2,1)} %get-tuple-element.145.k_ref, bf16[1024,768]{1,0:T(8,128)(2,1)} %get-tuple-element.146.v_ref, ...), custom_call_target="tpu_custom_call" | custom-call | flops 322122560 | bytes 125829 | tf_op jit(solution)/shard_map/attend_back_0/pallas_call | solution.py:112
  209.3 2.2 fusion.2
  214.0 2.6 add_convert_fusion
  219.0 6.7 %collective-permute-start.31 = (bf16[2,4,24,1920]{3,2,1,0:T(8,128)(2,1)}, bf16[2,4,24,1920]{3,2,1,0:T(8,128)(2,1)}, u32[]{:S(2)}, u32[]{:S(2)}) collective-permute-start(bf16[2,4,24,1920]{3,2,1,0:T(8,128)(2,1)} %dynamic-slice_bitcast_fusion.1), channel_id=1, source_target_pairs={{0,2},{1,3},{2,0},{3,1},{4,6},{5,7},{6,4},{7,5},{8,10},{9,11},{10,... | collective-permute-start | bytes 2211848 | tf_op jit(solution)/shard_map/ppermute | solution.py:607
  232.0 13.0 %attend_back_1.1 = (bf16[1024,768]{1,0:T(8,128)(2,1)}, bf16[1024,768]{1,0:T(8,128)(2,1)}, bf16[1024,768]{1,0:T(8,128)(2,1)}) custom-call(s32[5]{0:T(128)} %stack.45.at_ref, bf16[1024,768]{1,0:T(8,128)(2,1)} %get-tuple-element.144.q_ref, bf16[1024,768]{1,0:T(8,128)(2,1)} %get-tuple-element.145.k_ref, ...), custom_call_target="tpu_custom_call", output_to_operand_aliasing={{0}: (7, {}), {1}: (8, {}), {2}: (9, {})} | custom-call | flops 322122560 | bytes 125829 | tf_op jit(solution)/shard_map/attend_back_1/pallas_call | solution.py:112
  248.7 3.2 collective-permute-done.33
  256.1 9.3 %grad_qkv.1 = (bf16[3,384,768]{2,1,0:T(8,128)(2,1)}, bf16[3,384,768]{2,1,0:T(8,128)(2,1)}) custom-call(s32[5]{0:T(128)} %stack.45.at_ref, bf16[1024,768]{1,0:T(8,128)(2,1)} %get-tuple-element.159.n_ref, bf16[1024,768]{1,0:T(8,128)(2,1)} %get-tuple-element.160.dq_ref.refs_16_, bf16[1024,768]{1,0:T(8,128)(2,1)} %get-tuple-element.161.dk_ref.refs_17_, ...), custom_call_target="tpu_custom_call" | custom-call | flops 72477576 | bytes 314572 | tf_op jit(solution)/shard_map/grad_qkv/pallas_call | solution.py:112
  265.6 2.5 broadcast_select_fusion.1
  268.1 2.4 collective-permute-start.40
  275.0 12.1 %unqkv.1 = (bf16[512,768]{1,0:T(8,128)(2,1)}, bf16[512,768]{1,0:T(8,128)(2,1)}, f32[3,768]{1,0:T(4,128)}) custom-call(s32[5]{0:T(128)} %stack.45.at_ref, bf16[1024,768]{1,0:T(8,128)(2,1)} %get-tuple-element.109.x_ref.x_any, f32[8,768]{1,0:T(8,128)} %pad_convert_fusion.row_ref.refs_9_, f32[1024,768]{1,0:T(8,128)} %get-tuple-element.170.dmid_any, ...), custom_call_target="tpu_custom_call" | custom-call | flops 72477576 | bytes 471859 | tf_op jit(solution)/shard_map/unqkv/pallas_call | solution.py:112
  293.2 5.2 %collective-permute-done.48 = bf16[24,3840]{1,0:T(8,128)(2,1)S(1)} collective-permute-done((bf16[24,3840]{1,0:T(8,128)(2,1)S(1)}, bf16[24,3840]{1,0:T(8,128)(2,1)S(1)}, u32[]{:S(2)}, u32[]{:S(2)}) %collective-permute-start.48) | collective-permute-done | bytes 184352 | tf_op jit(solution)/shard_map/ppermute | solution.py:610
  300.8 3.0 all-to-all-start.2
  305.9 2.4 collective-permute-start.45
  309.7 4.6 %all-to-all-done.2 = f32[32,1,240]{2,1,0:T(1,128)S(1)} async-done(((f32[32,1,240]{2,1,0:T(1,128)}), f32[32,1,240]{2,1,0:T(1,128)S(1)}, u32[]{:S(2)}, u32[]{:S(2)}) %all-to-all-start.2) | async-done | bytes 30752 | tf_op jit(solution)/shard_map/all_to_all | solution.py:849
  (278 shorter events, 83.0 us)
Async XLA Ops:
  0.8 16.7 %collective-permute-start = (bf16[24,2304]{1,0:T(8,128)(2,1)}, bf16[24,2304]{1,0:T(8,128)(2,1)S(1)}, u32[]{:S(2)}, u32[]{:S(2)}) collective-permute-start(bf16[24,2304]{1,0:T(8,128)(2,1)} %param.19), channel_id=1, source_target_pairs={{0,12},{1,13},{2,14},{3,15},{4,0},{5,1},{6,2},{7,3},{8,4},{9,5},{1... | collective-permute-start | bytes 331784 | tf_op jit(solution)/shard_map/ppermute | solution.py:613
  8.1 25.3 %collective-permute-start.5 = (bf16[512,768]{1,0:T(8,128)(2,1)S(1)}, bf16[512,768]{1,0:T(8,128)(2,1)S(1)}, u32[]{:S(2)}, u32[]{:S(2)}) collective-permute-start(bf16[512,768]{1,0:T(8,128)(2,1)S(1)} %dynamic-slice_bitcast_fusion), channel_id=1, source_target_pairs={{0,16},{16,0},{1,17},{17,1},{2,18},{18,2},{3,19},{19,3},{4,20},{20... | collective-permute-start | bytes 2359304 | tf_op jit(solution)/shard_map/ppermute | solution.py:698
  10.5 19.4 %all-to-all-start = ((bf16[32,1,220]{2,1,0:T(2,128)(2,1)}), bf16[32,1,220]{2,1,0:T(2,128)(2,1)S(1)}, u32[]{:S(2)}, u32[]{:S(2)}) async-start(bf16[32,1,220]{2,1,0:T(2,128)(2,1)} %broadcast_in_dim.54), calls=%async_computation | async-start | bytes 65536 | tf_op jit(solution)/shard_map/all_to_all | solution.py:722
  14.7 18.7 %collective-permute-start.6 = (bf16[24,6912]{1,0:T(8,128)(2,1)S(1)}, bf16[24,6912]{1,0:T(8,128)(2,1)}, u32[]{:S(2)}, u32[]{:S(2)}) collective-permute-start(bf16[24,6912]{1,0:T(8,128)(2,1)S(1)} %constant_dynamic-update-slice_fusion), channel_id=1, source_target_pairs={{0,8},{1,9},{2,10},{3,11},{4,12},{5,13},{6,14},{7,15},{8,0},{9,1},... | collective-permute-start | bytes 995336 | tf_op jit(solution)/shard_map/ppermute | solution.py:610
  34.7 20.2 %collective-permute-start.7 = (bf16[2,24,6912]{2,1,0:T(8,128)(2,1)S(1)}, bf16[2,24,6912]{2,1,0:T(8,128)(2,1)}, u32[]{:S(2)}, u32[]{:S(2)}) collective-permute-start(bf16[2,24,6912]{2,1,0:T(8,128)(2,1)S(1)} %broadcast_select_fusion.4), channel_id=1, source_target_pairs={{0,4},{1,5},{2,6},{3,7},{4,0},{5,1},{6,2},{7,3},{8,12},{9,13},{10,... | collective-permute-start | bytes 1990664 | tf_op jit(solution)/shard_map/ppermute | solution.py:610
  36.3 18.7 %collective-permute-start.8 = (bf16[2,4,24,1280]{3,2,1,0:T(8,128)(2,1)S(1)}, bf16[2,4,24,1280]{3,2,1,0:T(8,128)(2,1)S(1)}, u32[]{:S(2)}, u32[]{:S(2)}) collective-permute-start(bf16[2,4,24,1280]{3,2,1,0:T(8,128)(2,1)S(1)} %broadcast_select_fusion.5), channel_id=1, source_target_pairs={{0,2},{1,3},{2,0},{3,1},{4,6},{5,7},{6,4},{7,5},{8,10},{9,11},{10,... | collective-permute-start | bytes 1474568 | tf_op jit(solution)/shard_map/ppermute | solution.py:607
  37.8 17.1 %collective-permute-start.9 = (bf16[4,2,24,1024]{3,2,1,0:T(8,128)(2,1)}, bf16[4,2,24,1024]{3,2,1,0:T(8,128)(2,1)}, u32[]{:S(2)}, u32[]{:S(2)}) collective-permute-start(bf16[4,2,24,1024]{3,2,1,0:T(8,128)(2,1)} %broadcast_select_fusion.6), channel_id=1, source_target_pairs={{0,16},{1,17},{2,18},{3,19},{4,20},{5,21},{6,22},{7,23},{8,24},{9,... | collective-permute-start | bytes 1179656 | tf_op jit(solution)/shard_map/ppermute | solution.py:607
  57.3 15.4 %collective-permute-start.11 = (bf16[4,24,3072]{2,1,0:T(8,128)(2,1)}, bf16[4,24,3072]{2,1,0:T(8,128)(2,1)}, u32[]{:S(2)}, u32[]{:S(2)}) collective-permute-start(bf16[4,24,3072]{2,1,0:T(8,128)(2,1)} %slice.135), channel_id=1, source_target_pairs={{0,2},{1,3},{2,0},{3,1},{4,6},{5,7},{6,4},{7,5},{8,10},{9,11},{10,... | collective-permute-start | bytes 1769480 | tf_op jit(solution)/shard_map/ppermute | solution.py:607
  59.7 18.0 %collective-permute-start.10 = (bf16[4,24,3840]{2,1,0:T(8,128)(2,1)S(1)}, bf16[4,24,3840]{2,1,0:T(8,128)(2,1)S(1)}, u32[]{:S(2)}, u32[]{:S(2)}) collective-permute-start(bf16[4,24,3840]{2,1,0:T(8,128)(2,1)S(1)} %slice.134), channel_id=1, source_target_pairs={{0,16},{1,17},{2,18},{3,19},{4,20},{5,21},{6,22},{7,23},{8,24},{9,... | collective-permute-start | bytes 2211848 | tf_op jit(solution)/shard_map/ppermute | solution.py:607
  79.1 36.5 %collective-permute-start.12 = (bf16[2,4,24,3840]{3,2,1,0:T(8,128)(2,1)S(1)}, bf16[2,4,24,3840]{3,2,1,0:T(8,128)(2,1)S(1)}, u32[]{:S(2)}, u32[]{:S(2)}) collective-permute-start(bf16[2,4,24,3840]{3,2,1,0:T(8,128)(2,1)S(1)} %broadcast_select_fusion.2), channel_id=1, source_target_pairs={{0,2},{1,3},{2,0},{3,1},{4,6},{5,7},{6,4},{7,5},{8,10},{9,11},{10,... | collective-permute-start | bytes 4423688 | tf_op jit(solution)/shard_map/ppermute | solution.py:607
  80.6 34.9 %collective-permute-start.13 = (bf16[4,2,24,3072]{3,2,1,0:T(8,128)(2,1)}, bf16[4,2,24,3072]{3,2,1,0:T(8,128)(2,1)}, u32[]{:S(2)}, u32[]{:S(2)}) collective-permute-start(bf16[4,2,24,3072]{3,2,1,0:T(8,128)(2,1)} %broadcast_select_fusion.3), channel_id=1, source_target_pairs={{0,16},{1,17},{2,18},{3,19},{4,20},{5,21},{6,22},{7,23},{8,24},{9,... | collective-permute-start | bytes 3538952 | tf_op jit(solution)/shard_map/ppermute | solution.py:607
  85.8 29.7 %collective-permute-start.18 = (bf16[256,768]{1,0:T(8,128)(2,1)S(1)}, bf16[256,768]{1,0:T(8,128)(2,1)S(1)}, u32[]{:S(2)}, u32[]{:S(2)}) collective-permute-start(bf16[256,768]{1,0:T(8,128)(2,1)S(1)} %get-tuple-element.194), channel_id=1, source_target_pairs={{0,16},{16,0},{1,17},{17,1},{2,18},{18,2},{3,19},{19,3},{4,20},{20... | collective-permute-start | bytes 1179656 | tf_op jit(solution)/shard_map/ppermute | solution.py:698
  87.3 33.0 %collective-permute-start.19 = (bf16[2,4,24,3840]{3,2,1,0:T(8,128)(2,1)S(1)}, bf16[2,4,24,3840]{3,2,1,0:T(8,128)(2,1)S(1)}, u32[]{:S(2)}, u32[]{:S(2)}) collective-permute-start(bf16[2,4,24,3840]{3,2,1,0:T(8,128)(2,1)S(1)} %broadcast_select_fusion.2), channel_id=1, source_target_pairs={{0,1},{1,0},{2,3},{3,2},{4,5},{5,4},{6,7},{7,6},{8,9},{9,8},{10,11... | collective-permute-start | bytes 4423688 | tf_op jit(solution)/shard_map/ppermute | solution.py:607
  115.6 15.3 %collective-permute-start.22 = (bf16[2,4,24,3840]{3,2,1,0:T(8,128)(2,1)S(1)}, bf16[2,4,24,3840]{3,2,1,0:T(8,128)(2,1)}, u32[]{:S(2)}, u32[]{:S(2)}) collective-permute-start(bf16[2,4,24,3840]{3,2,1,0:T(8,128)(2,1)S(1)} %collective-permute-done.12), channel_id=1, source_target_pairs={{0,1},{1,0},{2,3},{3,2},{4,5},{5,4},{6,7},{7,6},{8,9},{9,8},{10,11... | collective-permute-start | bytes 4423688 | tf_op jit(solution)/shard_map/ppermute | solution.py:607
  115.7 15.2 %collective-permute-start.23 = (bf16[4,2,24,3072]{3,2,1,0:T(8,128)(2,1)}, bf16[4,2,24,3072]{3,2,1,0:T(8,128)(2,1)}, u32[]{:S(2)}, u32[]{:S(2)}) collective-permute-start(bf16[4,2,24,3072]{3,2,1,0:T(8,128)(2,1)} %broadcast_select_fusion.3), channel_id=1, source_target_pairs={{0,1},{1,0},{2,3},{3,2},{4,5},{5,4},{6,7},{7,6},{8,9},{9,8},{10,11... | collective-permute-start | bytes 3538952 | tf_op jit(solution)/shard_map/ppermute | solution.py:607
  116.2 14.7 %collective-permute-start.24 = (bf16[4,2,24,3072]{3,2,1,0:T(8,128)(2,1)}, bf16[4,2,24,3072]{3,2,1,0:T(8,128)(2,1)}, u32[]{:S(2)}, u32[]{:S(2)}) collective-permute-start(bf16[4,2,24,3072]{3,2,1,0:T(8,128)(2,1)} %collective-permute-done.13), channel_id=1, source_target_pairs={{0,1},{1,0},{2,3},{3,2},{4,5},{5,4},{6,7},{7,6},{8,9},{9,8},{10,11... | collective-permute-start | bytes 3538952 | tf_op jit(solution)/shard_map/ppermute | solution.py:607
  165.8 24.5 %collective-permute-start.26 = (bf16[1536,768]{1,0:T(8,128)(2,1)}, bf16[1536,768]{1,0:T(8,128)(2,1)}, u32[]{:S(2)}, u32[]{:S(2)}) collective-permute-start(bf16[1536,768]{1,0:T(8,128)(2,1)} %get-tuple-element.139), channel_id=1, source_target_pairs={{0,1},{1,0},{2,3},{3,2},{4,5},{5,4},{6,7},{7,6},{8,9},{9,8},{10,11... | collective-permute-start | bytes 7077896 | tf_op jit(solution)/shard_map/ppermute | solution.py:607
  166.0 24.1 %collective-permute-start.25 = (bf16[512,768]{1,0:T(8,128)(2,1)}, bf16[512,768]{1,0:T(8,128)(2,1)}, u32[]{:S(2)}, u32[]{:S(2)}) collective-permute-start(bf16[512,768]{1,0:T(8,128)(2,1)} %get-tuple-element.135), channel_id=1, source_target_pairs={{0,16},{16,0},{1,17},{17,1},{2,18},{18,2},{3,19},{19,3},{4,20},{20... | collective-permute-start | bytes 2359304 | tf_op jit(solution)/shard_map/ppermute | solution.py:698
  190.1 23.9 %collective-permute-start.27 = (bf16[384,3840]{1,0:T(8,128)(2,1)}, bf16[384,3840]{1,0:T(8,128)(2,1)}, u32[]{:S(2)}, u32[]{:S(2)}) collective-permute-start(bf16[384,3840]{1,0:T(8,128)(2,1)} %get-tuple-element.142), channel_id=1, source_target_pairs={{0,1},{1,0},{2,3},{3,2},{4,5},{5,4},{6,7},{7,6},{8,9},{9,8},{10,11... | collective-permute-start | bytes 8847368 | tf_op jit(solution)/shard_map/ppermute | solution.py:607
  192.9 16.4 %collective-permute-start.29 = (bf16[2,4,96,384]{3,2,1,0:T(8,128)(2,1)S(1)}, bf16[2,4,96,384]{3,2,1,0:T(8,128)(2,1)}, u32[]{:S(2)}, u32[]{:S(2)}) collective-permute-start(bf16[2,4,96,384]{3,2,1,0:T(8,128)(2,1)S(1)} %dynamic-slice_bitcast_fusion.3), channel_id=1, source_target_pairs={{0,2},{1,3},{2,0},{3,1},{4,6},{5,7},{6,4},{7,5},{8,10},{9,11},{10,... | collective-permute-start | bytes 1769480 | tf_op jit(solution)/shard_map/ppermute | solution.py:607
  196.2 15.7 %collective-permute-start.28 = (bf16[4,2,96,384]{3,2,0,1:T(8,128)(2,1)}, bf16[4,2,96,384]{3,2,0,1:T(8,128)(2,1)}, u32[]{:S(2)}, u32[]{:S(2)}) collective-permute-start(bf16[4,2,96,384]{3,2,0,1:T(8,128)(2,1)} %dynamic-slice_bitcast_fusion.4), channel_id=1, source_target_pairs={{0,16},{1,17},{2,18},{3,19},{4,20},{5,21},{6,22},{7,23},{8,24},{9,... | collective-permute-start | bytes 1769480 | tf_op jit(solution)/shard_map/ppermute | solution.py:607
  219.0 26.0 %collective-permute-start.31 = (bf16[2,4,24,1920]{3,2,1,0:T(8,128)(2,1)}, bf16[2,4,24,1920]{3,2,1,0:T(8,128)(2,1)}, u32[]{:S(2)}, u32[]{:S(2)}) collective-permute-start(bf16[2,4,24,1920]{3,2,1,0:T(8,128)(2,1)} %dynamic-slice_bitcast_fusion.1), channel_id=1, source_target_pairs={{0,2},{1,3},{2,0},{3,1},{4,6},{5,7},{6,4},{7,5},{8,10},{9,11},{10,... | collective-permute-start | bytes 2211848 | tf_op jit(solution)/shard_map/ppermute | solution.py:607
  227.5 19.5 %collective-permute-start.30 = (bf16[4,2,24,1920]{3,2,0,1:T(8,128)(2,1)S(1)}, bf16[4,2,24,1920]{3,2,0,1:T(8,128)(2,1)S(1)}, u32[]{:S(2)}, u32[]{:S(2)}) collective-permute-start(bf16[4,2,24,1920]{3,2,0,1:T(8,128)(2,1)S(1)} %dynamic-slice_bitcast_fusion.2), channel_id=1, source_target_pairs={{0,16},{1,17},{2,18},{3,19},{4,20},{5,21},{6,22},{7,23},{8,24},{9,... | collective-permute-start | bytes 2211848 | tf_op jit(solution)/shard_map/ppermute | solution.py:607
  229.0 19.7 %collective-permute-start.32 = (bf16[4,96,384]{2,1,0:T(8,128)(2,1)S(1)}, bf16[4,96,384]{2,1,0:T(8,128)(2,1)S(1)}, u32[]{:S(2)}, u32[]{:S(2)}) collective-permute-start(bf16[4,96,384]{2,1,0:T(8,128)(2,1)S(1)} %dynamic-slice_bitcast_fusion.12), channel_id=1, source_target_pairs={{0,2},{1,3},{2,0},{3,1},{4,6},{5,7},{6,4},{7,5},{8,10},{9,11},{10,... | collective-permute-start | bytes 884744 | tf_op jit(solution)/shard_map/ppermute | solution.py:607
  231.2 20.7 %collective-permute-start.33 = (bf16[4,96,384]{2,1,0:T(8,128)(2,1)S(1)}, bf16[4,96,384]{2,1,0:T(8,128)(2,1)S(1)}, u32[]{:S(2)}, u32[]{:S(2)}) collective-permute-start(bf16[4,96,384]{2,1,0:T(8,128)(2,1)S(1)} %dynamic-slice_bitcast_fusion.11), channel_id=1, source_target_pairs={{0,16},{1,17},{2,18},{3,19},{4,20},{5,21},{6,22},{7,23},{8,24},{9,... | collective-permute-start | bytes 884744 | tf_op jit(solution)/shard_map/ppermute | solution.py:607
  252.2 15.9 %collective-permute-start.39 = (bf16[2,96,768]{2,1,0:T(8,128)(2,1)S(1)}, bf16[2,96,768]{2,1,0:T(8,128)(2,1)S(1)}, u32[]{:S(2)}, u32[]{:S(2)}) collective-permute-start(bf16[2,96,768]{2,1,0:T(8,128)(2,1)S(1)} %dynamic-slice_bitcast_fusion.10), channel_id=1, source_target_pairs={{0,4},{1,5},{2,6},{3,7},{4,0},{5,1},{6,2},{7,3},{8,12},{9,13},{10,... | collective-permute-start | bytes 884744 | tf_op jit(solution)/shard_map/ppermute | solution.py:610
  252.5 18.1 %collective-permute-start.34 = (bf16[4,24,1920]{2,1,0:T(8,128)(2,1)S(1)}, bf16[4,24,1920]{2,1,0:T(8,128)(2,1)S(1)}, u32[]{:S(2)}, u32[]{:S(2)}) collective-permute-start(bf16[4,24,1920]{2,1,0:T(8,128)(2,1)S(1)} %dynamic-slice_bitcast_fusion.9), channel_id=1, source_target_pairs={{0,2},{1,3},{2,0},{3,1},{4,6},{5,7},{6,4},{7,5},{8,10},{9,11},{10,... | collective-permute-start | bytes 1105928 | tf_op jit(solution)/shard_map/ppermute | solution.py:607
  254.3 16.2 %collective-permute-start.35 = (bf16[4,24,1920]{2,1,0:T(8,128)(2,1)S(1)}, bf16[4,24,1920]{2,1,0:T(8,128)(2,1)S(1)}, u32[]{:S(2)}, u32[]{:S(2)}) collective-permute-start(bf16[4,24,1920]{2,1,0:T(8,128)(2,1)S(1)} %dynamic-slice_bitcast_fusion.8), channel_id=1, source_target_pairs={{0,16},{1,17},{2,18},{3,19},{4,20},{5,21},{6,22},{7,23},{8,24},{9,... | collective-permute-start | bytes 1105928 | tf_op jit(solution)/shard_map/ppermute | solution.py:607
  268.1 20.9 %collective-permute-start.40 = (bf16[96,768]{1,0:T(8,128)(2,1)S(1)}, bf16[96,768]{1,0:T(8,128)(2,1)S(1)}, u32[]{:S(2)}, u32[]{:S(2)}) collective-permute-start(bf16[96,768]{1,0:T(8,128)(2,1)S(1)} %fusion.26), channel_id=1, source_target_pairs={{0,8},{1,9},{2,10},{3,11},{4,12},{5,13},{6,14},{7,15},{8,0},{9,1},... | collective-permute-start | bytes 442376 | tf_op jit(solution)/shard_map/ppermute | solution.py:610
  272.8 15.9 %collective-permute-start.38 = (bf16[2,4,24,1152]{3,2,1,0:T(8,128)(2,1)S(1)}, bf16[2,4,24,1152]{3,2,1,0:T(8,128)(2,1)S(1)}, u32[]{:S(2)}, u32[]{:S(2)}) collective-permute-start(bf16[2,4,24,1152]{3,2,1,0:T(8,128)(2,1)S(1)} %fusion.13), channel_id=1, source_target_pairs={{0,2},{1,3},{2,0},{3,1},{4,6},{5,7},{6,4},{7,5},{8,10},{9,11},{10,... | collective-permute-start | bytes 1327112 | tf_op jit(solution)/shard_map/ppermute | solution.py:607
  273.8 15.0 %collective-permute-start.37 = (bf16[4,2,24,1152]{3,2,0,1:T(8,128)(2,1)S(1)}, bf16[4,2,24,1152]{3,2,0,1:T(8,128)(2,1)S(1)}, u32[]{:S(2)}, u32[]{:S(2)}) collective-permute-start(bf16[4,2,24,1152]{3,2,0,1:T(8,128)(2,1)S(1)} %fusion.17), channel_id=1, source_target_pairs={{0,16},{1,17},{2,18},{3,19},{4,20},{5,21},{6,22},{7,23},{8,24},{9,... | collective-permute-start | bytes 1327112 | tf_op jit(solution)/shard_map/ppermute | solution.py:607
  292.2 25.3 %collective-permute-start.41 = (bf16[512,768]{1,0:T(8,128)(2,1)}, bf16[512,768]{1,0:T(8,128)(2,1)S(1)}, u32[]{:S(2)}, u32[]{:S(2)}) collective-permute-start(bf16[512,768]{1,0:T(8,128)(2,1)} %get-tuple-element.176), channel_id=1, source_target_pairs={{0,16},{16,0},{1,17},{17,1},{2,18},{18,2},{3,19},{19,3},{4,20},{20... | collective-permute-start | bytes 2359304 | tf_op jit(solution)/shard_map/ppermute | solution.py:698
  (56 other events, 615.1 us)

commit v6 on v5

--- a/solution.py
+++ b/solution.py
@@ -134,7 +134,7 @@
     n_ref[...] = (xhat * row_ref[1:2, :] + row_ref[2:3, :]).astype(bf16)
 
 
-def norm_one(at, both, other, rows, tb=256):
+def norm_one(at, both, other, rows, tb=512):
     half, d = other.shape
     t = 2 * half
     steps = half // tb
@@ -314,7 +314,7 @@
     ]
 
 
-def mix(at, x, o, out, rows, tb=256):
+def mix(at, x, o, out, rows, tb=512):
     t, d = x.shape
     tok = pl.BlockSpec((tb, d), lambda i, s: (i, 0))
     return call(

time: 324 us -> 324 us (level)
  transfers between devices with their start and end apart: 52 -> 52, of which waited for: 15 -> 14; matrix products, arithmetic and copies ran while one was open for 10% -> 10% of each run, Pallas kernels for 32% -> 32%
where the time goes in v6:
time: 324 us; the launch traced here: 319 us
  Pallas kernels  136 us (42%)
  starting transfers between devices  72 us (22%)
  waiting for transfers between devices  58.4 us (18%)
  other arithmetic  26.6 us (8%)
  local copies, waits for them, and re-layouts  21.7 us (7%)
    pallas_call x9, Pallas kernels, call(): pl.pallas_call(kernel, grid_spec=pltpu.PrefetchScalarGridSpec(num_scalar_...  136 us
    ppermute x32, starting transfers between devices, swap(): return lax.ppermute(v, BOTH, self.table(move))  32 us
    ppermute x32, waiting for transfers between devices, swap(): return lax.ppermute(v, BOTH, self.table(move))  20.2 us
    ppermute x6, starting transfers between devices, shift(): lax.ppermute(v, BOTH, self.table(lambda x, z, y, c: (x, (z + by) % 4, y,...  11.8 us
    all_to_all x1, waiting for transfers between devices, look_up(): found = lax.all_to_all(found, BOTH, split_axis=0, concat_axis=0, tiled=True)  11.7 us
    convert_element_type x15, other arithmetic, add(): return (a.astype(f32) + b.astype(f32)).astype(bf16)  11.7 us
    select_n x8, other arithmetic, pair(): return jnp.where(here, spread(own, axis, 2), spread(other, axis, 2))  11.3 us
    ppermute x6, starting transfers between devices, cross(): lax.ppermute(v, BOTH, self.table(lambda x, z, y, c: (x, z ^ bit, y, c)))  9.95 us
  transfers between devices with their start and end apart: 52, of which 14 were waited for; matrix products, arithmetic and copies ran while one was open for 10% of the time, Pallas kernels for 32%

profile of v6, /device:TPU:0, one launch (start us, length us, event | category | flops | bytes accessed | tf_op | source)
XLA Modules:
  0.0 318.6 jit_solution(9856609601097132132)
XLA Ops:
  0.8 5.1 %collective-permute-start = (bf16[24,2304]{1,0:T(8,128)(2,1)}, bf16[24,2304]{1,0:T(8,128)(2,1)S(1)}, u32[]{:S(2)}, u32[]{:S(2)}) collective-permute-start(bf16[24,2304]{1,0:T(8,128)(2,1)} %param.19), channel_id=1, source_target_pairs={{0,12},{1,13},{2,14},{3,15},{4,0},{5,1},{6,2},{7,3},{8,4},{9,5},{1... | collective-permute-start | bytes 331784 | tf_op jit(solution)/shard_map/ppermute | solution.py:613
  10.5 4.1 %all-to-all-start = ((bf16[32,1,220]{2,1,0:T(2,128)(2,1)}), bf16[32,1,220]{2,1,0:T(2,128)(2,1)S(1)}, u32[]{:S(2)}, u32[]{:S(2)}) async-start(bf16[32,1,220]{2,1,0:T(2,128)(2,1)} %broadcast_in_dim.54), calls=%async_computation | async-start | bytes 65536 | tf_op jit(solution)/shard_map/all_to_all | solution.py:722
  14.7 2.7 collective-permute-start.6
  20.8 9.0 %all-to-all-done = bf16[32,1,220]{2,1,0:T(2,128)(2,1)S(1)} async-done(((bf16[32,1,220]{2,1,0:T(2,128)(2,1)}), bf16[32,1,220]{2,1,0:T(2,128)(2,1)S(1)}, u32[]{:S(2)}, u32[]{:S(2)}) %all-to-all-start) | async-done | bytes 14112 | tf_op jit(solution)/shard_map/all_to_all | solution.py:722
  40.4 2.5 all-to-all-start.1
  43.1 11.7 %all-to-all-done.1 = bf16[32,1,24]{2,1,0:T(2,128)(2,1)S(1)} async-done(((bf16[32,1,24]{2,1,0:T(2,128)(2,1)}), bf16[32,1,24]{2,1,0:T(2,128)(2,1)S(1)}, u32[]{:S(2)}, u32[]{:S(2)}) %all-to-all-start.1) | async-done | bytes 1568 | tf_op jit(solution)/shard_map/all_to_all | solution.py:732
  61.2 4.4 %norm_one.1 = (bf16[1024,768]{1,0:T(8,128)(2,1)}, bf16[1024,768]{1,0:T(8,128)(2,1)}) custom-call(s32[5]{0:T(128)} %stack.45.at_ref, bf16[2,512,768]{2,1,0:T(8,128)(2,1)} %own_ref.1, bf16[512,768]{1,0:T(8,128)(2,1)} %copy-done.17, f32[8,768]{1,0:T(8,128)} %pad_convert_fusion.row_ref.refs_9_), custom_call_target="tpu_custom_call" | custom-call | flops 157286 | bytes 62914 | tf_op jit(solution)/shard_map/norm_one/pallas_call | solution.py:112
  65.6 7.1 %collective-permute-done.11 = bf16[4,24,3072]{2,1,0:T(8,128)(2,1)} collective-permute-done((bf16[4,24,3072]{2,1,0:T(8,128)(2,1)}, bf16[4,24,3072]{2,1,0:T(8,128)(2,1)}, u32[]{:S(2)}, u32[]{:S(2)}) %collective-permute-start.11) | collective-permute-done | bytes 589856 | tf_op jit(solution)/shard_map/ppermute | solution.py:607
  72.7 2.4 broadcast_select_fusion.3
  75.1 2.6 collective-permute-done.10
  88.2 20.3 %attend.1 = (bf16[1024,768]{1,0:T(8,128)(2,1)}, bf16[1024,768]{1,0:T(8,128)(2,1)}, bf16[1024,768]{1,0:T(8,128)(2,1)}, bf16[1024,768]{1,0:T(8,128)(2,1)}, f32[6,2,1024]{2,1,0:T(2,128)}) custom-call(s32[5]{0:T(128)} %stack.45.at_ref, bf16[1024,768]{1,0:T(8,128)(2,1)} %get-tuple-element.159.n_ref, bf16[192,1280]{1,0:T(8,128)(2,1)} %bitcast.185, ...), custom_call_target="tpu_custom_call" | custom-call | flops 330175616 | bytes 314572 | tf_op jit(solution)/shard_map/attend/pallas_call | solution.py:112
  108.5 7.1 %collective-permute-done.18.there_ref = bf16[256,768]{1,0:T(8,128)(2,1)S(1)} collective-permute-done((bf16[256,768]{1,0:T(8,128)(2,1)S(1)}, bf16[256,768]{1,0:T(8,128)(2,1)S(1)}, u32[]{:S(2)}, u32[]{:S(2)}) %collective-permute-start.18) | collective-permute-done | bytes 393248 | tf_op jit(solution)/shard_map/ppermute | solution.py:698
  116.2 3.4 %collective-permute-start.21 = (bf16[256,768]{1,0:T(8,128)(2,1)}, bf16[256,768]{1,0:T(8,128)(2,1)}, u32[]{:S(2)}, u32[]{:S(2)}) collective-permute-start(bf16[256,768]{1,0:T(8,128)(2,1)} %get-tuple-element.193), channel_id=1, source_target_pairs={{0,16},{16,0},{1,17},{17,1},{2,18},{18,2},{3,19},{19,3},{4,20},{20... | collective-permute-start | bytes 1179656 | tf_op jit(solution)/shard_map/ppermute | solution.py:698
  124.0 6.2 %mix.1 = (f32[1024,768]{1,0:T(8,128)}, bf16[1024,768]{1,0:T(8,128)(2,1)}) custom-call(s32[5]{0:T(128)} %stack.45.at_ref, bf16[1024,768]{1,0:T(8,128)(2,1)} %get-tuple-element.109.x_ref.x_any, bf16[1024,768]{1,0:T(8,128)(2,1)} %get-tuple-element.122.o_ref.o_any, bf16[192,3840]{1,0:T(8,128)(2,1)} %bitcast.169, bf16[192,3840]{1,0:T(8,128)(2,1)} %bitcast.175, ...), custom_call_target="tpu_custom_call" | custom-call | flops 24159192 | bytes 188743 | tf_op jit(solution)/shard_map/mix/pallas_call | solution.py:112
  130.3 34.9 %ffn.1 = (bf16[512,768]{1,0:T(8,128)(2,1)}, bf16[512,768]{1,0:T(8,128)(2,1)}, bf16[1024,3072]{1,0:T(8,128)(2,1)}, bf16[1536,768]{1,0:T(8,128)(2,1)}, bf16[1536,7...) custom-call(s32[5]{0:T(128)} %stack.45.at_ref, ...), custom_call_target="tpu_custom_call" | custom-call | flops 386547072 | bytes 692060 | tf_op jit(solution)/shard_map/ffn/pallas_call | solution.py:112
  166.8 22.7 %unffn.1 = (f32[1024,768]{1,0:T(8,128)}, bf16[1024,768]{1,0:T(8,128)(2,1)}, bf16[384,3840]{1,0:T(8,128)(2,1)}, bf16[384,3840]{1,0:T(8,128)(2,1)}, f32[2,768]{1,0:T(2,128)}) custom-call(s32[5]{0:T(128)} %stack.45.at_ref, bf16[1024,768]{1,0:T(8,128)(2,1)} %get-tuple-element.124.n_ref, bf16[1024,768]{1,0:T(8,128)(2,1)} %get-tuple-element.128.dy_any, ...), custom_call_target="tpu_custom_call" | custom-call | flops 241591904 | bytes 692060 | tf_op jit(solution)/shard_map/unffn/pallas_call | solution.py:112
  189.7 2.3 add_convert_fusion.1
  192.3 2.1 collective-permute-start.29
  195.7 13.0 %attend_back_0.1 = (bf16[1024,768]{1,0:T(8,128)(2,1)}, bf16[1024,768]{1,0:T(8,128)(2,1)}, bf16[1024,768]{1,0:T(8,128)(2,1)}) custom-call(s32[5]{0:T(128)} %stack.45.at_ref, bf16[1024,768]{1,0:T(8,128)(2,1)} %get-tuple-element.144.q_ref, bf16[1024,768]{1,0:T(8,128)(2,1)} %get-tuple-element.145.k_ref, bf16[1024,768]{1,0:T(8,128)(2,1)} %get-tuple-element.146.v_ref, ...), custom_call_target="tpu_custom_call" | custom-call | flops 322122560 | bytes 125829 | tf_op jit(solution)/shard_map/attend_back_0/pallas_call | solution.py:112
  208.7 2.2 fusion.2
  213.4 2.6 add_convert_fusion
  221.2 7.2 %collective-permute-start.30 = (bf16[4,2,24,1920]{3,2,0,1:T(8,128)(2,1)S(1)}, bf16[4,2,24,1920]{3,2,0,1:T(8,128)(2,1)S(1)}, u32[]{:S(2)}, u32[]{:S(2)}) collective-permute-start(bf16[4,2,24,1920]{3,2,0,1:T(8,128)(2,1)S(1)} %dynamic-slice_bitcast_fusion.2), channel_id=1, source_target_pairs={{0,16},{1,17},{2,18},{3,19},{4,20},{5,21},{6,22},{7,23},{8,24},{9,... | collective-permute-start | bytes 2211848 | tf_op jit(solution)/shard_map/ppermute | solution.py:607
  231.4 13.0 %attend_back_1.1 = (bf16[1024,768]{1,0:T(8,128)(2,1)}, bf16[1024,768]{1,0:T(8,128)(2,1)}, bf16[1024,768]{1,0:T(8,128)(2,1)}) custom-call(s32[5]{0:T(128)} %stack.45.at_ref, bf16[1024,768]{1,0:T(8,128)(2,1)} %get-tuple-element.144.q_ref, bf16[1024,768]{1,0:T(8,128)(2,1)} %get-tuple-element.145.k_ref, ...), custom_call_target="tpu_custom_call", output_to_operand_aliasing={{0}: (7, {}), {1}: (8, {}), {2}: (9, {})} | custom-call | flops 322122560 | bytes 125829 | tf_op jit(solution)/shard_map/attend_back_1/pallas_call | solution.py:112
  246.0 5.3 %collective-permute-done.33 = bf16[4,96,384]{2,1,0:T(8,128)(2,1)S(1)} collective-permute-done((bf16[4,96,384]{2,1,0:T(8,128)(2,1)S(1)}, bf16[4,96,384]{2,1,0:T(8,128)(2,1)S(1)}, u32[]{:S(2)}, u32[]{:S(2)}) %collective-permute-start.33) | collective-permute-done | bytes 294944 | tf_op jit(solution)/shard_map/ppermute | solution.py:607
  254.0 2.1 collective-permute-start.35
  256.1 9.3 %grad_qkv.1 = (bf16[3,384,768]{2,1,0:T(8,128)(2,1)}, bf16[3,384,768]{2,1,0:T(8,128)(2,1)}) custom-call(s32[5]{0:T(128)} %stack.45.at_ref, bf16[1024,768]{1,0:T(8,128)(2,1)} %get-tuple-element.159.n_ref, bf16[1024,768]{1,0:T(8,128)(2,1)} %get-tuple-element.160.dq_ref.refs_16_, bf16[1024,768]{1,0:T(8,128)(2,1)} %get-tuple-element.161.dk_ref.refs_17_, ...), custom_call_target="tpu_custom_call" | custom-call | flops 72477576 | bytes 314572 | tf_op jit(solution)/shard_map/grad_qkv/pallas_call | solution.py:112
  265.5 2.5 broadcast_select_fusion.1
  274.4 12.1 %unqkv.1 = (bf16[512,768]{1,0:T(8,128)(2,1)}, bf16[512,768]{1,0:T(8,128)(2,1)}, f32[3,768]{1,0:T(4,128)}) custom-call(s32[5]{0:T(128)} %stack.45.at_ref, bf16[1024,768]{1,0:T(8,128)(2,1)} %get-tuple-element.109.x_ref.x_any, f32[8,768]{1,0:T(8,128)} %pad_convert_fusion.row_ref.refs_9_, f32[1024,768]{1,0:T(8,128)} %get-tuple-element.170.dmid_any, ...), custom_call_target="tpu_custom_call" | custom-call | flops 72477576 | bytes 471859 | tf_op jit(solution)/shard_map/unqkv/pallas_call | solution.py:112
  292.6 5.2 %collective-permute-done.48 = bf16[24,3840]{1,0:T(8,128)(2,1)S(1)} collective-permute-done((bf16[24,3840]{1,0:T(8,128)(2,1)S(1)}, bf16[24,3840]{1,0:T(8,128)(2,1)S(1)}, u32[]{:S(2)}, u32[]{:S(2)}) %collective-permute-start.48) | collective-permute-done | bytes 184352 | tf_op jit(solution)/shard_map/ppermute | solution.py:610
  300.2 3.6 %all-to-all-start.2 = ((f32[32,1,240]{2,1,0:T(1,128)}), f32[32,1,240]{2,1,0:T(1,128)S(1)}, u32[]{:S(2)}, u32[]{:S(2)}) async-start(f32[32,1,240]{2,1,0:T(1,128)} %all_to_all.27), calls=%async_computation.2 | async-start | bytes 65536 | tf_op jit(solution)/shard_map/all_to_all | solution.py:849
  305.8 2.4 collective-permute-start.45
  309.7 4.1 %all-to-all-done.2 = f32[32,1,240]{2,1,0:T(1,128)S(1)} async-done(((f32[32,1,240]{2,1,0:T(1,128)}), f32[32,1,240]{2,1,0:T(1,128)S(1)}, u32[]{:S(2)}, u32[]{:S(2)}) %all-to-all-start.2) | async-done | bytes 30752 | tf_op jit(solution)/shard_map/all_to_all | solution.py:849
  (278 shorter events, 80.6 us)
Async XLA Ops:
  0.8 16.7 %collective-permute-start = (bf16[24,2304]{1,0:T(8,128)(2,1)}, bf16[24,2304]{1,0:T(8,128)(2,1)S(1)}, u32[]{:S(2)}, u32[]{:S(2)}) collective-permute-start(bf16[24,2304]{1,0:T(8,128)(2,1)} %param.19), channel_id=1, source_target_pairs={{0,12},{1,13},{2,14},{3,15},{4,0},{5,1},{6,2},{7,3},{8,4},{9,5},{1... | collective-permute-start | bytes 331784 | tf_op jit(solution)/shard_map/ppermute | solution.py:613
  8.1 25.3 %collective-permute-start.5 = (bf16[512,768]{1,0:T(8,128)(2,1)S(1)}, bf16[512,768]{1,0:T(8,128)(2,1)S(1)}, u32[]{:S(2)}, u32[]{:S(2)}) collective-permute-start(bf16[512,768]{1,0:T(8,128)(2,1)S(1)} %dynamic-slice_bitcast_fusion), channel_id=1, source_target_pairs={{0,16},{16,0},{1,17},{17,1},{2,18},{18,2},{3,19},{19,3},{4,20},{20... | collective-permute-start | bytes 2359304 | tf_op jit(solution)/shard_map/ppermute | solution.py:698
  10.5 19.4 %all-to-all-start = ((bf16[32,1,220]{2,1,0:T(2,128)(2,1)}), bf16[32,1,220]{2,1,0:T(2,128)(2,1)S(1)}, u32[]{:S(2)}, u32[]{:S(2)}) async-start(bf16[32,1,220]{2,1,0:T(2,128)(2,1)} %broadcast_in_dim.54), calls=%async_computation | async-start | bytes 65536 | tf_op jit(solution)/shard_map/all_to_all | solution.py:722
  14.7 18.7 %collective-permute-start.6 = (bf16[24,6912]{1,0:T(8,128)(2,1)S(1)}, bf16[24,6912]{1,0:T(8,128)(2,1)}, u32[]{:S(2)}, u32[]{:S(2)}) collective-permute-start(bf16[24,6912]{1,0:T(8,128)(2,1)S(1)} %constant_dynamic-update-slice_fusion), channel_id=1, source_target_pairs={{0,8},{1,9},{2,10},{3,11},{4,12},{5,13},{6,14},{7,15},{8,0},{9,1},... | collective-permute-start | bytes 995336 | tf_op jit(solution)/shard_map/ppermute | solution.py:610
  34.7 20.2 %collective-permute-start.7 = (bf16[2,24,6912]{2,1,0:T(8,128)(2,1)S(1)}, bf16[2,24,6912]{2,1,0:T(8,128)(2,1)}, u32[]{:S(2)}, u32[]{:S(2)}) collective-permute-start(bf16[2,24,6912]{2,1,0:T(8,128)(2,1)S(1)} %broadcast_select_fusion.4), channel_id=1, source_target_pairs={{0,4},{1,5},{2,6},{3,7},{4,0},{5,1},{6,2},{7,3},{8,12},{9,13},{10,... | collective-permute-start | bytes 1990664 | tf_op jit(solution)/shard_map/ppermute | solution.py:610
  36.3 18.7 %collective-permute-start.8 = (bf16[2,4,24,1280]{3,2,1,0:T(8,128)(2,1)S(1)}, bf16[2,4,24,1280]{3,2,1,0:T(8,128)(2,1)S(1)}, u32[]{:S(2)}, u32[]{:S(2)}) collective-permute-start(bf16[2,4,24,1280]{3,2,1,0:T(8,128)(2,1)S(1)} %broadcast_select_fusion.5), channel_id=1, source_target_pairs={{0,2},{1,3},{2,0},{3,1},{4,6},{5,7},{6,4},{7,5},{8,10},{9,11},{10,... | collective-permute-start | bytes 1474568 | tf_op jit(solution)/shard_map/ppermute | solution.py:607
  37.8 17.1 %collective-permute-start.9 = (bf16[4,2,24,1024]{3,2,1,0:T(8,128)(2,1)}, bf16[4,2,24,1024]{3,2,1,0:T(8,128)(2,1)}, u32[]{:S(2)}, u32[]{:S(2)}) collective-permute-start(bf16[4,2,24,1024]{3,2,1,0:T(8,128)(2,1)} %broadcast_select_fusion.6), channel_id=1, source_target_pairs={{0,16},{1,17},{2,18},{3,19},{4,20},{5,21},{6,22},{7,23},{8,24},{9,... | collective-permute-start | bytes 1179656 | tf_op jit(solution)/shard_map/ppermute | solution.py:607
  40.4 14.4 %all-to-all-start.1 = ((bf16[32,1,24]{2,1,0:T(2,128)(2,1)}), bf16[32,1,24]{2,1,0:T(2,128)(2,1)S(1)}, u32[]{:S(2)}, u32[]{:S(2)}) async-start(bf16[32,1,24]{2,1,0:T(2,128)(2,1)} %copy.111), calls=%async_computation.1 | async-start | bytes 32768 | tf_op jit(solution)/shard_map/all_to_all | solution.py:732
  57.3 15.4 %collective-permute-start.11 = (bf16[4,24,3072]{2,1,0:T(8,128)(2,1)}, bf16[4,24,3072]{2,1,0:T(8,128)(2,1)}, u32[]{:S(2)}, u32[]{:S(2)}) collective-permute-start(bf16[4,24,3072]{2,1,0:T(8,128)(2,1)} %slice.135), channel_id=1, source_target_pairs={{0,2},{1,3},{2,0},{3,1},{4,6},{5,7},{6,4},{7,5},{8,10},{9,11},{10,... | collective-permute-start | bytes 1769480 | tf_op jit(solution)/shard_map/ppermute | solution.py:607
  59.7 18.0 %collective-permute-start.10 = (bf16[4,24,3840]{2,1,0:T(8,128)(2,1)S(1)}, bf16[4,24,3840]{2,1,0:T(8,128)(2,1)S(1)}, u32[]{:S(2)}, u32[]{:S(2)}) collective-permute-start(bf16[4,24,3840]{2,1,0:T(8,128)(2,1)S(1)} %slice.134), channel_id=1, source_target_pairs={{0,16},{1,17},{2,18},{3,19},{4,20},{5,21},{6,22},{7,23},{8,24},{9,... | collective-permute-start | bytes 2211848 | tf_op jit(solution)/shard_map/ppermute | solution.py:607
  79.1 36.5 %collective-permute-start.12 = (bf16[2,4,24,3840]{3,2,1,0:T(8,128)(2,1)S(1)}, bf16[2,4,24,3840]{3,2,1,0:T(8,128)(2,1)S(1)}, u32[]{:S(2)}, u32[]{:S(2)}) collective-permute-start(bf16[2,4,24,3840]{3,2,1,0:T(8,128)(2,1)S(1)} %broadcast_select_fusion.2), channel_id=1, source_target_pairs={{0,2},{1,3},{2,0},{3,1},{4,6},{5,7},{6,4},{7,5},{8,10},{9,11},{10,... | collective-permute-start | bytes 4423688 | tf_op jit(solution)/shard_map/ppermute | solution.py:607
  80.6 34.9 %collective-permute-start.13 = (bf16[4,2,24,3072]{3,2,1,0:T(8,128)(2,1)}, bf16[4,2,24,3072]{3,2,1,0:T(8,128)(2,1)}, u32[]{:S(2)}, u32[]{:S(2)}) collective-permute-start(bf16[4,2,24,3072]{3,2,1,0:T(8,128)(2,1)} %broadcast_select_fusion.3), channel_id=1, source_target_pairs={{0,16},{1,17},{2,18},{3,19},{4,20},{5,21},{6,22},{7,23},{8,24},{9,... | collective-permute-start | bytes 3538952 | tf_op jit(solution)/shard_map/ppermute | solution.py:607
  85.8 29.7 %collective-permute-start.18 = (bf16[256,768]{1,0:T(8,128)(2,1)S(1)}, bf16[256,768]{1,0:T(8,128)(2,1)S(1)}, u32[]{:S(2)}, u32[]{:S(2)}) collective-permute-start(bf16[256,768]{1,0:T(8,128)(2,1)S(1)} %get-tuple-element.194), channel_id=1, source_target_pairs={{0,16},{16,0},{1,17},{17,1},{2,18},{18,2},{3,19},{19,3},{4,20},{20... | collective-permute-start | bytes 1179656 | tf_op jit(solution)/shard_map/ppermute | solution.py:698
  87.3 33.0 %collective-permute-start.19 = (bf16[2,4,24,3840]{3,2,1,0:T(8,128)(2,1)S(1)}, bf16[2,4,24,3840]{3,2,1,0:T(8,128)(2,1)S(1)}, u32[]{:S(2)}, u32[]{:S(2)}) collective-permute-start(bf16[2,4,24,3840]{3,2,1,0:T(8,128)(2,1)S(1)} %broadcast_select_fusion.2), channel_id=1, source_target_pairs={{0,1},{1,0},{2,3},{3,2},{4,5},{5,4},{6,7},{7,6},{8,9},{9,8},{10,11... | collective-permute-start | bytes 4423688 | tf_op jit(solution)/shard_map/ppermute | solution.py:607
  115.6 14.7 %collective-permute-start.22 = (bf16[2,4,24,3840]{3,2,1,0:T(8,128)(2,1)S(1)}, bf16[2,4,24,3840]{3,2,1,0:T(8,128)(2,1)}, u32[]{:S(2)}, u32[]{:S(2)}) collective-permute-start(bf16[2,4,24,3840]{3,2,1,0:T(8,128)(2,1)S(1)} %collective-permute-done.12), channel_id=1, source_target_pairs={{0,1},{1,0},{2,3},{3,2},{4,5},{5,4},{6,7},{7,6},{8,9},{9,8},{10,11... | collective-permute-start | bytes 4423688 | tf_op jit(solution)/shard_map/ppermute | solution.py:607
  115.7 14.6 %collective-permute-start.23 = (bf16[4,2,24,3072]{3,2,1,0:T(8,128)(2,1)}, bf16[4,2,24,3072]{3,2,1,0:T(8,128)(2,1)}, u32[]{:S(2)}, u32[]{:S(2)}) collective-permute-start(bf16[4,2,24,3072]{3,2,1,0:T(8,128)(2,1)} %broadcast_select_fusion.3), channel_id=1, source_target_pairs={{0,1},{1,0},{2,3},{3,2},{4,5},{5,4},{6,7},{7,6},{8,9},{9,8},{10,11... | collective-permute-start | bytes 3538952 | tf_op jit(solution)/shard_map/ppermute | solution.py:607
  165.2 24.5 %collective-permute-start.26 = (bf16[1536,768]{1,0:T(8,128)(2,1)}, bf16[1536,768]{1,0:T(8,128)(2,1)}, u32[]{:S(2)}, u32[]{:S(2)}) collective-permute-start(bf16[1536,768]{1,0:T(8,128)(2,1)} %get-tuple-element.139), channel_id=1, source_target_pairs={{0,1},{1,0},{2,3},{3,2},{4,5},{5,4},{6,7},{7,6},{8,9},{9,8},{10,11... | collective-permute-start | bytes 7077896 | tf_op jit(solution)/shard_map/ppermute | solution.py:607
  165.4 24.0 %collective-permute-start.25 = (bf16[512,768]{1,0:T(8,128)(2,1)}, bf16[512,768]{1,0:T(8,128)(2,1)}, u32[]{:S(2)}, u32[]{:S(2)}) collective-permute-start(bf16[512,768]{1,0:T(8,128)(2,1)} %get-tuple-element.135), channel_id=1, source_target_pairs={{0,16},{16,0},{1,17},{17,1},{2,18},{18,2},{3,19},{19,3},{4,20},{20... | collective-permute-start | bytes 2359304 | tf_op jit(solution)/shard_map/ppermute | solution.py:698
  189.5 23.9 %collective-permute-start.27 = (bf16[384,3840]{1,0:T(8,128)(2,1)}, bf16[384,3840]{1,0:T(8,128)(2,1)}, u32[]{:S(2)}, u32[]{:S(2)}) collective-permute-start(bf16[384,3840]{1,0:T(8,128)(2,1)} %get-tuple-element.142), channel_id=1, source_target_pairs={{0,1},{1,0},{2,3},{3,2},{4,5},{5,4},{6,7},{7,6},{8,9},{9,8},{10,11... | collective-permute-start | bytes 8847368 | tf_op jit(solution)/shard_map/ppermute | solution.py:607
  192.3 16.4 %collective-permute-start.29 = (bf16[2,4,96,384]{3,2,1,0:T(8,128)(2,1)S(1)}, bf16[2,4,96,384]{3,2,1,0:T(8,128)(2,1)}, u32[]{:S(2)}, u32[]{:S(2)}) collective-permute-start(bf16[2,4,96,384]{3,2,1,0:T(8,128)(2,1)S(1)} %dynamic-slice_bitcast_fusion.3), channel_id=1, source_target_pairs={{0,2},{1,3},{2,0},{3,1},{4,6},{5,7},{6,4},{7,5},{8,10},{9,11},{10,... | collective-permute-start | bytes 1769480 | tf_op jit(solution)/shard_map/ppermute | solution.py:607
  195.6 15.7 %collective-permute-start.28 = (bf16[4,2,96,384]{3,2,0,1:T(8,128)(2,1)}, bf16[4,2,96,384]{3,2,0,1:T(8,128)(2,1)}, u32[]{:S(2)}, u32[]{:S(2)}) collective-permute-start(bf16[4,2,96,384]{3,2,0,1:T(8,128)(2,1)} %dynamic-slice_bitcast_fusion.4), channel_id=1, source_target_pairs={{0,16},{1,17},{2,18},{3,19},{4,20},{5,21},{6,22},{7,23},{8,24},{9,... | collective-permute-start | bytes 1769480 | tf_op jit(solution)/shard_map/ppermute | solution.py:607
  218.4 26.0 %collective-permute-start.31 = (bf16[2,4,24,1920]{3,2,1,0:T(8,128)(2,1)}, bf16[2,4,24,1920]{3,2,1,0:T(8,128)(2,1)}, u32[]{:S(2)}, u32[]{:S(2)}) collective-permute-start(bf16[2,4,24,1920]{3,2,1,0:T(8,128)(2,1)} %dynamic-slice_bitcast_fusion.1), channel_id=1, source_target_pairs={{0,2},{1,3},{2,0},{3,1},{4,6},{5,7},{6,4},{7,5},{8,10},{9,11},{10,... | collective-permute-start | bytes 2211848 | tf_op jit(solution)/shard_map/ppermute | solution.py:607
  221.2 24.6 %collective-permute-start.30 = (bf16[4,2,24,1920]{3,2,0,1:T(8,128)(2,1)S(1)}, bf16[4,2,24,1920]{3,2,0,1:T(8,128)(2,1)S(1)}, u32[]{:S(2)}, u32[]{:S(2)}) collective-permute-start(bf16[4,2,24,1920]{3,2,0,1:T(8,128)(2,1)S(1)} %dynamic-slice_bitcast_fusion.2), channel_id=1, source_target_pairs={{0,16},{1,17},{2,18},{3,19},{4,20},{5,21},{6,22},{7,23},{8,24},{9,... | collective-permute-start | bytes 2211848 | tf_op jit(solution)/shard_map/ppermute | solution.py:607
  228.5 17.5 %collective-permute-start.32 = (bf16[4,96,384]{2,1,0:T(8,128)(2,1)S(1)}, bf16[4,96,384]{2,1,0:T(8,128)(2,1)S(1)}, u32[]{:S(2)}, u32[]{:S(2)}) collective-permute-start(bf16[4,96,384]{2,1,0:T(8,128)(2,1)S(1)} %dynamic-slice_bitcast_fusion.12), channel_id=1, source_target_pairs={{0,2},{1,3},{2,0},{3,1},{4,6},{5,7},{6,4},{7,5},{8,10},{9,11},{10,... | collective-permute-start | bytes 884744 | tf_op jit(solution)/shard_map/ppermute | solution.py:607
  230.6 20.7 %collective-permute-start.33 = (bf16[4,96,384]{2,1,0:T(8,128)(2,1)S(1)}, bf16[4,96,384]{2,1,0:T(8,128)(2,1)S(1)}, u32[]{:S(2)}, u32[]{:S(2)}) collective-permute-start(bf16[4,96,384]{2,1,0:T(8,128)(2,1)S(1)} %dynamic-slice_bitcast_fusion.11), channel_id=1, source_target_pairs={{0,16},{1,17},{2,18},{3,19},{4,20},{5,21},{6,22},{7,23},{8,24},{9,... | collective-permute-start | bytes 884744 | tf_op jit(solution)/shard_map/ppermute | solution.py:607
  251.6 16.4 %collective-permute-start.39 = (bf16[2,96,768]{2,1,0:T(8,128)(2,1)S(1)}, bf16[2,96,768]{2,1,0:T(8,128)(2,1)S(1)}, u32[]{:S(2)}, u32[]{:S(2)}) collective-permute-start(bf16[2,96,768]{2,1,0:T(8,128)(2,1)S(1)} %dynamic-slice_bitcast_fusion.10), channel_id=1, source_target_pairs={{0,4},{1,5},{2,6},{3,7},{4,0},{5,1},{6,2},{7,3},{8,12},{9,13},{10,... | collective-permute-start | bytes 884744 | tf_op jit(solution)/shard_map/ppermute | solution.py:610
  253.5 16.7 %collective-permute-start.34 = (bf16[4,24,1920]{2,1,0:T(8,128)(2,1)S(1)}, bf16[4,24,1920]{2,1,0:T(8,128)(2,1)S(1)}, u32[]{:S(2)}, u32[]{:S(2)}) collective-permute-start(bf16[4,24,1920]{2,1,0:T(8,128)(2,1)S(1)} %dynamic-slice_bitcast_fusion.9), channel_id=1, source_target_pairs={{0,2},{1,3},{2,0},{3,1},{4,6},{5,7},{6,4},{7,5},{8,10},{9,11},{10,... | collective-permute-start | bytes 1105928 | tf_op jit(solution)/shard_map/ppermute | solution.py:607
  254.0 16.2 %collective-permute-start.35 = (bf16[4,24,1920]{2,1,0:T(8,128)(2,1)S(1)}, bf16[4,24,1920]{2,1,0:T(8,128)(2,1)S(1)}, u32[]{:S(2)}, u32[]{:S(2)}) collective-permute-start(bf16[4,24,1920]{2,1,0:T(8,128)(2,1)S(1)} %dynamic-slice_bitcast_fusion.8), channel_id=1, source_target_pairs={{0,16},{1,17},{2,18},{3,19},{4,20},{5,21},{6,22},{7,23},{8,24},{9,... | collective-permute-start | bytes 1105928 | tf_op jit(solution)/shard_map/ppermute | solution.py:607
  268.1 20.3 %collective-permute-start.40 = (bf16[96,768]{1,0:T(8,128)(2,1)S(1)}, bf16[96,768]{1,0:T(8,128)(2,1)S(1)}, u32[]{:S(2)}, u32[]{:S(2)}) collective-permute-start(bf16[96,768]{1,0:T(8,128)(2,1)S(1)} %fusion.26), channel_id=1, source_target_pairs={{0,8},{1,9},{2,10},{3,11},{4,12},{5,13},{6,14},{7,15},{8,0},{9,1},... | collective-permute-start | bytes 442376 | tf_op jit(solution)/shard_map/ppermute | solution.py:610
  272.6 15.5 %collective-permute-start.38 = (bf16[2,4,24,1152]{3,2,1,0:T(8,128)(2,1)S(1)}, bf16[2,4,24,1152]{3,2,1,0:T(8,128)(2,1)S(1)}, u32[]{:S(2)}, u32[]{:S(2)}) collective-permute-start(bf16[2,4,24,1152]{3,2,1,0:T(8,128)(2,1)S(1)} %fusion.13), channel_id=1, source_target_pairs={{0,2},{1,3},{2,0},{3,1},{4,6},{5,7},{6,4},{7,5},{8,10},{9,11},{10,... | collective-permute-start | bytes 1327112 | tf_op jit(solution)/shard_map/ppermute | solution.py:607
  273.7 14.6 %collective-permute-start.37 = (bf16[4,2,24,1152]{3,2,0,1:T(8,128)(2,1)S(1)}, bf16[4,2,24,1152]{3,2,0,1:T(8,128)(2,1)S(1)}, u32[]{:S(2)}, u32[]{:S(2)}) collective-permute-start(bf16[4,2,24,1152]{3,2,0,1:T(8,128)(2,1)S(1)} %fusion.17), channel_id=1, source_target_pairs={{0,16},{1,17},{2,18},{3,19},{4,20},{5,21},{6,22},{7,23},{8,24},{9,... | collective-permute-start | bytes 1327112 | tf_op jit(solution)/shard_map/ppermute | solution.py:607
  291.6 25.4 %collective-permute-start.41 = (bf16[512,768]{1,0:T(8,128)(2,1)}, bf16[512,768]{1,0:T(8,128)(2,1)S(1)}, u32[]{:S(2)}, u32[]{:S(2)}) collective-permute-start(bf16[512,768]{1,0:T(8,128)(2,1)} %get-tuple-element.176), channel_id=1, source_target_pairs={{0,16},{16,0},{1,17},{17,1},{2,18},{18,2},{3,19},{19,3},{4,20},{20... | collective-permute-start | bytes 2359304 | tf_op jit(solution)/shard_map/ppermute | solution.py:698
  (56 other events, 617.4 us)
